TPU v7x, 256 devices: a whole 4x4x8 slice. The times are simulated.
256 devices in a mesh: view: 32 (over z_lo, y, core), head: 4 (over x), branch: 2 (over z_hi).
Axes of the slice: x: 4, y: 4, z: 8 (z_hi: 2, z_lo: 4; z = z_hi * 4 + z_lo), core: 2. Of those that a mesh axis runs over, the one named last changes fastest.
Arguments:
- tokens: bfloat16 [2, 64, 128, 1024], P('branch', 'view'), may hold values from -14 to 14
- partners: int32 [8, 64], P(None, 'view'), may hold values from 0 to 63, as said below
- counts: int32 [64], P('view'), may hold values from 4 to 8
- w_query: bfloat16 [1024, 1024], P(None, 'head'), may hold values from -1 to 1
- w_key: bfloat16 [1024, 1024], P(None, 'head'), may hold values from -1 to 1
- w_value: bfloat16 [1024, 1024], P(None, 'head'), may hold values from -0.75 to 0.75
- w_out: bfloat16 [1024, 1024], P('head'), may hold values from -0.75 to 0.75
- w_in: bfloat16 [1024, 4096], P(None, 'head'), may hold values from -0.1875 to 0.1875
- w_back: bfloat16 [4096, 1024], P('head'), may hold values from -0.09375 to 0.09375
- guidance: float32 [1], replicated, may hold values from 2 to 6
Outputs:
- guided: bfloat16 [64, 128, 1024], P('view', ('head', 'branch'))
Inputs may be any that keep to these rules, and one draw needn't show every extreme that they name: In each round the views are paired: partners[r, partners[r, v]] = v and partners[r, v] != v; the two views of a pair lie a cyclic distance apart that is a power of two up to 8, the same for all pairs of the round; each such distance is taken by one of the first rounds.
All inputs are finite; a program needn't handle non-finite values.
Results may differ from a plain program's by a relative error of at most 0.022.
Values may be sent and summed in bfloat16 or wider, within the bound.
No kernel may reach another device: no remote copies, remote signals or barrier semaphores. Data moves between devices by JAX's collectives and lax.ppermute only.
A program may use at most 64 MiB of HBM per device.

v0:
```python
import jax
import jax.numpy as jnp
from jax import lax
from jax.sharding import PartitionSpec as P

HD = 64
ROUNDS = 8
HOP_MAX = 8


masked_score = -1e30


def passed_along(block, axis, distance):
    devices = range(lax.axis_size(axis))
    route = [((i - distance) % len(devices), i) for i in devices]
    return lax.ppermute(block, axis, route)


def partner(block, axis, apart):
    count = lax.axis_size(axis)
    route = []
    for low in range(count):
        high = low | 1 << apart
        if high != low and high < count:
            route += [(low, high), (high, low)]
    return lax.ppermute(block, axis, route)


def rms_rows(values):
    return values * lax.rsqrt(jnp.mean(values * values, axis=-1, keepdims=True) + 1e-06)


def block_weight(partners, active, own_views, source, per_device):
    key_views = source * per_device + jnp.arange(per_device, dtype=jnp.int32)
    matches = (partners[:, :, None] == key_views[None, None, :]) & active[:, :, None]
    itself = (own_views[:, None] == key_views[None, :]).astype(jnp.float32)
    return jnp.sum(matches.astype(jnp.float32), axis=0) + itself


def merge_pair(carry_state, incoming_kv, pair_weight, queries, query_view, key_view):
    running_max, running_sum, weighted = carry_state
    tok_rows = incoming_kv.shape[1]
    per_device = incoming_kv.shape[2]
    near_keys = incoming_kv[0].reshape(tok_rows, per_device, -1, HD)[:, key_view]
    near_values = incoming_kv[1].reshape(tok_rows, per_device, -1, HD)[:, key_view]
    scores = jnp.einsum(
        "qhd,khd->hqk", queries[:, query_view], near_keys, preferred_element_type=jnp.float32
    )
    old_max = running_max[query_view]
    new_max = jnp.maximum(old_max, jnp.max(scores, axis=2))
    weights = jnp.exp(scores - new_max[..., None]) * pair_weight
    rescale = jnp.exp(old_max - new_max)
    new_sum = running_sum[query_view] * rescale + jnp.sum(weights, axis=2)
    new_weighted = weighted[:, query_view] * jnp.transpose(rescale)[..., None] + jnp.einsum(
        "hqk,khd->qhd",
        weights.astype(jnp.bfloat16),
        near_values,
        preferred_element_type=jnp.float32,
    )
    return (
        running_max.at[query_view].set(new_max),
        running_sum.at[query_view].set(new_sum),
        weighted.at[:, query_view].set(new_weighted),
    )


def on_device(tokens, partners, counts, w_query, w_key, w_value, w_out, w_in, w_back, guidance):
    per_device = tokens.shape[1]
    tok_rows = tokens.shape[2]
    feature = tokens.shape[3]
    view_count = lax.axis_size("view")
    my_index = lax.axis_index("view")
    flat_rows = jnp.transpose(tokens[0], (1, 0, 2)).reshape(tok_rows * per_device, feature)
    all_rows = flat_rows.shape[0]
    heads_here = w_query.shape[1] // HD
    queries = (
        (jnp.dot(flat_rows, w_query, preferred_element_type=jnp.float32) * HD ** (-0.5))
        .astype(jnp.bfloat16)
        .reshape(tok_rows, per_device, heads_here, HD)
    )
    key_value = (
        jnp.stack(
            [
                jnp.dot(flat_rows, w_key, preferred_element_type=jnp.float32),
                jnp.dot(flat_rows, w_value, preferred_element_type=jnp.float32),
            ]
        )
        .astype(jnp.bfloat16)
        .reshape(2, tok_rows, per_device, heads_here * HD)
    )
    own_views = my_index * per_device + jnp.arange(per_device, dtype=jnp.int32)
    active = jnp.arange(ROUNDS, dtype=jnp.int32)[:, None] < counts[None, :]

    def absorb(carry_state, incoming_kv, source):
        multiplicity = block_weight(partners, active, own_views, source, per_device)
        for query_view in range(per_device):
            for key_view in range(per_device):
                pair_weight = multiplicity[query_view, key_view]
                carry_state = lax.cond(
                    pair_weight > 0,
                    lambda held_state: merge_pair(
                        held_state, incoming_kv, pair_weight, queries, query_view, key_view
                    ),
                    lambda held_state: held_state,
                    carry_state,
                )
        return carry_state

    carry_state = (
        jnp.full((per_device, heads_here, tok_rows), masked_score, jnp.float32),
        jnp.zeros((per_device, heads_here, tok_rows), jnp.float32),
        jnp.zeros((tok_rows, per_device, heads_here, HD), jnp.float32),
    )
    carry_state = absorb(carry_state, key_value, my_index)
    distance = 1
    while distance * per_device <= HOP_MAX and 2 * distance <= view_count:
        earlier = passed_along(key_value, "view", distance)
        carry_state = absorb(carry_state, earlier, (my_index - distance) % view_count)
        later = passed_along(key_value, "view", -distance)
        carry_state = absorb(carry_state, later, (my_index + distance) % view_count)
        distance = distance * 2
    running_max, running_sum, weighted = carry_state
    attended = (
        (weighted / jnp.transpose(running_sum, (2, 0, 1))[..., None])
        .astype(jnp.bfloat16)
        .reshape(all_rows, heads_here * HD)
    )
    head_count = lax.axis_size("head")
    span_rows = all_rows // head_count
    first_own = lax.axis_index("head") * span_rows
    attention = lax.psum(
        jnp.dot(attended, w_out, preferred_element_type=jnp.float32).astype(jnp.bfloat16), "head"
    ).astype(jnp.float32)
    normed = rms_rows(flat_rows.astype(jnp.float32) + attention).astype(jnp.bfloat16)
    attention_own = lax.dynamic_slice_in_dim(attention, first_own, span_rows, 0)
    hidden = jax.nn.gelu(jnp.dot(normed, w_in, preferred_element_type=jnp.float32)).astype(
        jnp.bfloat16
    )
    branch_index = lax.axis_index("branch")
    strength = guidance[0]
    own_weight = jnp.where(branch_index == 0, strength, 1.0 - strength)
    half_rows = span_rows // 2
    update = (
        lax.psum_scatter(
            jnp.dot(hidden, w_back, preferred_element_type=jnp.float32).astype(jnp.bfloat16),
            "head",
            scatter_dimension=0,
            tiled=True,
        ).astype(jnp.float32)
        + attention_own
    )
    outgoing = lax.dynamic_slice_in_dim(update, (1 - branch_index) * half_rows, half_rows, 0)
    incoming = partner(outgoing.astype(jnp.bfloat16), "branch", 0).astype(outgoing.dtype)
    retained = lax.dynamic_slice_in_dim(update, branch_index * half_rows, half_rows, 0)
    guided = own_weight * retained + (1.0 - own_weight) * incoming
    return jnp.transpose(
        guided.reshape(half_rows // per_device, per_device, feature), (1, 0, 2)
    ).astype(jnp.bfloat16)


def solution(mesh):
    placed = (
        P("branch", "view", None, None),
        P(None, "view"),
        P("view"),
        P(None, "head"),
        P(None, "head"),
        P(None, "head"),
        P("head", None),
        P(None, "head"),
        P("head", None),
        P(),
    )
    return jax.shard_map(
        on_device,
        mesh=mesh,
        in_specs=placed,
        out_specs=P("view", ("head", "branch"), None),
        check_vma=False,
    )
```

profile of v0, /device:TPU:8, one launch (start us, length us, event | category | flops | bytes accessed | tf_op | source)
XLA Modules:
  0.0 233.3 jit_solution(10015634985807446898)
XLA Ops:
  10.5 1.7 collective-permute-start.1
  13.8 4.5 %collective-permute-start.3 = (bf16[2,128,2,256]{3,1,2,0:T(8,128)(2,1)}, bf16[2,128,2,256]{3,1,2,0:T(8,128)(2,1)}, u32[]{:S(2)}, u32[]{:S(2)}) collective-permute-start(bf16[2,128,2,256]{3,1,2,0:T(8,128)(2,1)} %pad_maximum_fusion), channel_id=1, source_target_pairs={{16,0},{24,8},{32,16},{40,24},{48,32},{56,40},{64,48},{72,56},{80,... | collective-permute-start | bytes 786440 | tf_op jit(solution)/shard_map/ppermute | solution.py:17
  25.3 6.3 %collective-permute-start.5 = (bf16[2,128,2,256]{3,1,2,0:T(8,128)(2,1)}, bf16[2,128,2,256]{3,1,2,0:T(8,128)(2,1)}, u32[]{:S(2)}, u32[]{:S(2)}) collective-permute-start(bf16[2,128,2,256]{3,1,2,0:T(8,128)(2,1)} %pad_maximum_fusion), channel_id=1, source_target_pairs={{32,0},{40,8},{48,16},{56,24},{64,32},{72,40},{80,48},{88,56},{96,... | collective-permute-start | bytes 786440 | tf_op jit(solution)/shard_map/ppermute | solution.py:17
  51.1 4.6 %conditional.28 = (f32[2,4,128]{2,1,0:T(4,128)S(1)}, f32[2,4,128]{2,1,0:T(4,128)S(1)}, f32[128,2,4,64]{0,3,2,1:T(8,128)S(1)}) conditional(s32[]{:T(128)} %convert_element_type.296, () %tuple.508, (bf16[128,2,4,64]{3,2,1,0:T(4,128)(2,1)S(1)}, bf16[2,128,2,256]{3,1,2,0:T(8,128)(2,1)}, f32[]{:T(128)}) %tuple.509), branch_computations={%region_7.8_spmd, %region_8.11_spmd} | conditional | flops 17271296 | bytes 2854956 | solution.py:100
  55.8 7.2 %conditional.31 = ((f32[2,4,128]{2,1,0:T(4,128)S(1)}, f32[2,4,128]{2,1,0:T(4,128)S(1)}, f32[128,2,4,64]{0,3,2,1:T(8,128)S(1)})) conditional(s32[]{:T(128)} %convert_element_type.293, (f32[2,4,128]{2,1,0:T(4,128)S(1)}, f32[2,4,128]{2,1,0:T(4,128)S(1)}, f32[128,2,4,64]{0,3,2,1:T(8,128)S(1)}) %get-tuple-element.2753, (f32[2,4,128]{2,1,0:T(4,128)S(1)}, ...), branch_computations={%region_19.20_spmd, %region_20.23_spmd} | conditional | flops 17303552 | bytes 2849316 | solution.py:100
  55.8 1.8 copy.222
  63.0 7.3 %conditional.32 = ((f32[2,4,128]{2,1,0:T(4,128)S(1)}, f32[2,4,128]{2,1,0:T(4,128)S(1)}, f32[128,2,4,64]{0,3,2,1:T(8,128)S(1)})) conditional(s32[]{:T(128)} %convert_element_type.290, (f32[2,4,128]{2,1,0:T(4,128)S(1)}, f32[2,4,128]{2,1,0:T(4,128)S(1)}, f32[128,2,4,64]{0,3,2,1:T(8,128)S(1)}) %get-tuple-element.2754, (f32[2,4,128]{2,1,0:T(4,128)S(1)}, ...), branch_computations={%region_23.24_spmd, %region_24.27_spmd} | conditional | flops 17303552 | bytes 2849316 | solution.py:100
  63.0 1.8 copy.224
  67.8 1.7 fusion.50
  70.3 7.1 %conditional.33 = ((f32[2,4,128]{2,1,0:T(4,128)S(1)}, f32[2,4,128]{2,1,0:T(4,128)S(1)}, f32[128,2,4,64]{0,3,2,1:T(8,128)S(1)})) conditional(s32[]{:T(128)} %convert_element_type.289, (f32[2,4,128]{2,1,0:T(4,128)S(1)}, f32[2,4,128]{2,1,0:T(4,128)S(1)}, f32[128,2,4,64]{0,3,2,1:T(8,128)S(1)}) %get-tuple-element.2755, (f32[2,4,128]{2,1,0:T(4,128)S(1)}, ...), branch_computations={%region_27.28_spmd, %region_28.31_spmd} | conditional | flops 17303552 | bytes 2849316 | solution.py:100
  70.3 1.8 copy.226
  77.4 7.3 %conditional.35 = ((f32[2,4,128]{2,1,0:T(4,128)S(1)}, f32[2,4,128]{2,1,0:T(4,128)S(1)}, f32[128,2,4,64]{0,3,2,1:T(8,128)S(1)})) conditional(s32[]{:T(128)} %convert_element_type.287, (f32[2,4,128]{2,1,0:T(4,128)S(1)}, f32[2,4,128]{2,1,0:T(4,128)S(1)}, f32[128,2,4,64]{0,3,2,1:T(8,128)S(1)}) %get-tuple-element.2757, (f32[2,4,128]{2,1,0:T(4,128)S(1)}, ...), branch_computations={%region_35.36_spmd, %region_36.39_spmd} | conditional | flops 17303552 | bytes 2849316 | solution.py:100
  77.4 1.8 copy.230
  82.2 1.7 fusion.89
  84.9 7.3 %conditional.38 = ((f32[2,4,128]{2,1,0:T(4,128)S(1)}, f32[2,4,128]{2,1,0:T(4,128)S(1)}, f32[128,2,4,64]{0,3,2,1:T(8,128)S(1)})) conditional(s32[]{:T(128)} %convert_element_type.282, (f32[2,4,128]{2,1,0:T(4,128)S(1)}, f32[2,4,128]{2,1,0:T(4,128)S(1)}, f32[128,2,4,64]{0,3,2,1:T(8,128)S(1)}) %get-tuple-element.2760, (f32[2,4,128]{2,1,0:T(4,128)S(1)}, ...), branch_computations={%region_47.48_spmd, %region_48.51_spmd} | conditional | flops 17303552 | bytes 2849316 | solution.py:100
  85.0 1.8 copy.236
  89.8 1.7 fusion.128
  92.3 7.1 %conditional.39 = ((f32[2,4,128]{2,1,0:T(4,128)S(1)}, f32[2,4,128]{2,1,0:T(4,128)S(1)}, f32[128,2,4,64]{0,3,2,1:T(8,128)S(1)})) conditional(s32[]{:T(128)} %convert_element_type.281, (f32[2,4,128]{2,1,0:T(4,128)S(1)}, f32[2,4,128]{2,1,0:T(4,128)S(1)}, f32[128,2,4,64]{0,3,2,1:T(8,128)S(1)}) %get-tuple-element.2761, (f32[2,4,128]{2,1,0:T(4,128)S(1)}, ...), branch_computations={%region_51.52_spmd, %region_52.55_spmd} | conditional | flops 17303552 | bytes 2849316 | solution.py:100
  92.3 1.8 copy.238
  99.4 7.2 %conditional.40 = ((f32[2,4,128]{2,1,0:T(4,128)S(1)}, f32[2,4,128]{2,1,0:T(4,128)S(1)}, f32[128,2,4,64]{0,3,2,1:T(8,128)S(1)})) conditional(s32[]{:T(128)} %convert_element_type.278, (f32[2,4,128]{2,1,0:T(4,128)S(1)}, f32[2,4,128]{2,1,0:T(4,128)S(1)}, f32[128,2,4,64]{0,3,2,1:T(8,128)S(1)}) %get-tuple-element.2762, (f32[2,4,128]{2,1,0:T(4,128)S(1)}, ...), branch_computations={%region_55.56_spmd, %region_56.59_spmd} | conditional | flops 17303552 | bytes 2849316 | solution.py:100
  99.4 1.8 copy.240
  101.2 1.7 fusion.428
  106.7 7.3 %conditional.43 = ((f32[2,4,128]{2,1,0:T(4,128)S(1)}, f32[2,4,128]{2,1,0:T(4,128)S(1)}, f32[128,2,4,64]{0,3,2,1:T(8,128)S(1)})) conditional(s32[]{:T(128)} %convert_element_type.275, (f32[2,4,128]{2,1,0:T(4,128)S(1)}, f32[2,4,128]{2,1,0:T(4,128)S(1)}, f32[128,2,4,64]{0,3,2,1:T(8,128)S(1)}) %get-tuple-element.2765, (f32[2,4,128]{2,1,0:T(4,128)S(1)}, ...), branch_computations={%region_67.68_spmd, %region_68.71_spmd} | conditional | flops 17303552 | bytes 2849316 | solution.py:100
  106.7 1.8 copy.246
  114.1 5.6 %conditional.52 = ((f32[2,4,128]{2,1,0:T(4,128)S(1)}, f32[2,4,128]{2,1,0:T(4,128)S(1)}, f32[128,2,4,64]{0,3,2,1:T(8,128)S(1)})) conditional(s32[]{:T(128)} %convert_element_type.260, (f32[2,4,128]{2,1,0:T(4,128)S(1)}, f32[2,4,128]{2,1,0:T(4,128)S(1)}, f32[128,2,4,64]{0,3,2,1:T(8,128)S(1)}) %get-tuple-element.2774, ...), branch_computations={%region_103.104_spmd, %region_104.107_spmd} | conditional | flops 17303552 | bytes 2849316 | solution.py:100
  119.8 4.9 %conditional.55 = ((f32[2,4,128]{2,1,0:T(4,128)S(1)}, f32[128,2,4,64]{0,3,2,1:T(8,128)S(1)})) conditional(s32[]{:T(128)} %convert_element_type.257, (f32[2,4,128]{2,1,0:T(4,128)S(1)}, f32[128,2,4,64]{0,3,2,1:T(8,128)S(1)}) %tuple.536, (f32[2,4,128]{2,1,0:T(4,128)S(1)}, f32[2,4,128]{2,1,0:T(4,128)S(1)}, bf16[128,2,4,64]{3,2,1,0:T(4,128)(2,1)S(1)}, ...), branch_computations={%region_115.116_spmd, %region_116.0_spmd} | conditional | flops 17303552 | bytes 2847260 | solution.py:100
  125.1 2.2 convolution_convert_fusion
  127.3 58.8 %all-reduce.5.cloned.1.call-done = bf16[256,1024]{1,0:T(8,128)(2,1)} async-done(((bf16[256,1024]{1,0:T(8,128)(2,1)}), bf16[256,1024]{1,0:T(8,128)(2,1)}) %all-reduce.5.cloned.1.call-update) | async-done | bytes 524304 | tf_op jit(solution)/shard_map/psum | solution.py:132
  187.5 4.2 %convolution_convert_fusion.1 = bf16[256,1024]{1,0:T(8,128)(2,1)} fusion(bf16[1024,1024]{1,0:T(8,128)(2,1)S(1)} %copy-done, bf16[1024,1024]{1,0:T(8,128)(2,1)} %param.239, bf16[256,1024]{1,0:T(8,128)(2,1)S(1)} %reshape.3017, f32[256]{0:T(256)S(1)} %add_rsqrt_fusion, bf16[256,1024]{1,0:T(8,128)(2,1)} %all-reduce.5.cloned.1.call-done), kind=kOutput, calls=%fused_computation.613 | convolution fusion | flops 1077673984 | bytes 5768192 | tf_op jit(solution)/shard_map/dot_general | solution.py:146
  192.8 23.7 %reduce-scatter.2.cloned.1.call-done = bf16[64,1024]{1,0:T(8,128)(2,1)} async-done(((bf16[256,1024]{1,0:T(8,128)(2,1)}), bf16[64,1024]{1,0:T(8,128)(2,1)}) %reduce-scatter.2.cloned.1.call-update) | async-done | bytes 131088 | tf_op jit(solution)/shard_map/reduce_scatter | solution.py:145
  217.5 5.8 %collective-permute-start.6 = (bf16[32,1024]{1,0:T(8,128)(2,1)S(1)}, bf16[32,1024]{1,0:T(8,128)(2,1)S(1)}, u32[]{:S(2)}, u32[]{:S(2)}) collective-permute-start(bf16[32,1024]{1,0:T(8,128)(2,1)S(1)} %dynamic-slice_convert_fusion), channel_id=1, source_target_pairs={{0,1},{1,0},{2,3},{3,2},{4,5},{5,4},{6,7},{7,6},{8,9},{9,8},{10,11... | collective-permute-start | bytes 196616 | tf_op jit(solution)/shard_map/ppermute | solution.py:27
  223.9 1.9 collective-permute-done.6
  (161 shorter events, 70.6 us)
Async XLA Ops:
  6.5 180.9 %copy-start = (bf16[1024,1024]{1,0:T(8,128)(2,1)S(1)}, bf16[1024,1024]{1,0:T(8,128)(2,1)}, u32[]{:S(2)}) copy-start(bf16[1024,1024]{1,0:T(8,128)(2,1)} %param.240) | copy-start | bytes 6291460
  6.5 14.8 %copy-start.1 = (bf16[1,2,128,1024]{3,2,1,0:T(8,128)(2,1)S(1)}, bf16[1,2,128,1024]{3,2,1,0:T(8,128)(2,1)}, u32[]{:S(2)}) copy-start(bf16[1,2,128,1024]{3,2,1,0:T(8,128)(2,1)} %param.232) | copy-start | bytes 1572868
  6.5 11.8 %copy-start.4 = (s32[2]{0:T(128)S(1)}, s32[2]{0:T(128)}, u32[]{:S(2)}) copy-start(s32[2]{0:T(128)} %param.234) | copy-start | bytes 28
  6.5 11.9 %copy-start.3 = (s32[8,2]{0,1:T(2,128)S(1)}, s32[8,2]{0,1:T(2,128)}, u32[]{:S(2)}) copy-start(s32[8,2]{0,1:T(2,128)} %param.233) | copy-start | bytes 196
  6.5 179.6 %all-reduce.5.cloned.1.call-start = ((), (), s32[]{:S(2)}) async-start(), calls=%async_computation.1 | async-start | bytes 1048576 | tf_op jit(solution)/shard_map/psum | solution.py:132
  10.5 14.8 %collective-permute-start = (bf16[2,128,2,256]{3,1,2,0:T(8,128)(2,1)}, bf16[2,128,2,256]{3,1,2,0:T(8,128)(2,1)}, u32[]{:S(2)}, u32[]{:S(2)}) collective-permute-start(bf16[2,128,2,256]{3,1,2,0:T(8,128)(2,1)} %pad_maximum_fusion), channel_id=1, source_target_pairs={{248,0},{0,8},{8,16},{16,24},{24,32},{32,40},{40,48},{48,56},{56,6... | collective-permute-start | bytes 786440 | tf_op jit(solution)/shard_map/ppermute | solution.py:17
  10.5 74.2 %collective-permute-start.1 = (bf16[2,128,2,256]{3,1,2,0:T(8,128)(2,1)}, bf16[2,128,2,256]{3,1,2,0:T(8,128)(2,1)}, u32[]{:S(2)}, u32[]{:S(2)}) collective-permute-start(bf16[2,128,2,256]{3,1,2,0:T(8,128)(2,1)} %pad_maximum_fusion), channel_id=1, source_target_pairs={{8,0},{16,8},{24,16},{32,24},{40,32},{48,40},{56,48},{64,56},{72,6... | collective-permute-start | bytes 786440 | tf_op jit(solution)/shard_map/ppermute | solution.py:17
  12.2 87.2 %collective-permute-start.2 = (bf16[2,128,2,256]{3,1,2,0:T(8,128)(2,1)}, bf16[2,128,2,256]{3,1,2,0:T(8,128)(2,1)}, u32[]{:S(2)}, u32[]{:S(2)}) collective-permute-start(bf16[2,128,2,256]{3,1,2,0:T(8,128)(2,1)} %pad_maximum_fusion), channel_id=1, source_target_pairs={{240,0},{248,8},{0,16},{8,24},{16,32},{24,40},{32,48},{40,56},{48,... | collective-permute-start | bytes 786440 | tf_op jit(solution)/shard_map/ppermute | solution.py:17
  13.8 100.2 %collective-permute-start.3 = (bf16[2,128,2,256]{3,1,2,0:T(8,128)(2,1)}, bf16[2,128,2,256]{3,1,2,0:T(8,128)(2,1)}, u32[]{:S(2)}, u32[]{:S(2)}) collective-permute-start(bf16[2,128,2,256]{3,1,2,0:T(8,128)(2,1)} %pad_maximum_fusion), channel_id=1, source_target_pairs={{16,0},{24,8},{32,16},{40,24},{48,32},{56,40},{64,48},{72,56},{80,... | collective-permute-start | bytes 786440 | tf_op jit(solution)/shard_map/ppermute | solution.py:17
  18.3 95.7 %collective-permute-start.4 = (bf16[2,128,2,256]{3,1,2,0:T(8,128)(2,1)}, bf16[2,128,2,256]{3,1,2,0:T(8,128)(2,1)S(1)}, u32[]{:S(2)}, u32[]{:S(2)}) collective-permute-start(bf16[2,128,2,256]{3,1,2,0:T(8,128)(2,1)} %pad_maximum_fusion), channel_id=1, source_target_pairs={{224,0},{232,8},{240,16},{248,24},{0,32},{8,40},{16,48},{24,56},{3... | collective-permute-start | bytes 786440 | tf_op jit(solution)/shard_map/ppermute | solution.py:17
  25.3 88.9 %collective-permute-start.5 = (bf16[2,128,2,256]{3,1,2,0:T(8,128)(2,1)}, bf16[2,128,2,256]{3,1,2,0:T(8,128)(2,1)}, u32[]{:S(2)}, u32[]{:S(2)}) collective-permute-start(bf16[2,128,2,256]{3,1,2,0:T(8,128)(2,1)} %pad_maximum_fusion), channel_id=1, source_target_pairs={{32,0},{40,8},{48,16},{56,24},{64,32},{72,40},{80,48},{88,56},{96,... | collective-permute-start | bytes 786440 | tf_op jit(solution)/shard_map/ppermute | solution.py:17
  127.3 89.2 %reduce-scatter.2.cloned.1.call-start = ((), (), s32[]{:S(2)}) async-start(), calls=%async_computation.2 | async-start | bytes 655360 | tf_op jit(solution)/shard_map/reduce_scatter | solution.py:145
  187.5 4.2 %copy-start.2 = (bf16[256,1024]{1,0:T(8,128)(2,1)S(1)}, bf16[256,1024]{1,0:T(8,128)(2,1)}, u32[]{:S(2)}) copy-start(bf16[256,1024]{1,0:T(8,128)(2,1)} %all-reduce.5.cloned.1.call-done) | copy-start | bytes 1572868
  217.5 8.3 %collective-permute-start.6 = (bf16[32,1024]{1,0:T(8,128)(2,1)S(1)}, bf16[32,1024]{1,0:T(8,128)(2,1)S(1)}, u32[]{:S(2)}, u32[]{:S(2)}) collective-permute-start(bf16[32,1024]{1,0:T(8,128)(2,1)S(1)} %dynamic-slice_convert_fusion), channel_id=1, source_target_pairs={{0,1},{1,0},{2,3},{3,2},{4,5},{5,4},{6,7},{7,6},{8,9},{9,8},{10,11... | collective-permute-start | bytes 196616 | tf_op jit(solution)/shard_map/ppermute | solution.py:27
Sparse Core Ops, SparseCore 0:
  127.4 58.7 all-reduce.4
  191.8 24.6 reduce-scatter.1
where the time goes:
time: 236 us; the launch traced here: 233 us
  waiting for transfers between devices  84.4 us (36%)
  local copies, waits for them, and re-layouts  44 us (19%)
  matrix products  39.4 us (17%)
  between operations  31.9 us (14%)
  starting transfers between devices  20 us (8%)
  other arithmetic  12.6 us (5%)
    psum x1, waiting for transfers between devices, on_device(): lax.psum(jnp.dot(attended, w_out, preferred_element_type=jnp.float32).ast...  58.8 us
    reduce_scatter x1, waiting for transfers between devices, on_device(): lax.psum_scatter(jnp.dot(hidden, w_back, preferred_element_type=jnp.float...  23.7 us
    another operation x22, local copies, waits for them, and re-layouts  19.8 us
    dot_general x11, matrix products, merge_pair(): jnp.einsum('hqk,khd->qhd', weights.astype(jnp.bfloat16), near_values, pre...  17.3 us
    slice x11, local copies, waits for them, and re-layouts, merge_pair(): incoming_kv[1].reshape(tok_rows, per_device, -1, HD)[:, key_view]  15.6 us
    ppermute x6, starting transfers between devices, passed_along(): return lax.ppermute(block, axis, route)  14.1 us
    dot_general x11, matrix products, merge_pair(): jnp.einsum('qhd,khd->hqk', queries[:, query_view], near_keys, preferred_e...  11.2 us
    reduce_sum x11, other arithmetic, merge_pair(): new_sum = running_sum[query_view] * rescale + jnp.sum(weights, axis=2)  7.71 us
  transfers between devices with their start and end apart: 9, of which 3 were waited for; matrix products, arithmetic and copies ran while one was open for 31% of the time, Pallas kernels for 0%

commit v1 on v0

v1 whole, which is shorter than its diff:
```python
import functools

import jax
import jax.numpy as jnp
from jax import lax
from jax.experimental import pallas as pl
from jax.experimental.pallas import tpu as pltpu
from jax.sharding import PartitionSpec as P

HD = 64
ROUNDS = 8
MASKED = -1e30

NT = (((1,), (1,)), ((), ()))
VMEM = pl.BlockSpec(memory_space=pltpu.VMEM)
SMEM = pl.BlockSpec(memory_space=pltpu.SMEM)
ANY = pl.BlockSpec(memory_space=pl.ANY)


def params(mib):
    return pltpu.CompilerParams(vmem_limit_bytes=mib * 1024 * 1024)


def matched(axis, count, apart, parity):
    route = []
    for low in range(count):
        if (low // apart) % 2 == parity:
            high = (low + apart) % count
            route += [(low, high), (high, low)]
    return functools.partial(lax.ppermute, axis_name=axis, perm=route)


def flipped(axis, count, bits):
    return functools.partial(lax.ppermute, axis_name=axis, perm=[(i, i ^ bits) for i in range(count)])


def dot(a, b):
    return jnp.dot(a, b, preferred_element_type=jnp.float32)


def project_kernel(x_ref, wq_ref, wk_ref, wv_ref, q_ref, kv_ref):
    x = x_ref[...]
    q = (dot(x, wq_ref[...]) * HD ** (-0.5)).astype(jnp.bfloat16)
    k = dot(x, wk_ref[...]).astype(jnp.bfloat16)
    v = dot(x, wv_ref[...]).astype(jnp.bfloat16)
    zeros = jnp.zeros((x.shape[0], HD), jnp.bfloat16)
    for h in range(q_ref.shape[0]):
        cols = slice(h * HD, (h + 1) * HD)
        q_ref[h] = jnp.concatenate([q[:, cols], zeros], axis=1)
        kv_ref[h] = jnp.concatenate([k[:, cols], v[:, cols]], axis=1)


def project(x, w_query, w_key, w_value):
    rows, width = x.shape
    heads = w_query.shape[1] // HD
    shape = jax.ShapeDtypeStruct((heads, rows, 2 * HD), jnp.bfloat16)
    return pl.pallas_call(
        project_kernel,
        out_shape=(shape, shape),
        in_specs=[VMEM] * 4,
        out_specs=(VMEM, VMEM),
        compiler_params=params(32),
        cost_estimate=pl.CostEstimate(flops=6 * rows * width * heads * HD, bytes_accessed=3_000_000, transcendentals=0),
        name="project",
    )(x, w_query, w_key, w_value)


def attend_kernel(blocks, first, last, bias_ref, q_ref, *refs):
    count = len(blocks)
    kv_refs = refs[:count]
    state_ref = None if first else refs[count]
    out_ref = refs[-1]
    heads, rows, _ = q_ref.shape
    tok = rows // 2
    for qv in range(2):
        for h in range(heads):
            q = q_ref[h, qv * tok : (qv + 1) * tok, :]
            scores, taken = [], []
            for (slot, both), kv_ref in zip(blocks, kv_refs):
                for kvw in (0, 1) if both else (qv,):
                    kv = kv_ref[h, kvw * tok : (kvw + 1) * tok, :]
                    s = lax.dot_general(q, kv, NT, preferred_element_type=jnp.float32)
                    scores.append(s + bias_ref[qv, 2 * slot + kvw])
                    taken.append(kv)
            top = functools.reduce(jnp.maximum, scores)
            top = jnp.max(top, axis=1, keepdims=True)
            if not first:
                held = state_ref[qv * heads + h]
                old_top, old_sum = held[:, 0:1], held[:, 1:2]
                top = jnp.maximum(top, old_top)
            weights = [jnp.exp(s - top) for s in scores]
            total = jnp.sum(functools.reduce(jnp.add, weights), axis=1, keepdims=True)
            blended = dot(jnp.concatenate([w.astype(jnp.bfloat16) for w in weights], axis=1), jnp.concatenate(taken, axis=0))
            if not first:
                scale = jnp.exp(old_top - top)
                total = total + scale * old_sum
                blended = blended + scale * held
            if last:
                done = blended[:, HD:] / total
                out_ref[qv * tok : (qv + 1) * tok, h * HD : (h + 1) * HD] = done.astype(jnp.bfloat16)
            else:
                lane = lax.broadcasted_iota(jnp.int32, blended.shape, 1)
                kept = jnp.where(lane == 0, top, jnp.where(lane == 1, total, blended))
                out_ref[qv * heads + h] = kept


def attend(blocks, first, last, bias, q, kvs, state=None):
    heads, rows, _ = q.shape
    tok = rows // 2
    if last:
        out = jax.ShapeDtypeStruct((rows, heads * HD), jnp.bfloat16)
    else:
        out = jax.ShapeDtypeStruct((2 * heads, tok, 2 * HD), jnp.float32)
    pairs = sum(4 if both else 2 for _, both in blocks)
    held = () if first else (state,)
    return pl.pallas_call(
        functools.partial(attend_kernel, blocks, first, last),
        out_shape=out,
        in_specs=[SMEM] + [VMEM] * (1 + len(kvs) + len(held)),
        out_specs=VMEM,
        compiler_params=params(32),
        cost_estimate=pl.CostEstimate(
            flops=pairs * heads * tok * tok * 8 * HD, bytes_accessed=1_000_000, transcendentals=pairs * heads * tok * tok
        ),
        name="attend",
    )(bias, q, *kvs, *held)


def feed_kernel(head_ref, x_ref, a0, a1, a2, a3, o0, o1, o2, o3, win_hbm, wback_hbm, own_ref, r1, r2, r3, win, wback, sems):
    load_in = pltpu.make_async_copy(win_hbm, win, sems.at[0])
    load_back = pltpu.make_async_copy(wback_hbm, wback, sems.at[1])
    load_in.start()
    load_back.start()
    head = head_ref[0]
    rows, width = x_ref.shape
    tok = rows // 2
    part = tok // 4

    def turned(ref):
        pieces = []
        for j in range(4):
            for view in range(2):
                start = pl.multiple_of(view * tok + jnp.bitwise_xor(head, j) * part, part)
                pieces.append(ref[pl.ds(start, part), :])
        return jnp.concatenate(pieces, axis=0)

    attention = dot(turned(a0), o0[...])
    for a, o in ((a1, o1), (a2, o2), (a3, o3)):
        attention = attention + dot(turned(a), o[...])
    y = turned(x_ref).astype(jnp.float32) + attention
    normed = (y * lax.rsqrt(jnp.mean(y * y, axis=-1, keepdims=True) + 1e-06)).astype(jnp.bfloat16)
    load_in.wait()
    hidden = jax.nn.gelu(dot(normed, win[...])).astype(jnp.bfloat16)
    load_back.wait()
    update = dot(hidden, wback[...])
    own_ref[...] = attention[: 2 * part] + update[: 2 * part]
    for j, ref in ((1, r1), (2, r2), (3, r3)):
        ref[...] = update[2 * part * j : 2 * part * (j + 1)].astype(jnp.bfloat16)


def feed(head, x, attended, w_outs, w_in, w_back):
    rows, width = x.shape
    piece = jax.ShapeDtypeStruct((rows // 4, width), jnp.bfloat16)
    return pl.pallas_call(
        feed_kernel,
        out_shape=(jax.ShapeDtypeStruct((rows // 4, width), jnp.float32), piece, piece, piece),
        in_specs=[SMEM] + [VMEM] * 9 + [ANY, ANY],
        out_specs=(VMEM,) * 4,
        scratch_shapes=[
            pltpu.VMEM(w_in.shape, jnp.bfloat16),
            pltpu.VMEM(w_back.shape, jnp.bfloat16),
            pltpu.SemaphoreType.DMA((2,)),
        ],
        compiler_params=params(40),
        cost_estimate=pl.CostEstimate(flops=6 * rows * width * width, bytes_accessed=8_000_000, transcendentals=rows * width),
        name="feed",
    )(head, x, *attended, *w_outs, w_in, w_back)


def gather_kernel(branch_ref, own_ref, r1, r2, r3, kept_ref, sent_ref):
    branch = branch_ref[0]
    part = own_ref.shape[0] // 2
    half = part // 2
    for view in range(2):
        for side, ref in ((branch, kept_ref), (1 - branch, sent_ref)):
            rows = pl.ds(pl.multiple_of(view * part + side * half, half), half)
            total = own_ref[rows, :]
            for r in (r1, r2, r3):
                total = total + r[rows, :].astype(jnp.float32)
            ref[view * half : (view + 1) * half, :] = total.astype(ref.dtype)


def gather(branch, own, received):
    rows, width = own.shape
    return pl.pallas_call(
        gather_kernel,
        out_shape=(
            jax.ShapeDtypeStruct((rows // 2, width), jnp.float32),
            jax.ShapeDtypeStruct((rows // 2, width), jnp.bfloat16),
        ),
        in_specs=[SMEM] + [VMEM] * 4,
        out_specs=(VMEM, VMEM),
        name="gather",
    )(branch, own, *received)


def on_device(tokens, partners, counts, w_query, w_key, w_value, w_out, w_in, w_back, guidance):
    per_device, tok, width = tokens.shape[1:]
    x = tokens[0].reshape(per_device * tok, width)
    count = lax.axis_size("view")
    me = lax.axis_index("view")
    head = lax.axis_index("head").astype(jnp.int32)
    branch = lax.axis_index("branch").astype(jnp.int32)

    q, kv = project(x, w_query, w_key, w_value)

    chip_odd, pair_odd, core = (me // 2) % 2, (me // 4) % 2, me % 2
    near_a, near_b = me + 2 - 4 * chip_odd, me - 2 + 4 * chip_odd
    far_a, far_b = me + 4 - 8 * pair_odd, me - 4 + 8 * pair_odd
    sources = jnp.stack([me, me + 1 - 2 * core, near_a, near_b, me - 1 + 2 * core, far_a, far_b]) % count
    key_views = (sources[:, None] * per_device + jnp.arange(per_device)[None, :]).reshape(-1)
    active = jnp.arange(ROUNDS, dtype=jnp.int32)[:, None] < counts[None, :]
    matches = (partners[:, :, None] == key_views[None, None, :]) & active[:, :, None]
    own_views = me * per_device + jnp.arange(per_device)
    times = jnp.sum(matches.astype(jnp.float32), axis=0) + (own_views[:, None] == key_views[None, :])
    bias = jnp.where(times > 0, jnp.log(jnp.maximum(times, 1.0)), MASKED).astype(jnp.float32)

    sibling = matched("view", count, 1, 0)
    kv_sibling = sibling(kv)
    kv_near_a = matched("view", count, 2, 0)(kv)
    kv_near_b = matched("view", count, 2, 1)(kv)
    kv_far_a = matched("view", count, 4, 0)(kv)
    kv_far_b = matched("view", count, 4, 1)(kv)
    kv_cross = sibling(jnp.where((chip_odd + core) % 2 == 0, kv_near_a, kv_near_b))

    w_1 = flipped("head", 4, 1)(w_out)
    w_32 = flipped("head", 4, 3)(jnp.stack([w_out, w_1]))
    w_outs = (w_out, w_1, w_32[1], w_32[0])

    state = attend(((0, True), (1, True)), True, False, bias, q, (kv, kv_sibling))
    state = attend(((2, False), (3, False), (4, True)), False, False, bias, q, (kv_near_a, kv_near_b, kv_cross), state)
    attended = attend(((5, False), (6, False)), False, True, bias, q, (kv_far_a, kv_far_b), state)

    pieces = [attended] + [flipped("head", 4, j)(attended) for j in (1, 2, 3)]
    own, *outgoing = feed(head[None], x, pieces, w_outs, w_in, w_back)
    received = [flipped("head", 4, j)(r) for j, r in zip((1, 2, 3), outgoing)]
    kept, sent = gather(branch[None], own, received)
    other = flipped("branch", 2, 1)(sent)
    strength = guidance[0]
    weight = jnp.where(branch == 0, strength, 1.0 - strength)
    guided = weight * kept + (1.0 - weight) * other.astype(jnp.float32)
    return guided.reshape(per_device, -1, width).astype(jnp.bfloat16)


def solution(mesh):
    placed = (
        P("branch", "view", None, None),
        P(None, "view"),
        P("view"),
        P(None, "head"),
        P(None, "head"),
        P(None, "head"),
        P("head", None),
        P(None, "head"),
        P("head", None),
        P(),
    )
    return jax.shard_map(
        on_device,
        mesh=mesh,
        in_specs=placed,
        out_specs=P("view", ("head", "branch"), None),
        check_vma=False,
    )
```

time: 236 us -> 78.8 us (0.33)
  waiting for transfers between devices: 84.4 us -> 17 us
  matrix products: 39.4 us -> 0 us
  local copies, waits for them, and re-layouts: 44 us -> 6.98 us
  between operations: 31.9 us -> 0.81 us
  Pallas kernels: 0 us -> 15.6 us
  starting transfers between devices: 20 us -> 34.2 us
  other arithmetic: 12.6 us -> 2.99 us
    psum x1 -> x0, waiting for transfers between devices: 58.8 us -> none  [on_device(): lax.psum(jnp.dot(attended, w_out, preferred_element_type=jnp.float32).ast...]
    dot_general x27 -> x0, matrix products: 39.4 us -> none  [the longest x11 17.3 us: merge_pair(): jnp.einsum('hqk,khd->qhd', weights.astype(jnp.bfloat16), near_values, pre...]
    reduce_scatter x1 -> x0, waiting for transfers between devices: 23.7 us -> none  [on_device(): lax.psum_scatter(jnp.dot(hidden, w_back, preferred_element_type=jnp.float...]
    slice x28 -> x0, local copies, waits for them, and re-layouts: 20.4 us -> none  [the longest x11 15.6 us: merge_pair(): incoming_kv[1].reshape(tok_rows, per_device, -1, HD)[:, key_view]]
    another operation x22 -> x1, local copies, waits for them, and re-layouts: 19.8 us -> 0.08 us  [on_device(): jnp.stack([me, me + 1 - 2 * core, near_a, near_b, me - 1 + 2 * core, far_...]
    pallas_call x0 -> x6, Pallas kernels: none -> 15.6 us  [the longest x3 10.3 us: attend(): pl.pallas_call(functools.partial(attend_kernel, blocks, first, last), out...]
    ppermute x7 -> x15, waiting for transfers between devices: 1.89 us -> 17 us  [the longest x3 7.77 us: on_device(): pieces = [attended] + [flipped('head', 4, j)(attended) for j in (1, 2, 3)]]
    ppermute x7 -> x15, starting transfers between devices: 19.9 us -> 34.2 us  [the longest x1 7.74 us: on_device(): other = flipped('branch', 2, 1)(sent)]
  transfers between devices with their start and end apart: 9 -> 15, of which waited for: 3 -> 7; matrix products, arithmetic and copies ran while one was open for 31% -> 4% of each run, Pallas kernels for 0% -> 14%
where the time goes in v1:
time: 78.8 us; the launch traced here: 77.5 us
  starting transfers between devices  34.2 us (43%)
  waiting for transfers between devices  17 us (22%)
  Pallas kernels  15.6 us (20%)
  local copies, waits for them, and re-layouts  6.98 us (9%)
  other arithmetic  2.99 us (4%)
  between operations  0.81 us (1%)
    pallas_call x3, Pallas kernels, attend(): pl.pallas_call(functools.partial(attend_kernel, blocks, first, last), out...  10.3 us
    ppermute x3, waiting for transfers between devices, on_device(): pieces = [attended] + [flipped('head', 4, j)(attended) for j in (1, 2, 3)]  7.77 us
    ppermute x1, starting transfers between devices, on_device(): other = flipped('branch', 2, 1)(sent)  7.74 us
    ppermute x1, starting transfers between devices, on_device(): kv_far_b = matched('view', count, 4, 1)(kv)  6.44 us
    unnamed x28, local copies, waits for them, and re-layouts  5.54 us
    ppermute x3, waiting for transfers between devices, on_device(): received = [flipped('head', 4, j)(r) for j, r in zip((1, 2, 3), outgoing)]  5.42 us
    ppermute x3, starting transfers between devices, on_device(): pieces = [attended] + [flipped('head', 4, j)(attended) for j in (1, 2, 3)]  5.36 us
    ppermute x3, starting transfers between devices, on_device(): received = [flipped('head', 4, j)(r) for j, r in zip((1, 2, 3), outgoing)]  4.7 us
  transfers between devices with their start and end apart: 15, of which 7 were waited for; matrix products, arithmetic and copies ran while one was open for 4% of the time, Pallas kernels for 14%

profile of v1, /device:TPU:8, one launch (start us, length us, event | category | flops | bytes accessed | tf_op | source)
XLA Modules:
  0.0 77.5 jit_solution(9035716715972333919)
XLA Ops:
  0.0 1.5 %collective-permute-start.9 = (bf16[256,1024]{1,0:T(8,128)(2,1)}, bf16[256,1024]{1,0:T(8,128)(2,1)S(1)}, u32[]{:S(2)}, u32[]{:S(2)}) collective-permute-start(bf16[256,1024]{1,0:T(8,128)(2,1)} %o0.1), channel_id=1, source_target_pairs={{0,2},{2,0},{4,6},{6,4},{1,3},{3,1},{5,7},{7,5},{8,10},{10,8},{12,... | collective-permute-start | bytes 1572872 | tf_op jit(solution)/shard_map/ppermute | solution.py:236
  1.5 1.0 %copy-done.2 = bf16[1,2,128,1024]{3,2,1,0:T(8,128)(2,1)S(1)} copy-done((bf16[1,2,128,1024]{3,2,1,0:T(8,128)(2,1)S(1)}, bf16[1,2,128,1024]{3,2,1,0:T(8,128)(2,1)}, u32[]{:S(2)}) %copy-start.2) | copy-done | bytes 524312
  2.5 1.0 %copy-done.5 = bf16[1024,256]{1,0:T(8,128)(2,1)S(1)} copy-done((bf16[1024,256]{1,0:T(8,128)(2,1)S(1)}, bf16[1024,256]{1,0:T(8,128)(2,1)}, u32[]{:S(2)}) %copy-start.5) | copy-done | bytes 524312
  3.6 1.0 %copy-done.6 = bf16[1024,256]{1,0:T(8,128)(2,1)S(1)} copy-done((bf16[1024,256]{1,0:T(8,128)(2,1)S(1)}, bf16[1024,256]{1,0:T(8,128)(2,1)}, u32[]{:S(2)}) %copy-start.6) | copy-done | bytes 524312
  4.6 1.0 %copy-done.7 = bf16[1024,256]{1,0:T(8,128)(2,1)S(1)} copy-done((bf16[1024,256]{1,0:T(8,128)(2,1)S(1)}, bf16[1024,256]{1,0:T(8,128)(2,1)}, u32[]{:S(2)}) %copy-start.7) | copy-done | bytes 524312
  5.7 0.6 project.1
  6.4 0.8 %collective-permute-start.2 = (bf16[4,256,128]{2,1,0:T(8,128)(2,1)S(1)}, bf16[4,256,128]{2,1,0:T(8,128)(2,1)S(1)}, u32[]{:S(2)}, u32[]{:S(2)}) collective-permute-start(bf16[4,256,128]{2,1,0:T(8,128)(2,1)S(1)} %get-tuple-element.14.refs_0_), channel_id=1, source_target_pairs={{0,16},{16,0},{8,24},{24,8},{32,48},{48,32},{40,56},{56,40},{64,80... | collective-permute-start | bytes 786440 | tf_op jit(solution)/shard_map/ppermute | solution.py:230
  7.2 2.2 %collective-permute-start.3 = (bf16[4,256,128]{2,1,0:T(8,128)(2,1)S(1)}, bf16[4,256,128]{2,1,0:T(8,128)(2,1)S(1)}, u32[]{:S(2)}, u32[]{:S(2)}) collective-permute-start(bf16[4,256,128]{2,1,0:T(8,128)(2,1)S(1)} %get-tuple-element.14.refs_0_), channel_id=1, source_target_pairs={{16,32},{32,16},{24,40},{40,24},{48,64},{64,48},{56,72},{72,56},{8... | collective-permute-start | bytes 786440 | tf_op jit(solution)/shard_map/ppermute | solution.py:231
  9.4 2.6 %collective-permute-start = (bf16[4,256,128]{2,1,0:T(8,128)(2,1)S(1)}, bf16[4,256,128]{2,1,0:T(8,128)(2,1)S(1)}, u32[]{:S(2)}, u32[]{:S(2)}) collective-permute-start(bf16[4,256,128]{2,1,0:T(8,128)(2,1)S(1)} %get-tuple-element.14.refs_0_), channel_id=1, source_target_pairs={{0,32},{32,0},{8,40},{40,8},{16,48},{48,16},{24,56},{56,24},{64,96... | collective-permute-start | bytes 786440 | tf_op jit(solution)/shard_map/ppermute | solution.py:232
  12.1 1.8 %collective-permute-done.9.o1 = bf16[256,1024]{1,0:T(8,128)(2,1)S(1)} collective-permute-done((bf16[256,1024]{1,0:T(8,128)(2,1)}, bf16[256,1024]{1,0:T(8,128)(2,1)S(1)}, u32[]{:S(2)}, u32[]{:S(2)}) %collective-permute-start.9) | collective-permute-done | bytes 524320 | tf_op jit(solution)/shard_map/ppermute | solution.py:236
  13.9 1.1 %pad_maximum_fusion = bf16[2,256,1024]{2,1,0:T(8,128)(2,1)} fusion(bf16[1,256,1024]{2,1,0:T(8,128)(2,1)S(1)} %bitcast.23, bf16[1,256,1024]{2,1,0:T(8,128)(2,1)S(1)} %bitcast.22), kind=kLoop, calls=%fused_computation | loop fusion | flops 524288 | bytes 2097152 | tf_op jit(solution)/shard_map/stack | solution.py:237
  15.0 2.8 %collective-permute-start.10 = (bf16[2,256,1024]{2,1,0:T(8,128)(2,1)}, bf16[2,256,1024]{2,1,0:T(8,128)(2,1)}, u32[]{:S(2)}, u32[]{:S(2)}) collective-permute-start(bf16[2,256,1024]{2,1,0:T(8,128)(2,1)} %pad_maximum_fusion), channel_id=1, source_target_pairs={{0,6},{2,4},{4,2},{6,0},{1,7},{3,5},{5,3},{7,1},{8,14},{10,12},{12... | collective-permute-start | bytes 3145736 | tf_op jit(solution)/shard_map/ppermute | solution.py:237
  18.0 6.4 %collective-permute-start.1 = (bf16[4,256,128]{2,1,0:T(8,128)(2,1)S(1)}, bf16[4,256,128]{2,1,0:T(8,128)(2,1)S(1)}, u32[]{:S(2)}, u32[]{:S(2)}) collective-permute-start(bf16[4,256,128]{2,1,0:T(8,128)(2,1)S(1)} %get-tuple-element.14.refs_0_), channel_id=1, source_target_pairs={{32,64},{64,32},{40,72},{72,40},{48,80},{80,48},{56,88},{88,56},{9... | collective-permute-start | bytes 786440 | tf_op jit(solution)/shard_map/ppermute | solution.py:233
  24.7 3.1 %attend.3.refs_3_ = f32[8,128,128]{2,1,0:T(8,128)S(1)} custom-call(f32[2,14]{1,0:T(2,128)S(1)} %compare_select_fusion.2.bias_ref, bf16[4,256,128]{2,1,0:T(8,128)(2,1)S(1)} %get-tuple-element.13.q_ref, bf16[4,256,128]{2,1,0:T(8,128)(2,1)S(1)} %get-tuple-element.14.refs_0_, bf16[4,256,128]{2,1,0:T(8,128)(2,1)S(1)} %collective-permute-done.5.refs_1_), custom_call_target="tpu_custom_call" | custom-call | flops 268435456 | bytes 1000000 | tf_op jit(solution)/shard_map/attend/pallas_call | solution.py:116
  27.8 3.8 %attend.4.refs_2_ = f32[8,128,128]{2,1,0:T(8,128)S(1)} custom-call(f32[2,14]{1,0:T(2,128)S(1)} %compare_select_fusion.2.bias_ref, bf16[4,256,128]{2,1,0:T(8,128)(2,1)S(1)} %get-tuple-element.13.q_ref, bf16[4,256,128]{2,1,0:T(8,128)(2,1)S(1)} %collective-permute-done.2.refs_0_, bf16[4,256,128]{2,1,0:T(8,128)(2,1)S(1)} %collective-permute-done.3.refs_1_, ...), custom_call_target="tpu_custom_call" | custom-call | flops 268435456 | bytes 1000000 | tf_op jit(solution)/shard_map/attend/pallas_call | solution.py:116
  31.7 3.4 %attend.5.a0 = bf16[256,256]{1,0:T(8,128)(2,1)S(1)} custom-call(f32[2,14]{1,0:T(2,128)S(1)} %compare_select_fusion.2.bias_ref, bf16[4,256,128]{2,1,0:T(8,128)(2,1)S(1)} %get-tuple-element.13.q_ref, bf16[4,256,128]{2,1,0:T(8,128)(2,1)S(1)} %collective-permute-done.refs_0_, bf16[4,256,128]{2,1,0:T(8,128)(2,1)S(1)} %collective-permute-done.1.refs_1_, ...), custom_call_target="tpu_custom_call" | custom-call | flops 134217728 | bytes 1000000 | tf_op jit(solution)/shard_map/attend/pallas_call | solution.py:116
  35.4 4.6 %collective-permute-start.7 = (bf16[256,256]{1,0:T(8,128)(2,1)S(1)}, bf16[256,256]{1,0:T(8,128)(2,1)S(1)}, u32[]{:S(2)}, u32[]{:S(2)}) collective-permute-start(bf16[256,256]{1,0:T(8,128)(2,1)S(1)} %attend.5.a0), channel_id=1, source_target_pairs={{0,4},{2,6},{4,0},{6,2},{1,5},{3,7},{5,1},{7,3},{8,12},{10,14},{12... | collective-permute-start | bytes 393224 | tf_op jit(solution)/shard_map/ppermute | solution.py:244
  40.5 1.3 %slice_bitcast_fusion = (bf16[256,1024]{1,0:T(8,128)(2,1)S(1)}, bf16[256,1024]{1,0:T(8,128)(2,1)S(1)}) fusion(bf16[2,256,1024]{2,1,0:T(8,128)(2,1)} %collective-permute-done.10), kind=kLoop, calls=%fused_computation.1 | loop fusion | bytes 2097152 | tf_op jit(solution)/shard_map/squeeze | solution.py:238
  41.8 5.2 %collective-permute-done.7.a2 = bf16[256,256]{1,0:T(8,128)(2,1)S(1)} collective-permute-done((bf16[256,256]{1,0:T(8,128)(2,1)S(1)}, bf16[256,256]{1,0:T(8,128)(2,1)S(1)}, u32[]{:S(2)}, u32[]{:S(2)}) %collective-permute-start.7) | collective-permute-done | bytes 131104 | tf_op jit(solution)/shard_map/ppermute | solution.py:244
  47.0 2.6 %collective-permute-done.8.a3 = bf16[256,256]{1,0:T(8,128)(2,1)S(1)} collective-permute-done((bf16[256,256]{1,0:T(8,128)(2,1)S(1)}, bf16[256,256]{1,0:T(8,128)(2,1)S(1)}, u32[]{:S(2)}, u32[]{:S(2)}) %collective-permute-start.8) | collective-permute-done | bytes 131104 | tf_op jit(solution)/shard_map/ppermute | solution.py:244
  49.6 2.8 %feed.1 = (f32[64,1024]{1,0:T(8,128)S(1)}, bf16[64,1024]{1,0:T(8,128)(2,1)S(1)}, bf16[64,1024]{1,0:T(8,128)(2,1)S(1)}, bf16[64,1024]{1,0:T(8,128)(2,1)S(1)}) custom-call(s32[1]{0:T(128)} %bitcast.2.head_ref, bf16[256,1024]{1,0:T(8,128)(2,1)S(1)} %bitcast.21, bf16[256,256]{1,0:T(8,128)(2,1)S(1)} %attend.5.a0, bf16[256,256]{1,0:T(8,128)(2,1)S(1)} %collective-permute-done.6.a1, ...), custom_call_target="tpu_custom_call" | custom-call | flops 1610612736 | bytes 8000000 | tf_op jit(solution)/shard_map/feed/pallas_call | solution.py:164
  52.4 0.7 copy-done.8
  53.1 2.0 %collective-permute-start.12 = (bf16[64,1024]{1,0:T(8,128)(2,1)S(1)}, bf16[64,1024]{1,0:T(8,128)(2,1)S(1)}, u32[]{:S(2)}, u32[]{:S(2)}) collective-permute-start(bf16[64,1024]{1,0:T(8,128)(2,1)S(1)} %get-tuple-element.17), channel_id=1, source_target_pairs={{0,4},{2,6},{4,0},{6,2},{1,5},{3,7},{5,1},{7,3},{8,12},{10,14},{12... | collective-permute-start | bytes 393224 | tf_op jit(solution)/shard_map/ppermute | solution.py:246
  55.1 2.7 %collective-permute-start.13 = (bf16[64,1024]{1,0:T(8,128)(2,1)S(1)}, bf16[64,1024]{1,0:T(8,128)(2,1)S(1)}, u32[]{:S(2)}, u32[]{:S(2)}) collective-permute-start(bf16[64,1024]{1,0:T(8,128)(2,1)S(1)} %get-tuple-element.18), channel_id=1, source_target_pairs={{0,6},{2,4},{4,2},{6,0},{1,7},{3,5},{5,3},{7,1},{8,14},{10,12},{12... | collective-permute-start | bytes 393224 | tf_op jit(solution)/shard_map/ppermute | solution.py:246
  57.8 1.7 %collective-permute-done.11.r1 = bf16[64,1024]{1,0:T(8,128)(2,1)S(1)} collective-permute-done((bf16[64,1024]{1,0:T(8,128)(2,1)S(1)}, bf16[64,1024]{1,0:T(8,128)(2,1)S(1)}, u32[]{:S(2)}, u32[]{:S(2)}) %collective-permute-start.11) | collective-permute-done | bytes 131104 | tf_op jit(solution)/shard_map/ppermute | solution.py:246
  59.4 1.7 %collective-permute-done.12.r2 = bf16[64,1024]{1,0:T(8,128)(2,1)S(1)} collective-permute-done((bf16[64,1024]{1,0:T(8,128)(2,1)S(1)}, bf16[64,1024]{1,0:T(8,128)(2,1)S(1)}, u32[]{:S(2)}, u32[]{:S(2)}) %collective-permute-start.12) | collective-permute-done | bytes 131104 | tf_op jit(solution)/shard_map/ppermute | solution.py:246
  61.1 2.1 %collective-permute-done.13.r3 = bf16[64,1024]{1,0:T(8,128)(2,1)S(1)} collective-permute-done((bf16[64,1024]{1,0:T(8,128)(2,1)S(1)}, bf16[64,1024]{1,0:T(8,128)(2,1)S(1)}, u32[]{:S(2)}, u32[]{:S(2)}) %collective-permute-start.13) | collective-permute-done | bytes 131104 | tf_op jit(solution)/shard_map/ppermute | solution.py:246
  63.2 0.6 copy-done.11
  63.8 1.8 %gather.1 = (f32[32,1024]{1,0:T(8,128)}, bf16[32,1024]{1,0:T(8,128)(2,1)}) custom-call(s32[1]{0:T(128)} %bitcast.1.branch_ref, f32[64,1024]{1,0:T(8,128)} %copy-done.8, bf16[64,1024]{1,0:T(8,128)(2,1)} %copy-done.9, bf16[64,1024]{1,0:T(8,128)(2,1)} %copy-done.10, bf16[64,1024]{1,0:T(8,128)(2,1)} %copy-done.11), custom_call_target="tpu_custom_call" | custom-call | tf_op jit(solution)/shard_map/gather/pallas_call | solution.py:195
  65.7 7.7 %collective-permute-start.14 = (bf16[32,1024]{1,0:T(8,128)(2,1)}, bf16[32,1024]{1,0:T(8,128)(2,1)S(1)}, u32[]{:S(2)}, u32[]{:S(2)}) collective-permute-start(bf16[32,1024]{1,0:T(8,128)(2,1)} %get-tuple-element.20), channel_id=1, source_target_pairs={{0,1},{1,0},{2,3},{3,2},{4,5},{5,4},{6,7},{7,6},{8,9},{9,8},{10,11... | collective-permute-start | bytes 196616 | tf_op jit(solution)/shard_map/ppermute | solution.py:248
  74.1 1.9 %collective-permute-done.14 = bf16[32,1024]{1,0:T(8,128)(2,1)S(1)} collective-permute-done((bf16[32,1024]{1,0:T(8,128)(2,1)}, bf16[32,1024]{1,0:T(8,128)(2,1)S(1)}, u32[]{:S(2)}, u32[]{:S(2)}) %collective-permute-start.14) | collective-permute-done | bytes 65568 | tf_op jit(solution)/shard_map/ppermute | solution.py:248
  76.0 1.6 %add_convert_fusion = bf16[32,1024]{1,0:T(8,128)(2,1)} fusion(bf16[32,1024]{1,0:T(8,128)(2,1)S(1)} %collective-permute-done.14, f32[32,1024]{1,0:T(8,128)} %get-tuple-element.19, f32[]{:T(128)S(6)} %sub.40, f32[]{:T(128)S(6)} %select_n.52), kind=kLoop, calls=%fused_computation.4 | loop fusion | flops 163840 | bytes 262152 | tf_op jit(solution)/shard_map/convert_element_type | solution.py:252
  (44 shorter events, 1.6 us)
Async XLA Ops:
  0.0 13.9 %collective-permute-start.9 = (bf16[256,1024]{1,0:T(8,128)(2,1)}, bf16[256,1024]{1,0:T(8,128)(2,1)S(1)}, u32[]{:S(2)}, u32[]{:S(2)}) collective-permute-start(bf16[256,1024]{1,0:T(8,128)(2,1)} %o0.1), channel_id=1, source_target_pairs={{0,2},{2,0},{4,6},{6,4},{1,3},{3,1},{5,7},{7,5},{8,10},{10,8},{12,... | collective-permute-start | bytes 1572872 | tf_op jit(solution)/shard_map/ppermute | solution.py:236
  1.5 1.0 %copy-start.2 = (bf16[1,2,128,1024]{3,2,1,0:T(8,128)(2,1)S(1)}, bf16[1,2,128,1024]{3,2,1,0:T(8,128)(2,1)}, u32[]{:S(2)}) copy-start(bf16[1,2,128,1024]{3,2,1,0:T(8,128)(2,1)} %param.10) | copy-start | bytes 1572868
  2.5 1.0 %copy-start.5 = (bf16[1024,256]{1,0:T(8,128)(2,1)S(1)}, bf16[1024,256]{1,0:T(8,128)(2,1)}, u32[]{:S(2)}) copy-start(bf16[1024,256]{1,0:T(8,128)(2,1)} %wq_ref.1) | copy-start | bytes 1572868
  3.6 1.0 %copy-start.6 = (bf16[1024,256]{1,0:T(8,128)(2,1)S(1)}, bf16[1024,256]{1,0:T(8,128)(2,1)}, u32[]{:S(2)}) copy-start(bf16[1024,256]{1,0:T(8,128)(2,1)} %wk_ref.1) | copy-start | bytes 1572868
  4.6 1.0 %copy-start.7 = (bf16[1024,256]{1,0:T(8,128)(2,1)S(1)}, bf16[1024,256]{1,0:T(8,128)(2,1)}, u32[]{:S(2)}) copy-start(bf16[1024,256]{1,0:T(8,128)(2,1)} %wv_ref.1) | copy-start | bytes 1572868
  5.7 8.2 %copy-start.4 = (bf16[256,1024]{1,0:T(8,128)(2,1)S(1)}, bf16[256,1024]{1,0:T(8,128)(2,1)}, u32[]{:S(2)}) copy-start(bf16[256,1024]{1,0:T(8,128)(2,1)} %o0.1) | copy-start | bytes 1572868
  5.7 12.2 %copy-start.13 = (s32[2]{0:T(128)S(1)}, s32[2]{0:T(128)}, u32[]{:S(2)}) copy-start(s32[2]{0:T(128)} %param.12) | copy-start | bytes 28
  5.7 12.3 %copy-start.12 = (s32[8,2]{0,1:T(2,128)S(1)}, s32[8,2]{0,1:T(2,128)}, u32[]{:S(2)}) copy-start(s32[8,2]{0,1:T(2,128)} %param.11) | copy-start | bytes 196
  6.3 18.4 %collective-permute-start.5 = (bf16[4,256,128]{2,1,0:T(8,128)(2,1)S(1)}, bf16[4,256,128]{2,1,0:T(8,128)(2,1)S(1)}, u32[]{:S(2)}, u32[]{:S(2)}) collective-permute-start(bf16[4,256,128]{2,1,0:T(8,128)(2,1)S(1)} %get-tuple-element.14.refs_0_), channel_id=1, source_target_pairs={{0,8},{8,0},{16,24},{24,16},{32,40},{40,32},{48,56},{56,48},{64,72... | collective-permute-start | bytes 786440 | tf_op jit(solution)/shard_map/ppermute | solution.py:229
  6.4 11.6 %collective-permute-start.2 = (bf16[4,256,128]{2,1,0:T(8,128)(2,1)S(1)}, bf16[4,256,128]{2,1,0:T(8,128)(2,1)S(1)}, u32[]{:S(2)}, u32[]{:S(2)}) collective-permute-start(bf16[4,256,128]{2,1,0:T(8,128)(2,1)S(1)} %get-tuple-element.14.refs_0_), channel_id=1, source_target_pairs={{0,16},{16,0},{8,24},{24,8},{32,48},{48,32},{40,56},{56,40},{64,80... | collective-permute-start | bytes 786440 | tf_op jit(solution)/shard_map/ppermute | solution.py:230
  7.2 17.3 %collective-permute-start.3 = (bf16[4,256,128]{2,1,0:T(8,128)(2,1)S(1)}, bf16[4,256,128]{2,1,0:T(8,128)(2,1)S(1)}, u32[]{:S(2)}, u32[]{:S(2)}) collective-permute-start(bf16[4,256,128]{2,1,0:T(8,128)(2,1)S(1)} %get-tuple-element.14.refs_0_), channel_id=1, source_target_pairs={{16,32},{32,16},{24,40},{40,24},{48,64},{64,48},{56,72},{72,56},{8... | collective-permute-start | bytes 786440 | tf_op jit(solution)/shard_map/ppermute | solution.py:231
  9.4 22.3 %collective-permute-start = (bf16[4,256,128]{2,1,0:T(8,128)(2,1)S(1)}, bf16[4,256,128]{2,1,0:T(8,128)(2,1)S(1)}, u32[]{:S(2)}, u32[]{:S(2)}) collective-permute-start(bf16[4,256,128]{2,1,0:T(8,128)(2,1)S(1)} %get-tuple-element.14.refs_0_), channel_id=1, source_target_pairs={{0,32},{32,0},{8,40},{40,8},{16,48},{48,16},{24,56},{56,24},{64,96... | collective-permute-start | bytes 786440 | tf_op jit(solution)/shard_map/ppermute | solution.py:232
  15.0 25.6 %collective-permute-start.10 = (bf16[2,256,1024]{2,1,0:T(8,128)(2,1)}, bf16[2,256,1024]{2,1,0:T(8,128)(2,1)}, u32[]{:S(2)}, u32[]{:S(2)}) collective-permute-start(bf16[2,256,1024]{2,1,0:T(8,128)(2,1)} %pad_maximum_fusion), channel_id=1, source_target_pairs={{0,6},{2,4},{4,2},{6,0},{1,7},{3,5},{5,3},{7,1},{8,14},{10,12},{12... | collective-permute-start | bytes 3145736 | tf_op jit(solution)/shard_map/ppermute | solution.py:237
  18.0 13.6 %collective-permute-start.1 = (bf16[4,256,128]{2,1,0:T(8,128)(2,1)S(1)}, bf16[4,256,128]{2,1,0:T(8,128)(2,1)S(1)}, u32[]{:S(2)}, u32[]{:S(2)}) collective-permute-start(bf16[4,256,128]{2,1,0:T(8,128)(2,1)S(1)} %get-tuple-element.14.refs_0_), channel_id=1, source_target_pairs={{32,64},{64,32},{40,72},{72,40},{48,80},{80,48},{56,88},{88,56},{9... | collective-permute-start | bytes 786440 | tf_op jit(solution)/shard_map/ppermute | solution.py:233
  24.5 3.3 %collective-permute-start.4 = (bf16[4,256,128]{2,1,0:T(8,128)(2,1)S(1)}, bf16[4,256,128]{2,1,0:T(8,128)(2,1)S(1)}, u32[]{:S(2)}, u32[]{:S(2)}) collective-permute-start(bf16[4,256,128]{2,1,0:T(8,128)(2,1)S(1)} %broadcast_select_fusion), channel_id=1, source_target_pairs={{0,8},{8,0},{16,24},{24,16},{32,40},{40,32},{48,56},{56,48},{64,72... | collective-permute-start | bytes 786440 | tf_op jit(solution)/shard_map/ppermute | solution.py:234
  27.8 21.7 %copy-start.1 = (bf16[1024,1024]{1,0:T(8,128)(2,1)S(1)}, bf16[1024,1024]{1,0:T(8,128)(2,1)}, u32[]{:S(2)}) copy-start(bf16[1024,1024]{1,0:T(8,128)(2,1)} %wback_hbm.1) | copy-start | bytes 6291460
  31.6 17.9 %copy-start = (bf16[1024,1024]{1,0:T(8,128)(2,1)S(1)}, bf16[1024,1024]{1,0:T(8,128)(2,1)}, u32[]{:S(2)}) copy-start(bf16[1024,1024]{1,0:T(8,128)(2,1)} %win_hbm.1) | copy-start | bytes 6291460
  31.6 17.9 %copy-start.3 = (bf16[1,2,128,1024]{3,2,1,0:T(8,128)(2,1)S(1)}, bf16[1,2,128,1024]{3,2,1,0:T(8,128)(2,1)}, u32[]{:S(2)}) copy-start(bf16[1,2,128,1024]{3,2,1,0:T(8,128)(2,1)} %param.10) | copy-start | bytes 1572868
  35.1 6.7 %collective-permute-start.6 = (bf16[256,256]{1,0:T(8,128)(2,1)S(1)}, bf16[256,256]{1,0:T(8,128)(2,1)S(1)}, u32[]{:S(2)}, u32[]{:S(2)}) collective-permute-start(bf16[256,256]{1,0:T(8,128)(2,1)S(1)} %attend.5.a0), channel_id=1, source_target_pairs={{0,2},{2,0},{4,6},{6,4},{1,3},{3,1},{5,7},{7,5},{8,10},{10,8},{12,... | collective-permute-start | bytes 393224 | tf_op jit(solution)/shard_map/ppermute | solution.py:244
  35.4 11.5 %collective-permute-start.7 = (bf16[256,256]{1,0:T(8,128)(2,1)S(1)}, bf16[256,256]{1,0:T(8,128)(2,1)S(1)}, u32[]{:S(2)}, u32[]{:S(2)}) collective-permute-start(bf16[256,256]{1,0:T(8,128)(2,1)S(1)} %attend.5.a0), channel_id=1, source_target_pairs={{0,4},{2,6},{4,0},{6,2},{1,5},{3,7},{5,1},{7,3},{8,12},{10,14},{12... | collective-permute-start | bytes 393224 | tf_op jit(solution)/shard_map/ppermute | solution.py:244
  40.0 9.6 %collective-permute-start.8 = (bf16[256,256]{1,0:T(8,128)(2,1)S(1)}, bf16[256,256]{1,0:T(8,128)(2,1)S(1)}, u32[]{:S(2)}, u32[]{:S(2)}) collective-permute-start(bf16[256,256]{1,0:T(8,128)(2,1)S(1)} %attend.5.a0), channel_id=1, source_target_pairs={{0,6},{2,4},{4,2},{6,0},{1,7},{3,5},{5,3},{7,1},{8,14},{10,12},{12... | collective-permute-start | bytes 393224 | tf_op jit(solution)/shard_map/ppermute | solution.py:244
  52.4 0.7 copy-start.8
  53.1 6.4 %collective-permute-start.11 = (bf16[64,1024]{1,0:T(8,128)(2,1)S(1)}, bf16[64,1024]{1,0:T(8,128)(2,1)S(1)}, u32[]{:S(2)}, u32[]{:S(2)}) collective-permute-start(bf16[64,1024]{1,0:T(8,128)(2,1)S(1)} %get-tuple-element.16), channel_id=1, source_target_pairs={{0,2},{2,0},{4,6},{6,4},{1,3},{3,1},{5,7},{7,5},{8,10},{10,8},{12,... | collective-permute-start | bytes 393224 | tf_op jit(solution)/shard_map/ppermute | solution.py:246
  53.1 8.1 %collective-permute-start.12 = (bf16[64,1024]{1,0:T(8,128)(2,1)S(1)}, bf16[64,1024]{1,0:T(8,128)(2,1)S(1)}, u32[]{:S(2)}, u32[]{:S(2)}) collective-permute-start(bf16[64,1024]{1,0:T(8,128)(2,1)S(1)} %get-tuple-element.17), channel_id=1, source_target_pairs={{0,4},{2,6},{4,0},{6,2},{1,5},{3,7},{5,1},{7,3},{8,12},{10,14},{12... | collective-permute-start | bytes 393224 | tf_op jit(solution)/shard_map/ppermute | solution.py:246
  55.1 8.1 %collective-permute-start.13 = (bf16[64,1024]{1,0:T(8,128)(2,1)S(1)}, bf16[64,1024]{1,0:T(8,128)(2,1)S(1)}, u32[]{:S(2)}, u32[]{:S(2)}) collective-permute-start(bf16[64,1024]{1,0:T(8,128)(2,1)S(1)} %get-tuple-element.18), channel_id=1, source_target_pairs={{0,6},{2,4},{4,2},{6,0},{1,7},{3,5},{5,3},{7,1},{8,14},{10,12},{12... | collective-permute-start | bytes 393224 | tf_op jit(solution)/shard_map/ppermute | solution.py:246
  59.4 3.8 %copy-start.9 = (bf16[64,1024]{1,0:T(8,128)(2,1)}, bf16[64,1024]{1,0:T(8,128)(2,1)S(1)}, u32[]{:S(2)}) copy-start(bf16[64,1024]{1,0:T(8,128)(2,1)S(1)} %collective-permute-done.11.r1) | copy-start | bytes 393220
  61.1 2.1 %copy-start.10 = (bf16[64,1024]{1,0:T(8,128)(2,1)}, bf16[64,1024]{1,0:T(8,128)(2,1)S(1)}, u32[]{:S(2)}) copy-start(bf16[64,1024]{1,0:T(8,128)(2,1)S(1)} %collective-permute-done.12.r2) | copy-start | bytes 393220
  63.2 0.7 copy-start.11
  65.7 10.3 %collective-permute-start.14 = (bf16[32,1024]{1,0:T(8,128)(2,1)}, bf16[32,1024]{1,0:T(8,128)(2,1)S(1)}, u32[]{:S(2)}, u32[]{:S(2)}) collective-permute-start(bf16[32,1024]{1,0:T(8,128)(2,1)} %get-tuple-element.20), channel_id=1, source_target_pairs={{0,1},{1,0},{2,3},{3,2},{4,5},{5,4},{6,7},{7,6},{8,9},{9,8},{10,11... | collective-permute-start | bytes 196616 | tf_op jit(solution)/shard_map/ppermute | solution.py:248

commit v2 on v1

v2 whole, which is shorter than its diff:
```python
import functools

import jax
import jax.numpy as jnp
from jax import lax
from jax.experimental import pallas as pl
from jax.experimental.pallas import tpu as pltpu
from jax.sharding import PartitionSpec as P

HD = 64
ROUNDS = 8
BIASES = 16
DIAGONAL = (2, 3, 5, 6)
MASKED = -1e30
LOG2E = 1.4426950408889634

NT = (((1,), (1,)), ((), ()))
VMEM = pl.BlockSpec(memory_space=pltpu.VMEM)
SMEM = pl.BlockSpec(memory_space=pltpu.SMEM)
HBM = pl.BlockSpec(memory_space=pltpu.HBM)
ANY = pl.BlockSpec(memory_space=pl.ANY)


def params(mib):
    return pltpu.CompilerParams(vmem_limit_bytes=int(mib * 1024 * 1024))


def shifted(axis, count, apart):
    return functools.partial(lax.ppermute, axis_name=axis, perm=[(i, (i - apart) % count) for i in range(count)])


def flipped(axis, count, bits):
    return functools.partial(lax.ppermute, axis_name=axis, perm=[(i, i ^ bits) for i in range(count)])


def held(shape, dtype):
    return pltpu.VMEM(shape, dtype)


def outside(*arrays):
    return tuple(pltpu.with_memory_space_constraint(a, pltpu.HBM) for a in arrays)


COST = pl.CostEstimate(flops=1000, bytes_accessed=1000, transcendentals=0)


def dot(a, b):
    return jnp.dot(a, b, preferred_element_type=jnp.float32)


def chunked(source, target, sems, count):
    rows = source.shape[0] // count
    pieces = [pl.ds(i * rows, rows) for i in range(count)]
    return [pltpu.make_async_copy(source.at[p], target.at[p], sems.at[i]) for i, p in enumerate(pieces)]


def key_views(count):
    me = lax.axis_index("view")
    core = me & 1
    sources = (me, me + 1 - 2 * core, me + 2, me - 2, me - 1 + 2 * core, me + 4, me - 4)
    return [2 * lax.rem(s + count, count) for s in sources]


def bias_kernel(count, partners_ref, counts_ref, bias_ref):
    bias_ref[...] = jnp.zeros_like(bias_ref)
    firsts = key_views(count)
    for qv in range(2):
        used = counts_ref[qv]
        named = [jnp.where(r < used, partners_ref[qv, r], -1) for r in range(ROUNDS)]
        for slot, first in enumerate(firsts):
            for kvw in range(2):
                if (slot in DIAGONAL or slot == 0) and (kvw == qv) == (slot == 0):
                    continue
                times = sum((n == first + kvw).astype(jnp.int32) for n in named)
                row = BIASES * qv + 2 * slot + kvw
                bias_ref[row : row + 1] = jnp.full((1, bias_ref.shape[1]), times.astype(jnp.float32))
    times = bias_ref[...]
    bias_ref[...] = jnp.where(times > 0, jnp.log2(jnp.maximum(times, 1.0)), MASKED)
    for qv in range(2):
        row = BIASES * qv + qv
        bias_ref[row : row + 1] = jnp.zeros((1, bias_ref.shape[1]), jnp.float32)


def biases(count, partners, counts):
    return pl.pallas_call(
        functools.partial(bias_kernel, count),
        out_shape=held((2 * BIASES, 2 * HD), jnp.float32),
        in_specs=[SMEM, SMEM],
        out_specs=VMEM,
        compiler_params=params(2),
        cost_estimate=COST,
        name="biases",
    )(partners, counts)


def project_kernel(x_hbm, wk_hbm, wv_hbm, wq_hbm, q_ref, kv_ref, x, wk, wv, wq, sems):
    loads = [
        chunked(source, target, sems.at[i], sems.shape[1])
        for i, (source, target) in enumerate(((x_hbm, x), (wk_hbm, wk), (wv_hbm, wv), (wq_hbm, wq)))
    ]
    for copies in loads:
        for copy in copies:
            copy.start()

    def arrived(i):
        for copy in loads[i]:
            copy.wait()

    rows = x.shape[0]
    arrived(0)
    arrived(1)
    kv_ref[:rows] = dot(x[...], wk[...]).astype(jnp.bfloat16)
    arrived(2)
    kv_ref[rows:] = dot(x[...], wv[...]).T.astype(jnp.bfloat16)
    arrived(3)
    q_ref[...] = (dot(x[...], wq[...]) * (HD ** (-0.5) * LOG2E)).astype(jnp.bfloat16)


def project(x, w_query, w_key, w_value):
    rows, width = x.shape
    columns = w_query.shape[1]
    chunks = 1
    return pl.pallas_call(
        project_kernel,
        out_shape=(
            held((rows, columns), jnp.bfloat16),
            held((rows + columns, rows), jnp.bfloat16),
        ),
        in_specs=[HBM] * 4,
        out_specs=(VMEM, VMEM),
        scratch_shapes=[pltpu.VMEM(x.shape, jnp.bfloat16)]
        + [pltpu.VMEM((width, columns), jnp.bfloat16)] * 3
        + [pltpu.SemaphoreType.DMA((4, chunks))],
        compiler_params=params(8),
        cost_estimate=COST,
        name="project",
    )(*outside(x, w_key, w_value, w_query))


def attend_kernel(blocks, first, last, bias_ref, q_ref, *refs):
    count = len(blocks)
    kv_refs = refs[:count]
    refs = refs[count:]
    if not first:
        held_ref, held_tops_ref = refs[:2]
        refs = refs[2:]
    refs = refs[-1:] if last else refs[-2:]
    rows, columns = q_ref.shape
    tok, heads = rows // 2, columns // HD
    lane = lax.broadcasted_iota(jnp.int32, (tok, columns), 1)
    for qv in range(2):
        mine = slice(qv * tok, (qv + 1) * tok)
        q = q_ref[mine]
        apart = jnp.concatenate([jnp.where(lane // HD == h, q, jnp.zeros_like(q)) for h in range(heads)], axis=0)
        scores, biases, values = [], [], []
        for (slot, part, both), kv_ref in zip(blocks, kv_refs):
            base = part * (rows + columns)
            for kvw in (0, 1) if both else (qv,):
                span = slice(kvw * tok, (kvw + 1) * tok)
                keys = kv_ref[base + kvw * tok : base + (kvw + 1) * tok]
                scores.append(lax.dot_general(keys, apart, NT, preferred_element_type=jnp.float32))
                row = BIASES * qv + 2 * slot + kvw
                biases.append(jnp.concatenate([bias_ref[row : row + 1]] * heads, axis=1))
                values.append(kv_ref[base + rows : base + rows + columns, span])
        top = functools.reduce(jnp.maximum, [jnp.max(s, axis=0, keepdims=True) + b for s, b in zip(scores, biases)])
        if not first:
            old_top, old_total = held_tops_ref[2 * qv : 2 * qv + 1], held_tops_ref[2 * qv + 1 : 2 * qv + 2]
            top = jnp.maximum(top, old_top)
            scale = jnp.exp2(old_top - top)
        weights = [jnp.exp2(s - (top - b)) for s, b in zip(scores, biases)]
        total = jnp.sum(functools.reduce(jnp.add, weights), axis=0, keepdims=True)
        if not first:
            total = total + scale * old_total
        rounded = jnp.concatenate([w.astype(jnp.bfloat16) for w in weights], axis=0)
        values = jnp.concatenate(values, axis=1)
        finished = []
        for p in range(heads // 2):
            two = dot(values[2 * p * HD : 2 * (p + 1) * HD], rounded[:, 2 * p * tok : 2 * (p + 1) * tok])
            for h in (2 * p, 2 * p + 1):
                lanes = slice(h * tok, (h + 1) * tok)
                blended = two[(h - 2 * p) * HD : (h - 2 * p + 1) * HD, (h - 2 * p) * tok : (h - 2 * p + 1) * tok]
                at = slice((qv * heads + h) * HD, (qv * heads + h + 1) * HD)
                if not first:
                    blended = blended + scale[:, lanes] * held_ref[at]
                if last:
                    finished.append(blended / total[:, lanes])
                else:
                    refs[0][at] = blended
        if last:
            refs[0][mine] = jnp.concatenate(finished, axis=0).T.astype(jnp.bfloat16)
        else:
            refs[1][2 * qv : 2 * qv + 1] = top
            refs[1][2 * qv + 1 : 2 * qv + 2] = total


def attend(blocks, first, last, bias, q, kvs, state=(), *after):
    rows, columns = q.shape
    tok, heads = rows // 2, columns // HD
    if last:
        out = held((rows, columns), jnp.bfloat16)
    else:
        out = (
            held((2 * columns, tok), jnp.float32),
            held((4, heads * tok), jnp.float32),
        )
    return pl.pallas_call(
        functools.partial(attend_kernel, blocks, first, last),
        out_shape=out,
        in_specs=[VMEM] * (2 + len(kvs) + len(state)) + [ANY] * len(after),
        out_specs=VMEM if last else (VMEM, VMEM),
        compiler_params=params(16),
        cost_estimate=COST,
        name="attend",
    )(bias, q, *kvs, *state, *after)


def pick_kernel(own_ref, a_ref, b_ref, *refs):
    rows = own_ref.shape[0]
    out_ref = refs[-1]
    out_ref[:rows] = own_ref[...]
    first = lax.axis_index("view") & 1 == 0

    @pl.when(first)
    def _():
        out_ref[rows:] = a_ref[...]

    @pl.when(jnp.logical_not(first))
    def _():
        out_ref[rows:] = b_ref[...]


def pick(own, a, b, *after):
    return pl.pallas_call(
        pick_kernel,
        out_shape=held((2 * own.shape[0], own.shape[1]), a.dtype),
        in_specs=[VMEM] * 3 + [ANY] * len(after),
        out_specs=VMEM,
        compiler_params=params(2),
        cost_estimate=COST,
        name="pick",
    )(own, a, b, *after)


def halves_kernel(a_ref, b_ref, after_ref, out_ref):
    half = a_ref.shape[0] // 2
    block = out_ref.shape[1]
    rows = pl.ds(pl.multiple_of((lax.axis_index("view") & 1) * half, half), half)
    for j in range(a_ref.shape[1] // block):
        columns = slice(j * block, (j + 1) * block)
        out_ref[2 * j * half : (2 * j + 1) * half] = a_ref[rows, columns]
        out_ref[(2 * j + 1) * half : (2 * j + 2) * half] = b_ref[rows, columns]


def halves(a, b, after):
    rows, columns = a.shape
    return pl.pallas_call(
        halves_kernel,
        out_shape=held((columns, rows), a.dtype),
        in_specs=[VMEM, VMEM, ANY],
        out_specs=VMEM,
        compiler_params=params(2),
        cost_estimate=COST,
        name="halves",
    )(a, b, after)


def kept_until_kernel(a_ref, after_ref, out_ref):
    out_ref[...] = a_ref[...]


def kept_until(a, after):
    return pl.pallas_call(
        kept_until_kernel,
        out_shape=held(a.shape, a.dtype),
        in_specs=[VMEM, ANY],
        out_specs=VMEM,
        compiler_params=params(2),
        cost_estimate=COST,
        name="kept_until",
    )(a, after)


def feed_kernel(x_ref, a0, a1, a2, a3, o0, o1, mine, pair, win_ref, wback_ref, own_ref, r1, r2, r3):
    head = lax.axis_index("head")
    rows, width = x_ref.shape
    tok = rows // 2
    part = tok // 4

    def turned(ref, columns=slice(None)):
        pieces = []
        for j in range(4):
            for view in range(2):
                start = pl.multiple_of(view * tok + jnp.bitwise_xor(head, j) * part, part)
                pieces.append(ref[pl.ds(start, part), columns])
        return jnp.concatenate(pieces, axis=0)

    block = o0.shape[0]
    core = lax.axis_index("view") & 1
    attention = dot(turned(a0), o0[...]) + dot(turned(a1), o1[...])
    parts = []
    for ref, first, which in ((mine, 0, core), (pair, pair.shape[0] - width, 1 - core)):
        columns = pl.ds(pl.multiple_of(which * (block // 2), block // 2), block // 2)
        both = jnp.concatenate([turned(a3, columns), turned(a2, columns)], axis=1)
        parts.append([dot(both, ref[first + i : first + i + block]) for i in range(0, width, block)])
    attention = attention + jnp.concatenate([m + p for m, p in zip(*parts)], axis=1)
    y = turned(x_ref).astype(jnp.float32) + attention
    normed = (y * lax.rsqrt(jnp.mean(y * y, axis=-1, keepdims=True) + 1e-06)).astype(jnp.bfloat16)
    hidden = jax.nn.gelu(dot(normed, win_ref[...])).astype(jnp.bfloat16)
    update = dot(hidden, wback_ref[...])
    own_ref[...] = attention[: 2 * part] + update[: 2 * part]
    for j, ref in ((1, r1), (2, r2), (3, r3)):
        ref[...] = update[2 * part * j : 2 * part * (j + 1)].astype(jnp.bfloat16)


def feed(x, attended, w_outs, w_in, w_back):
    rows, width = x.shape
    piece = held((rows // 4, width), jnp.bfloat16)
    return pl.pallas_call(
        feed_kernel,
        out_shape=(held((rows // 4, width), jnp.float32), piece, piece, piece),
        in_specs=[VMEM] * 11,
        out_specs=(VMEM,) * 4,
        compiler_params=params(16),
        cost_estimate=COST,
        name="feed",
    )(x, *attended, *w_outs, w_in, w_back)


def gather_kernel(own_ref, r1, r2, r3, kept_ref, sent_ref):
    branch = lax.axis_index("branch")
    part = own_ref.shape[0] // 2
    half = part // 2
    for view in range(2):
        for side, ref in ((1 - branch, sent_ref), (branch, kept_ref)):
            rows = pl.ds(pl.multiple_of(view * part + side * half, half), half)
            total = own_ref[rows, :]
            for r in (r1, r2, r3):
                total = total + r[rows, :].astype(jnp.float32)
            ref[view * half : (view + 1) * half, :] = total.astype(ref.dtype)


def gather(own, received):
    rows, width = own.shape
    return pl.pallas_call(
        gather_kernel,
        out_shape=(
            held((rows // 2, width), jnp.float32),
            held((rows // 2, width), jnp.bfloat16),
        ),
        in_specs=[VMEM] * 4,
        out_specs=(VMEM, VMEM),
        compiler_params=params(2),
        cost_estimate=COST,
        name="gather",
    )(own, *received)


def guide_kernel(guidance_ref, kept_ref, other_ref, out_ref):
    strength = guidance_ref[0]
    weight = jnp.where(lax.axis_index("branch") == 0, strength, 1.0 - strength)
    kept = kept_ref[...]
    guided = weight * kept + (1.0 - weight) * other_ref[...].astype(jnp.float32)
    out_ref[...] = guided.astype(out_ref.dtype)


def guide(guidance, kept, other):
    return pl.pallas_call(
        guide_kernel,
        out_shape=jax.ShapeDtypeStruct(other.shape, jnp.bfloat16),
        in_specs=[SMEM, VMEM, VMEM],
        out_specs=VMEM,
        compiler_params=params(2),
        cost_estimate=COST,
        name="guide",
    )(guidance, kept, other)


def on_device(tokens, partners, counts, w_query, w_key, w_value, w_out, w_in, w_back, guidance):
    per_device, tok, width = tokens.shape[1:]
    x = tokens[0].reshape(per_device * tok, width)
    count = lax.axis_size("view")

    q, kv = project(x, w_query, w_key, w_value)
    bias = biases(count, partners.T, counts)

    near = [shifted("view", count, d)(kv) for d in (2, -2)]
    far = [shifted("view", count, d)(kv) for d in (4, -4)]
    w_1 = flipped("head", 4, 1)(w_out)
    w_01 = halves(w_out, w_1, bias)
    w_32 = flipped("head", 4, 3)(w_01)
    state = attend(((0, 0, True), (2, 0, False), (3, 0, False)), True, False, bias, q, (kv, *near), (), *(w_01,))
    pair = flipped("view", count, 1)(pick(kv, *near, *far, state[1]))
    state = attend(((5, 0, False), (6, 0, False)), False, False, bias, q, far, state, w_32)
    attended = attend(((1, 0, True), (4, 1, True)), False, True, bias, q, (pair, pair), state)
    w_pair = flipped("view", count, 1)(kept_until(w_32, attended))

    pieces = [attended] + [flipped("head", 4, j)(attended) for j in (1, 2, 3)]
    own, *outgoing = feed(x, pieces, (w_out, w_1, w_32, w_pair), w_in, w_back)
    received = [flipped("head", 4, j)(r) for j, r in zip((1, 2, 3), outgoing)]
    kept, sent = gather(own, received)
    other = flipped("branch", 2, 1)(sent)
    return guide(guidance, kept, other).reshape(per_device, -1, width)


def solution(mesh):
    placed = (
        P("branch", "view", None, None),
        P(None, "view"),
        P("view"),
        P(None, "head"),
        P(None, "head"),
        P(None, "head"),
        P("head", None),
        P(None, "head"),
        P("head", None),
        P(),
    )
    return jax.shard_map(
        on_device,
        mesh=mesh,
        in_specs=placed,
        out_specs=P("view", ("head", "branch"), None),
        check_vma=False,
    )
```

time: 78.8 us -> 66.8 us (0.85)
  waiting for transfers between devices: 17 us -> 25.2 us
  local copies, waits for them, and re-layouts: 6.98 us -> 0.02 us
  Pallas kernels: 15.6 us -> 10.3 us
  starting transfers between devices: 34.2 us -> 29.3 us
  other arithmetic: 2.99 us -> 0 us
    ppermute x7, waiting for transfers between devices: 0.06 us -> 9.57 us  [the longest x2 5.09 us: on_device(): near = [shifted('view', count, d)(kv) for d in (2, -2)]]
    pallas_call x3, Pallas kernels: 10.3 us -> 4.12 us  [attend(): pl.pallas_call(functools.partial(attend_kernel, blocks, first, last), out...]
    unnamed x28 -> x12, local copies, waits for them, and re-layouts: 5.54 us -> 0.02 us
    ppermute x7, starting transfers between devices: 14.9 us -> 11.5 us  [the longest x2 6.36 us: on_device(): far = [shifted('view', count, d)(kv) for d in (4, -4)]]
    convert_element_type x1 -> x0, other arithmetic: 1.56 us -> none  [on_device(): return guided.reshape(per_device, -1, width).astype(jnp.bfloat16)]
    ppermute x3, waiting for transfers between devices: 5.42 us -> 6.73 us  [on_device(): received = [flipped('head', 4, j)(r) for j, r in zip((1, 2, 3), outgoing)]]
    squeeze x1 -> x0, local copies, waits for them, and re-layouts: 1.27 us -> none  [on_device(): w_outs = (w_out, w_1, w_32[1], w_32[0])]
    ppermute x3, waiting for transfers between devices: 7.77 us -> 6.51 us  [on_device(): pieces = [attended] + [flipped('head', 4, j)(attended) for j in (1, 2, 3)]]
  transfers between devices with their start and end apart: 15 -> 15, of which waited for: 7 -> 10; matrix products, arithmetic and copies ran while one was open for 4% -> 0% of each run, Pallas kernels for 14% -> 9%
where the time goes in v2:
time: 66.8 us; the launch traced here: 65.7 us
  starting transfers between devices  29.3 us (44%)
  waiting for transfers between devices  25.2 us (38%)
  Pallas kernels  10.3 us (15%)
  between operations  0.78 us (1%)
    ppermute x1, starting transfers between devices, on_device(): other = flipped('branch', 2, 1)(sent)  7.27 us
    ppermute x3, waiting for transfers between devices, on_device(): received = [flipped('head', 4, j)(r) for j, r in zip((1, 2, 3), outgoing)]  6.73 us
    ppermute x3, waiting for transfers between devices, on_device(): pieces = [attended] + [flipped('head', 4, j)(attended) for j in (1, 2, 3)]  6.51 us
    ppermute x2, starting transfers between devices, on_device(): far = [shifted('view', count, d)(kv) for d in (4, -4)]  6.36 us
    ppermute x2, waiting for transfers between devices, on_device(): near = [shifted('view', count, d)(kv) for d in (2, -2)]  5.09 us
    ppermute x3, starting transfers between devices, on_device(): received = [flipped('head', 4, j)(r) for j, r in zip((1, 2, 3), outgoing)]  4.79 us
    ppermute x3, starting transfers between devices, on_device(): pieces = [attended] + [flipped('head', 4, j)(attended) for j in (1, 2, 3)]  4.18 us
    pallas_call x3, Pallas kernels, attend(): pl.pallas_call(functools.partial(attend_kernel, blocks, first, last), out...  4.12 us
  transfers between devices with their start and end apart: 15, of which 10 were waited for; matrix products, arithmetic and copies ran while one was open for 0% of the time, Pallas kernels for 9%

profile of v2, /device:TPU:8, one launch (start us, length us, event | category | flops | bytes accessed | tf_op | source)
XLA Modules:
  0.0 65.7 jit_solution(13542272896471082572)
XLA Ops:
  0.0 1.6 %collective-permute-start.4 = (bf16[256,1024]{1,0:T(8,128)(2,1)}, bf16[256,1024]{1,0:T(8,128)(2,1)S(1)}, u32[]{:S(2)}, u32[]{:S(2)}) collective-permute-start(bf16[256,1024]{1,0:T(8,128)(2,1)} %o0.1), channel_id=1, source_target_pairs={{0,2},{2,0},{4,6},{6,4},{1,3},{3,1},{5,7},{7,5},{8,10},{10,8},{12,... | collective-permute-start | bytes 1572872 | tf_op jit(solution)/shard_map/ppermute | solution.py:388
  1.6 2.5 %project.1 = (bf16[256,256]{1,0:T(8,128)(2,1)S(1)}, bf16[512,256]{1,0:T(8,128)(2,1)S(1)}) custom-call(bf16[256,1024]{1,0:T(8,128)(2,1)} %bitcast.3, bf16[1024,256]{1,0:T(8,128)(2,1)} %wk_hbm.1, bf16[1024,256]{1,0:T(8,128)(2,1)} %wv_hbm.1, bf16[1024,256]{1,0:T(8,128)(2,1)} %wq_hbm.1), custom_call_target="tpu_custom_call" | custom-call | flops 1000 | bytes 1000 | tf_op jit(solution)/shard_map/project/pallas_call | solution.py:123
  4.0 1.7 %collective-permute-start.1 = (bf16[512,256]{1,0:T(8,128)(2,1)S(1)}, bf16[512,256]{1,0:T(8,128)(2,1)S(1)}, u32[]{:S(2)}, u32[]{:S(2)}) collective-permute-start(bf16[512,256]{1,0:T(8,128)(2,1)S(1)} %get-tuple-element.18.refs_0_.own_ref), channel_id=1, source_target_pairs={{0,16},{8,24},{16,32},{24,40},{32,48},{40,56},{48,64},{56,72},{64,... | collective-permute-start | bytes 786440 | tf_op jit(solution)/shard_map/ppermute | solution.py:386
  5.7 0.5 collective-permute-start
  6.2 2.3 %collective-permute-start.3 = (bf16[512,256]{1,0:T(8,128)(2,1)S(1)}, bf16[512,256]{1,0:T(8,128)(2,1)S(1)}, u32[]{:S(2)}, u32[]{:S(2)}) collective-permute-start(bf16[512,256]{1,0:T(8,128)(2,1)S(1)} %get-tuple-element.18.refs_0_.own_ref), channel_id=1, source_target_pairs={{0,32},{8,40},{16,48},{24,56},{32,64},{40,72},{48,80},{56,88},{64,... | collective-permute-start | bytes 786440 | tf_op jit(solution)/shard_map/ppermute | solution.py:387
  8.4 4.1 %collective-permute-start.2 = (bf16[512,256]{1,0:T(8,128)(2,1)S(1)}, bf16[512,256]{1,0:T(8,128)(2,1)S(1)}, u32[]{:S(2)}, u32[]{:S(2)}) collective-permute-start(bf16[512,256]{1,0:T(8,128)(2,1)S(1)} %get-tuple-element.18.refs_0_.own_ref), channel_id=1, source_target_pairs={{0,224},{8,232},{16,240},{24,248},{32,0},{40,8},{48,16},{56,24},{6... | collective-permute-start | bytes 786440 | tf_op jit(solution)/shard_map/ppermute | solution.py:387
  12.5 0.7 %biases.1.after_ref.bias_ref = f32[32,128]{1,0:T(8,128)S(1)} custom-call(s32[2,8]{1,0:T(2,128)S(1)} %bitcast.5, s32[2]{0:T(128)S(1)} %copy-done.5), custom_call_target="tpu_custom_call" | custom-call | flops 1000 | bytes 1000 | tf_op jit(solution)/shard_map/biases/pallas_call | solution.py:85
  13.3 0.7 %collective-permute-done.4.b_ref.o1 = bf16[256,1024]{1,0:T(8,128)(2,1)S(1)} collective-permute-done((bf16[256,1024]{1,0:T(8,128)(2,1)}, bf16[256,1024]{1,0:T(8,128)(2,1)S(1)}, u32[]{:S(2)}, u32[]{:S(2)}) %collective-permute-start.4) | collective-permute-done | bytes 524320 | tf_op jit(solution)/shard_map/ppermute | solution.py:388
  14.0 2.8 %collective-permute-start.6 = (bf16[1024,256]{1,0:T(8,128)(2,1)S(1)}, bf16[1024,256]{1,0:T(8,128)(2,1)S(1)}, u32[]{:S(2)}, u32[]{:S(2)}) collective-permute-start(bf16[1024,256]{1,0:T(8,128)(2,1)S(1)} %halves.1.refs_3_), channel_id=1, source_target_pairs={{0,6},{2,4},{4,2},{6,0},{1,7},{3,5},{5,3},{7,1},{8,14},{10,12},{12... | collective-permute-start | bytes 1572872 | tf_op jit(solution)/shard_map/ppermute | solution.py:390
  16.9 5.1 %collective-permute-done.refs_1_.a_ref = bf16[512,256]{1,0:T(8,128)(2,1)S(1)} collective-permute-done((bf16[512,256]{1,0:T(8,128)(2,1)S(1)}, bf16[512,256]{1,0:T(8,128)(2,1)S(1)}, u32[]{:S(2)}, u32[]{:S(2)}) %collective-permute-start) | collective-permute-done | bytes 262176 | tf_op jit(solution)/shard_map/ppermute | solution.py:386
  22.0 1.5 %attend.3 = (f32[512,128]{1,0:T(8,128)S(1)}, f32[4,512]{1,0:T(4,128)S(1)}) custom-call(f32[32,128]{1,0:T(8,128)S(1)} %biases.1.after_ref.bias_ref, bf16[256,256]{1,0:T(8,128)(2,1)S(1)} %get-tuple-element.17.q_ref, bf16[512,256]{1,0:T(8,128)(2,1)S(1)} %get-tuple-element.18.refs_0_.own_ref, bf16[512,256]{1,0:T(8,128)(2,1)S(1)} %collective-permute-done.refs_1_.a_ref, ...), custom_call_target="tpu_custom_call" | custom-call | flops 1000 | bytes 1000 | tf_op jit(solution)/shard_map/attend/pallas_call | solution.py:206
  23.5 2.3 %collective-permute-done.3.refs_1_ = bf16[512,256]{1,0:T(8,128)(2,1)S(1)} collective-permute-done((bf16[512,256]{1,0:T(8,128)(2,1)S(1)}, bf16[512,256]{1,0:T(8,128)(2,1)S(1)}, u32[]{:S(2)}, u32[]{:S(2)}) %collective-permute-start.3) | collective-permute-done | bytes 262176 | tf_op jit(solution)/shard_map/ppermute | solution.py:387
  25.9 0.1 collective-permute-start.5
  26.0 2.1 %collective-permute-done.6.refs_4_.a_ref.mine = bf16[1024,256]{1,0:T(8,128)(2,1)S(1)} collective-permute-done((bf16[1024,256]{1,0:T(8,128)(2,1)S(1)}, bf16[1024,256]{1,0:T(8,128)(2,1)S(1)}, u32[]{:S(2)}, u32[]{:S(2)}) %collective-permute-start.6) | collective-permute-done | bytes 524320 | tf_op jit(solution)/shard_map/ppermute | solution.py:390
  28.1 1.0 %attend.4 = (f32[512,128]{1,0:T(8,128)S(1)}, f32[4,512]{1,0:T(4,128)S(1)}) custom-call(f32[32,128]{1,0:T(8,128)S(1)} %biases.1.after_ref.bias_ref, bf16[256,256]{1,0:T(8,128)(2,1)S(1)} %get-tuple-element.17.q_ref, bf16[512,256]{1,0:T(8,128)(2,1)S(1)} %collective-permute-done.2.refs_0_, bf16[512,256]{1,0:T(8,128)(2,1)S(1)} %collective-permute-done.3.refs_1_, ...), custom_call_target="tpu_custom_call" | custom-call | flops 1000 | bytes 1000 | tf_op jit(solution)/shard_map/attend/pallas_call | solution.py:206
  29.1 1.6 %attend.5.after_ref.a0 = bf16[256,256]{1,0:T(8,128)(2,1)S(1)} custom-call(f32[32,128]{1,0:T(8,128)S(1)} %biases.1.after_ref.bias_ref, bf16[256,256]{1,0:T(8,128)(2,1)S(1)} %get-tuple-element.17.q_ref, bf16[1024,256]{1,0:T(8,128)(2,1)S(1)} %collective-permute-done.5.refs_0_.refs_1_, bf16[1024,256]{1,0:T(8,128)(2,1)S(1)} %collective-permute-done.5.refs_0_.refs_1_, ...), custom_call_target="tpu_custom_call" | custom-call | flops 1000 | bytes 1000 | tf_op jit(solution)/shard_map/attend/pallas_call | solution.py:206
  30.8 0.1 collective-permute-start.10
  30.9 2.8 %collective-permute-start.9 = (bf16[256,256]{1,0:T(8,128)(2,1)S(1)}, bf16[256,256]{1,0:T(8,128)(2,1)S(1)}, u32[]{:S(2)}, u32[]{:S(2)}) collective-permute-start(bf16[256,256]{1,0:T(8,128)(2,1)S(1)} %attend.5.after_ref.a0), channel_id=1, source_target_pairs={{0,6},{2,4},{4,2},{6,0},{1,7},{3,5},{5,3},{7,1},{8,14},{10,12},{12... | collective-permute-start | bytes 393224 | tf_op jit(solution)/shard_map/ppermute | solution.py:397
  33.7 1.3 %collective-permute-start.7 = (bf16[256,256]{1,0:T(8,128)(2,1)S(1)}, bf16[256,256]{1,0:T(8,128)(2,1)S(1)}, u32[]{:S(2)}, u32[]{:S(2)}) collective-permute-start(bf16[256,256]{1,0:T(8,128)(2,1)S(1)} %attend.5.after_ref.a0), channel_id=1, source_target_pairs={{0,2},{2,0},{4,6},{6,4},{1,3},{3,1},{5,7},{7,5},{8,10},{10,8},{12,... | collective-permute-start | bytes 393224 | tf_op jit(solution)/shard_map/ppermute | solution.py:397
  35.1 4.8 %collective-permute-done.9.a3 = bf16[256,256]{1,0:T(8,128)(2,1)S(1)} collective-permute-done((bf16[256,256]{1,0:T(8,128)(2,1)S(1)}, bf16[256,256]{1,0:T(8,128)(2,1)S(1)}, u32[]{:S(2)}, u32[]{:S(2)}) %collective-permute-start.9) | collective-permute-done | bytes 131104 | tf_op jit(solution)/shard_map/ppermute | solution.py:397
  39.9 1.7 %collective-permute-done.8.a2 = bf16[256,256]{1,0:T(8,128)(2,1)S(1)} collective-permute-done((bf16[256,256]{1,0:T(8,128)(2,1)S(1)}, bf16[256,256]{1,0:T(8,128)(2,1)S(1)}, u32[]{:S(2)}, u32[]{:S(2)}) %collective-permute-start.8) | collective-permute-done | bytes 131104 | tf_op jit(solution)/shard_map/ppermute | solution.py:397
  41.6 2.2 %feed.1 = (f32[64,1024]{1,0:T(8,128)S(1)}, bf16[64,1024]{1,0:T(8,128)(2,1)S(1)}, bf16[64,1024]{1,0:T(8,128)(2,1)S(1)}, bf16[64,1024]{1,0:T(8,128)(2,1)S(1)}) custom-call(bf16[256,1024]{1,0:T(8,128)(2,1)S(1)} %bitcast.4, bf16[256,256]{1,0:T(8,128)(2,1)S(1)} %attend.5.after_ref.a0, bf16[256,256]{1,0:T(8,128)(2,1)S(1)} %collective-permute-done.7.a1, ...), custom_call_target="tpu_custom_call" | custom-call | flops 1000 | bytes 1000 | tf_op jit(solution)/shard_map/feed/pallas_call | solution.py:318
  43.8 0.9 %collective-permute-start.11 = (bf16[64,1024]{1,0:T(8,128)(2,1)S(1)}, bf16[64,1024]{1,0:T(8,128)(2,1)S(1)}, u32[]{:S(2)}, u32[]{:S(2)}) collective-permute-start(bf16[64,1024]{1,0:T(8,128)(2,1)S(1)} %get-tuple-element.24), channel_id=1, source_target_pairs={{0,2},{2,0},{4,6},{6,4},{1,3},{3,1},{5,7},{7,5},{8,10},{10,8},{12,... | collective-permute-start | bytes 393224 | tf_op jit(solution)/shard_map/ppermute | solution.py:399
  44.7 3.2 %collective-permute-start.12 = (bf16[64,1024]{1,0:T(8,128)(2,1)S(1)}, bf16[64,1024]{1,0:T(8,128)(2,1)S(1)}, u32[]{:S(2)}, u32[]{:S(2)}) collective-permute-start(bf16[64,1024]{1,0:T(8,128)(2,1)S(1)} %get-tuple-element.25), channel_id=1, source_target_pairs={{0,4},{2,6},{4,0},{6,2},{1,5},{3,7},{5,1},{7,3},{8,12},{10,14},{12... | collective-permute-start | bytes 393224 | tf_op jit(solution)/shard_map/ppermute | solution.py:399
  47.9 0.7 %collective-permute-start.13 = (bf16[64,1024]{1,0:T(8,128)(2,1)S(1)}, bf16[64,1024]{1,0:T(8,128)(2,1)S(1)}, u32[]{:S(2)}, u32[]{:S(2)}) collective-permute-start(bf16[64,1024]{1,0:T(8,128)(2,1)S(1)} %get-tuple-element.26), channel_id=1, source_target_pairs={{0,6},{2,4},{4,2},{6,0},{1,7},{3,5},{5,3},{7,1},{8,14},{10,12},{12... | collective-permute-start | bytes 393224 | tf_op jit(solution)/shard_map/ppermute | solution.py:399
  48.6 1.5 %collective-permute-done.11.r1 = bf16[64,1024]{1,0:T(8,128)(2,1)S(1)} collective-permute-done((bf16[64,1024]{1,0:T(8,128)(2,1)S(1)}, bf16[64,1024]{1,0:T(8,128)(2,1)S(1)}, u32[]{:S(2)}, u32[]{:S(2)}) %collective-permute-start.11) | collective-permute-done | bytes 131104 | tf_op jit(solution)/shard_map/ppermute | solution.py:399
  50.1 3.4 %collective-permute-done.12.r2 = bf16[64,1024]{1,0:T(8,128)(2,1)S(1)} collective-permute-done((bf16[64,1024]{1,0:T(8,128)(2,1)S(1)}, bf16[64,1024]{1,0:T(8,128)(2,1)S(1)}, u32[]{:S(2)}, u32[]{:S(2)}) %collective-permute-start.12) | collective-permute-done | bytes 131104 | tf_op jit(solution)/shard_map/ppermute | solution.py:399
  53.5 1.8 %collective-permute-done.13.r3 = bf16[64,1024]{1,0:T(8,128)(2,1)S(1)} collective-permute-done((bf16[64,1024]{1,0:T(8,128)(2,1)S(1)}, bf16[64,1024]{1,0:T(8,128)(2,1)S(1)}, u32[]{:S(2)}, u32[]{:S(2)}) %collective-permute-start.13) | collective-permute-done | bytes 131104 | tf_op jit(solution)/shard_map/ppermute | solution.py:399
  55.3 0.1 gather.1
  55.4 7.3 %collective-permute-start.14 = (bf16[32,1024]{1,0:T(8,128)(2,1)S(1)}, bf16[32,1024]{1,0:T(8,128)(2,1)S(1)}, u32[]{:S(2)}, u32[]{:S(2)}) collective-permute-start(bf16[32,1024]{1,0:T(8,128)(2,1)S(1)} %get-tuple-element.28), channel_id=1, source_target_pairs={{0,1},{1,0},{2,3},{3,2},{4,5},{5,4},{6,7},{7,6},{8,9},{9,8},{10,11... | collective-permute-start | bytes 196616 | tf_op jit(solution)/shard_map/ppermute | solution.py:401
  63.3 1.7 %collective-permute-done.14.other_ref = bf16[32,1024]{1,0:T(8,128)(2,1)S(1)} collective-permute-done((bf16[32,1024]{1,0:T(8,128)(2,1)S(1)}, bf16[32,1024]{1,0:T(8,128)(2,1)S(1)}, u32[]{:S(2)}, u32[]{:S(2)}) %collective-permute-start.14) | collective-permute-done | bytes 65568 | tf_op jit(solution)/shard_map/ppermute | solution.py:401
  65.0 0.7 guide.1
  (21 shorter events, 0.1 us)
Async XLA Ops:
  0.0 14.0 %copy-start = (bf16[256,1024]{1,0:T(8,128)(2,1)S(1)}, bf16[256,1024]{1,0:T(8,128)(2,1)}, u32[]{:S(2)}) copy-start(bf16[256,1024]{1,0:T(8,128)(2,1)} %o0.1) | copy-start | bytes 1572868
  0.0 12.5 %copy-start.5 = (s32[2]{0:T(128)S(1)}, s32[2]{0:T(128)}, u32[]{:S(2)}) copy-start(s32[2]{0:T(128)} %counts_ref.1) | copy-start | bytes 28
  0.0 12.5 %copy-start.4 = (s32[8,2]{0,1:T(2,128)S(1)}, s32[8,2]{0,1:T(2,128)}, u32[]{:S(2)}) copy-start(s32[8,2]{0,1:T(2,128)} %param.11) | copy-start | bytes 196
  0.0 14.0 %collective-permute-start.4 = (bf16[256,1024]{1,0:T(8,128)(2,1)}, bf16[256,1024]{1,0:T(8,128)(2,1)S(1)}, u32[]{:S(2)}, u32[]{:S(2)}) collective-permute-start(bf16[256,1024]{1,0:T(8,128)(2,1)} %o0.1), channel_id=1, source_target_pairs={{0,2},{2,0},{4,6},{6,4},{1,3},{3,1},{5,7},{7,5},{8,10},{10,8},{12,... | collective-permute-start | bytes 1572872 | tf_op jit(solution)/shard_map/ppermute | solution.py:388
  4.0 12.8 %collective-permute-start.1 = (bf16[512,256]{1,0:T(8,128)(2,1)S(1)}, bf16[512,256]{1,0:T(8,128)(2,1)S(1)}, u32[]{:S(2)}, u32[]{:S(2)}) collective-permute-start(bf16[512,256]{1,0:T(8,128)(2,1)S(1)} %get-tuple-element.18.refs_0_.own_ref), channel_id=1, source_target_pairs={{0,16},{8,24},{16,32},{24,40},{32,48},{40,56},{48,64},{56,72},{64,... | collective-permute-start | bytes 786440 | tf_op jit(solution)/shard_map/ppermute | solution.py:386
  5.7 16.3 %collective-permute-start = (bf16[512,256]{1,0:T(8,128)(2,1)S(1)}, bf16[512,256]{1,0:T(8,128)(2,1)S(1)}, u32[]{:S(2)}, u32[]{:S(2)}) collective-permute-start(bf16[512,256]{1,0:T(8,128)(2,1)S(1)} %get-tuple-element.18.refs_0_.own_ref), channel_id=1, source_target_pairs={{0,240},{8,248},{16,0},{24,8},{32,16},{40,24},{48,32},{56,40},{64,... | collective-permute-start | bytes 786440 | tf_op jit(solution)/shard_map/ppermute | solution.py:386
  6.2 19.7 %collective-permute-start.3 = (bf16[512,256]{1,0:T(8,128)(2,1)S(1)}, bf16[512,256]{1,0:T(8,128)(2,1)S(1)}, u32[]{:S(2)}, u32[]{:S(2)}) collective-permute-start(bf16[512,256]{1,0:T(8,128)(2,1)S(1)} %get-tuple-element.18.refs_0_.own_ref), channel_id=1, source_target_pairs={{0,32},{8,40},{16,48},{24,56},{32,64},{40,72},{48,80},{56,88},{64,... | collective-permute-start | bytes 786440 | tf_op jit(solution)/shard_map/ppermute | solution.py:387
  8.4 17.4 %collective-permute-start.2 = (bf16[512,256]{1,0:T(8,128)(2,1)S(1)}, bf16[512,256]{1,0:T(8,128)(2,1)S(1)}, u32[]{:S(2)}, u32[]{:S(2)}) collective-permute-start(bf16[512,256]{1,0:T(8,128)(2,1)S(1)} %get-tuple-element.18.refs_0_.own_ref), channel_id=1, source_target_pairs={{0,224},{8,232},{16,240},{24,248},{32,0},{40,8},{48,16},{56,24},{6... | collective-permute-start | bytes 786440 | tf_op jit(solution)/shard_map/ppermute | solution.py:387
  14.0 14.1 %collective-permute-start.6 = (bf16[1024,256]{1,0:T(8,128)(2,1)S(1)}, bf16[1024,256]{1,0:T(8,128)(2,1)S(1)}, u32[]{:S(2)}, u32[]{:S(2)}) collective-permute-start(bf16[1024,256]{1,0:T(8,128)(2,1)S(1)} %halves.1.refs_3_), channel_id=1, source_target_pairs={{0,6},{2,4},{4,2},{6,0},{1,7},{3,5},{5,3},{7,1},{8,14},{10,12},{12... | collective-permute-start | bytes 1572872 | tf_op jit(solution)/shard_map/ppermute | solution.py:390
  25.8 15.8 %copy-start.3 = (bf16[1024,1024]{1,0:T(8,128)(2,1)S(1)}, bf16[1024,1024]{1,0:T(8,128)(2,1)}, u32[]{:S(2)}) copy-start(bf16[1024,1024]{1,0:T(8,128)(2,1)} %wback_ref.1) | copy-start | bytes 6291460
  25.9 3.3 %collective-permute-start.5 = (bf16[1024,256]{1,0:T(8,128)(2,1)S(1)}, bf16[1024,256]{1,0:T(8,128)(2,1)S(1)}, u32[]{:S(2)}, u32[]{:S(2)}) collective-permute-start(bf16[1024,256]{1,0:T(8,128)(2,1)S(1)} %pick.1), channel_id=1, source_target_pairs={{0,8},{8,0},{16,24},{24,16},{32,40},{40,32},{48,56},{56,48},{64,72... | collective-permute-start | bytes 1572872 | tf_op jit(solution)/shard_map/ppermute | solution.py:392
  28.1 13.5 %copy-start.1 = (bf16[1,2,128,1024]{3,2,1,0:T(8,128)(2,1)S(1)}, bf16[1,2,128,1024]{3,2,1,0:T(8,128)(2,1)}, u32[]{:S(2)}) copy-start(bf16[1,2,128,1024]{3,2,1,0:T(8,128)(2,1)} %param.10) | copy-start | bytes 1572868
  28.1 13.5 %copy-start.2 = (bf16[1024,1024]{1,0:T(8,128)(2,1)S(1)}, bf16[1024,1024]{1,0:T(8,128)(2,1)}, u32[]{:S(2)}) copy-start(bf16[1024,1024]{1,0:T(8,128)(2,1)} %win_ref.1) | copy-start | bytes 6291460
  30.8 10.8 %collective-permute-start.10 = (bf16[1024,256]{1,0:T(8,128)(2,1)S(1)}, bf16[1024,256]{1,0:T(8,128)(2,1)S(1)}, u32[]{:S(2)}, u32[]{:S(2)}) collective-permute-start(bf16[1024,256]{1,0:T(8,128)(2,1)S(1)} %kept_until.1), channel_id=1, source_target_pairs={{0,8},{8,0},{16,24},{24,16},{32,40},{40,32},{48,56},{56,48},{64,72... | collective-permute-start | bytes 1572872 | tf_op jit(solution)/shard_map/ppermute | solution.py:395
  30.9 9.0 %collective-permute-start.9 = (bf16[256,256]{1,0:T(8,128)(2,1)S(1)}, bf16[256,256]{1,0:T(8,128)(2,1)S(1)}, u32[]{:S(2)}, u32[]{:S(2)}) collective-permute-start(bf16[256,256]{1,0:T(8,128)(2,1)S(1)} %attend.5.after_ref.a0), channel_id=1, source_target_pairs={{0,6},{2,4},{4,2},{6,0},{1,7},{3,5},{5,3},{7,1},{8,14},{10,12},{12... | collective-permute-start | bytes 393224 | tf_op jit(solution)/shard_map/ppermute | solution.py:397
  33.7 7.8 %collective-permute-start.8 = (bf16[256,256]{1,0:T(8,128)(2,1)S(1)}, bf16[256,256]{1,0:T(8,128)(2,1)S(1)}, u32[]{:S(2)}, u32[]{:S(2)}) collective-permute-start(bf16[256,256]{1,0:T(8,128)(2,1)S(1)} %attend.5.after_ref.a0), channel_id=1, source_target_pairs={{0,4},{2,6},{4,0},{6,2},{1,5},{3,7},{5,1},{7,3},{8,12},{10,14},{12... | collective-permute-start | bytes 393224 | tf_op jit(solution)/shard_map/ppermute | solution.py:397
  33.7 7.8 %collective-permute-start.7 = (bf16[256,256]{1,0:T(8,128)(2,1)S(1)}, bf16[256,256]{1,0:T(8,128)(2,1)S(1)}, u32[]{:S(2)}, u32[]{:S(2)}) collective-permute-start(bf16[256,256]{1,0:T(8,128)(2,1)S(1)} %attend.5.after_ref.a0), channel_id=1, source_target_pairs={{0,2},{2,0},{4,6},{6,4},{1,3},{3,1},{5,7},{7,5},{8,10},{10,8},{12,... | collective-permute-start | bytes 393224 | tf_op jit(solution)/shard_map/ppermute | solution.py:397
  43.8 6.3 %collective-permute-start.11 = (bf16[64,1024]{1,0:T(8,128)(2,1)S(1)}, bf16[64,1024]{1,0:T(8,128)(2,1)S(1)}, u32[]{:S(2)}, u32[]{:S(2)}) collective-permute-start(bf16[64,1024]{1,0:T(8,128)(2,1)S(1)} %get-tuple-element.24), channel_id=1, source_target_pairs={{0,2},{2,0},{4,6},{6,4},{1,3},{3,1},{5,7},{7,5},{8,10},{10,8},{12,... | collective-permute-start | bytes 393224 | tf_op jit(solution)/shard_map/ppermute | solution.py:399
  44.7 8.8 %collective-permute-start.12 = (bf16[64,1024]{1,0:T(8,128)(2,1)S(1)}, bf16[64,1024]{1,0:T(8,128)(2,1)S(1)}, u32[]{:S(2)}, u32[]{:S(2)}) collective-permute-start(bf16[64,1024]{1,0:T(8,128)(2,1)S(1)} %get-tuple-element.25), channel_id=1, source_target_pairs={{0,4},{2,6},{4,0},{6,2},{1,5},{3,7},{5,1},{7,3},{8,12},{10,14},{12... | collective-permute-start | bytes 393224 | tf_op jit(solution)/shard_map/ppermute | solution.py:399
  47.9 7.4 %collective-permute-start.13 = (bf16[64,1024]{1,0:T(8,128)(2,1)S(1)}, bf16[64,1024]{1,0:T(8,128)(2,1)S(1)}, u32[]{:S(2)}, u32[]{:S(2)}) collective-permute-start(bf16[64,1024]{1,0:T(8,128)(2,1)S(1)} %get-tuple-element.26), channel_id=1, source_target_pairs={{0,6},{2,4},{4,2},{6,0},{1,7},{3,5},{5,3},{7,1},{8,14},{10,12},{12... | collective-permute-start | bytes 393224 | tf_op jit(solution)/shard_map/ppermute | solution.py:399
  55.4 9.6 %collective-permute-start.14 = (bf16[32,1024]{1,0:T(8,128)(2,1)S(1)}, bf16[32,1024]{1,0:T(8,128)(2,1)S(1)}, u32[]{:S(2)}, u32[]{:S(2)}) collective-permute-start(bf16[32,1024]{1,0:T(8,128)(2,1)S(1)} %get-tuple-element.28), channel_id=1, source_target_pairs={{0,1},{1,0},{2,3},{3,2},{4,5},{5,4},{6,7},{7,6},{8,9},{9,8},{10,11... | collective-permute-start | bytes 196616 | tf_op jit(solution)/shard_map/ppermute | solution.py:401

commit v3 on v2

--- a/solution.py
+++ b/solution.py
@@ -61,7 +61,7 @@
     return [2 * lax.rem(s + count, count) for s in sources]
 
 
-def bias_kernel(count, partners_ref, counts_ref, bias_ref):
+def bias_kernel(count, partners_ref, counts_ref, after_ref, bias_ref):
     bias_ref[...] = jnp.zeros_like(bias_ref)
     firsts = key_views(count)
     for qv in range(2):
@@ -81,60 +81,67 @@
         bias_ref[row : row + 1] = jnp.zeros((1, bias_ref.shape[1]), jnp.float32)
 
 
-def biases(count, partners, counts):
+def biases(count, partners, counts, after):
     return pl.pallas_call(
         functools.partial(bias_kernel, count),
         out_shape=held((2 * BIASES, 2 * HD), jnp.float32),
-        in_specs=[SMEM, SMEM],
+        in_specs=[SMEM, SMEM, ANY],
         out_specs=VMEM,
         compiler_params=params(2),
         cost_estimate=COST,
         name="biases",
-    )(partners, counts)
-
-
-def project_kernel(x_hbm, wk_hbm, wv_hbm, wq_hbm, q_ref, kv_ref, x, wk, wv, wq, sems):
-    loads = [
-        chunked(source, target, sems.at[i], sems.shape[1])
-        for i, (source, target) in enumerate(((x_hbm, x), (wk_hbm, wk), (wv_hbm, wv), (wq_hbm, wq)))
-    ]
-    for copies in loads:
-        for copy in copies:
-            copy.start()
-
-    def arrived(i):
-        for copy in loads[i]:
-            copy.wait()
-
-    rows = x.shape[0]
-    arrived(0)
-    arrived(1)
-    kv_ref[:rows] = dot(x[...], wk[...]).astype(jnp.bfloat16)
-    arrived(2)
-    kv_ref[rows:] = dot(x[...], wv[...]).T.astype(jnp.bfloat16)
-    arrived(3)
-    q_ref[...] = (dot(x[...], wq[...]) * (HD ** (-0.5) * LOG2E)).astype(jnp.bfloat16)
-
-
-def project(x, w_query, w_key, w_value):
+    )(partners, counts, after)
+
+
+def project_kernel(x_hbm, wk_hbm, wv_hbm, wo_hbm, x_ref, kv_ref, half_ref, wk, wv, sems):
+    half = half_ref.shape[0]
+    mine = pl.ds(pl.multiple_of((lax.axis_index("view") & 1) * half, half), half)
+    pairs = ((x_hbm, x_ref), (wk_hbm, wk), (wv_hbm, wv), (wo_hbm.at[mine], half_ref))
+    loads = [pltpu.make_async_copy(source, target, sems.at[i]) for i, (source, target) in enumerate(pairs)]
+    for copy in loads:
+        copy.start()
+    rows = x_ref.shape[0]
+    loads[0].wait()
+    loads[1].wait()
+    kv_ref[:rows] = dot(x_ref[...], wk[...]).astype(jnp.bfloat16)
+    loads[2].wait()
+    kv_ref[rows:] = dot(x_ref[...], wv[...]).T.astype(jnp.bfloat16)
+    loads[3].wait()
+
+
+def project(x, w_key, w_value, w_out):
     rows, width = x.shape
-    columns = w_query.shape[1]
-    chunks = 1
+    columns = w_key.shape[1]
     return pl.pallas_call(
         project_kernel,
         out_shape=(
-            held((rows, columns), jnp.bfloat16),
+            held(x.shape, x.dtype),
             held((rows + columns, rows), jnp.bfloat16),
+            held((w_out.shape[0] // 2, w_out.shape[1]), w_out.dtype),
         ),
         in_specs=[HBM] * 4,
-        out_specs=(VMEM, VMEM),
-        scratch_shapes=[pltpu.VMEM(x.shape, jnp.bfloat16)]
-        + [pltpu.VMEM((width, columns), jnp.bfloat16)] * 3
-        + [pltpu.SemaphoreType.DMA((4, chunks))],
+        out_specs=(VMEM,) * 3,
+        scratch_shapes=[pltpu.VMEM((width, columns), jnp.bfloat16)] * 2 + [pltpu.SemaphoreType.DMA((4,))],
         compiler_params=params(8),
         cost_estimate=COST,
         name="project",
-    )(*outside(x, w_key, w_value, w_query))
+    )(*outside(x, w_key, w_value, w_out))
+
+
+def ask_kernel(x_ref, wq_ref, after_ref, q_ref):
+    q_ref[...] = (dot(x_ref[...], wq_ref[...]) * (HD ** (-0.5) * LOG2E)).astype(jnp.bfloat16)
+
+
+def ask(x, w_query, after):
+    return pl.pallas_call(
+        ask_kernel,
+        out_shape=held((x.shape[0], w_query.shape[1]), jnp.bfloat16),
+        in_specs=[VMEM, VMEM, ANY],
+        out_specs=VMEM,
+        compiler_params=params(4),
+        cost_estimate=COST,
+        name="ask",
+    )(x, w_query, after)
 
 
 def attend_kernel(blocks, first, last, bias_ref, q_ref, *refs):
@@ -214,54 +221,52 @@
     )(bias, q, *kvs, *state, *after)
 
 
-def pick_kernel(own_ref, a_ref, b_ref, *refs):
-    rows = own_ref.shape[0]
+def pick_kernel(a_ref, b_ref, *refs):
     out_ref = refs[-1]
-    out_ref[:rows] = own_ref[...]
     first = lax.axis_index("view") & 1 == 0
 
     @pl.when(first)
     def _():
-        out_ref[rows:] = a_ref[...]
+        out_ref[...] = a_ref[...]
 
     @pl.when(jnp.logical_not(first))
     def _():
-        out_ref[rows:] = b_ref[...]
-
-
-def pick(own, a, b, *after):
+        out_ref[...] = b_ref[...]
+
+
+def pick(a, b, *after):
     return pl.pallas_call(
         pick_kernel,
-        out_shape=held((2 * own.shape[0], own.shape[1]), a.dtype),
-        in_specs=[VMEM] * 3 + [ANY] * len(after),
+        out_shape=held(a.shape, a.dtype),
+        in_specs=[VMEM] * 2 + [ANY] * len(after),
         out_specs=VMEM,
         compiler_params=params(2),
         cost_estimate=COST,
         name="pick",
-    )(own, a, b, *after)
-
-
-def halves_kernel(a_ref, b_ref, after_ref, out_ref):
-    half = a_ref.shape[0] // 2
+    )(a, b, *after)
+
+
+def halves_kernel(a_ref, b_ref, out_ref):
+    half = a_ref.shape[0]
     block = out_ref.shape[1]
     rows = pl.ds(pl.multiple_of((lax.axis_index("view") & 1) * half, half), half)
     for j in range(a_ref.shape[1] // block):
         columns = slice(j * block, (j + 1) * block)
-        out_ref[2 * j * half : (2 * j + 1) * half] = a_ref[rows, columns]
+        out_ref[2 * j * half : (2 * j + 1) * half] = a_ref[:, columns]
         out_ref[(2 * j + 1) * half : (2 * j + 2) * half] = b_ref[rows, columns]
 
 
-def halves(a, b, after):
-    rows, columns = a.shape
+def halves(a, b):
+    rows, columns = b.shape
     return pl.pallas_call(
         halves_kernel,
         out_shape=held((columns, rows), a.dtype),
-        in_specs=[VMEM, VMEM, ANY],
+        in_specs=[VMEM, VMEM],
         out_specs=VMEM,
         compiler_params=params(2),
         cost_estimate=COST,
         name="halves",
-    )(a, b, after)
+    )(a, b)
 
 
 def kept_until_kernel(a_ref, after_ref, out_ref):
@@ -380,18 +385,20 @@
     x = tokens[0].reshape(per_device * tok, width)
     count = lax.axis_size("view")
 
-    q, kv = project(x, w_query, w_key, w_value)
-    bias = biases(count, partners.T, counts)
+    x, kv, w_half = project(x, w_key, w_value, w_out)
 
     near = [shifted("view", count, d)(kv) for d in (2, -2)]
     far = [shifted("view", count, d)(kv) for d in (4, -4)]
     w_1 = flipped("head", 4, 1)(w_out)
-    w_01 = halves(w_out, w_1, bias)
+    w_01 = halves(w_half, w_1)
+    q = ask(x, w_query, w_01)
+    bias = biases(count, partners.T, counts, w_01)
     w_32 = flipped("head", 4, 3)(w_01)
     state = attend(((0, 0, True), (2, 0, False), (3, 0, False)), True, False, bias, q, (kv, *near), (), *(w_01,))
-    pair = flipped("view", count, 1)(pick(kv, *near, *far, state[1]))
-    state = attend(((5, 0, False), (6, 0, False)), False, False, bias, q, far, state, w_32)
-    attended = attend(((1, 0, True), (4, 1, True)), False, True, bias, q, (pair, pair), state)
+    other_core = flipped("view", count, 1)
+    other, cross = other_core(kv), other_core(pick(*near, *far, state[1]))
+    state = attend(((1, 0, True), (5, 0, False), (6, 0, False)), False, False, bias, q, (other, *far), state)
+    attended = attend(((4, 0, True),), False, True, bias, q, (cross,), state, w_32)
     w_pair = flipped("view", count, 1)(kept_until(w_32, attended))
 
     pieces = [attended] + [flipped("head", 4, j)(attended) for j in (1, 2, 3)]

time: 66.8 us -> 64.2 us (0.961); the launches traced: 65.7 us -> 64.1 us
  waiting for transfers between devices: 25.2 us -> 23.5 us
    ppermute x2, waiting for transfers between devices: 5.09 us -> 3.61 us  [on_device(): near = [shifted('view', count, d)(kv) for d in (2, -2)]]
    ppermute x1, waiting for transfers between devices: 2.14 us -> 0.88 us  [on_device(): w_32 = flipped('head', 4, 3)(w_01)]
    ppermute x1, waiting for transfers between devices: 0.71 us -> 1.77 us  [on_device(): w_1 = flipped('head', 4, 1)(w_out)]
    pallas_call x2 -> x3, Pallas kernels: 2.49 us -> 2.47 us  [the longest x1 2.14 us: project(): pl.pallas_call(project_kernel, out_shape=(held(x.shape, x.dtype), held((r...]
  transfers between devices with their start and end apart: 15 -> 16, of which waited for: 10 -> 10; matrix products, arithmetic and copies ran while one was open for 0% -> 0% of each run, Pallas kernels for 9% -> 10%
where the time goes in v3:
time: 64.2 us; the launch traced here: 64.1 us
  starting transfers between devices  29.4 us (46%)
  waiting for transfers between devices  23.5 us (37%)
  Pallas kernels  10.3 us (16%)
  between operations  0.83 us (1%)
    ppermute x1, starting transfers between devices, on_device(): other = flipped('branch', 2, 1)(sent)  7.27 us
    ppermute x3, waiting for transfers between devices, on_device(): received = [flipped('head', 4, j)(r) for j, r in zip((1, 2, 3), outgoing)]  6.72 us
    ppermute x3, waiting for transfers between devices, on_device(): pieces = [attended] + [flipped('head', 4, j)(attended) for j in (1, 2, 3)]  6.51 us
    ppermute x2, starting transfers between devices, on_device(): far = [shifted('view', count, d)(kv) for d in (4, -4)]  6.36 us
    ppermute x3, starting transfers between devices, on_device(): received = [flipped('head', 4, j)(r) for j, r in zip((1, 2, 3), outgoing)]  4.79 us
    ppermute x3, starting transfers between devices, on_device(): pieces = [attended] + [flipped('head', 4, j)(attended) for j in (1, 2, 3)]  4.18 us
    pallas_call x3, Pallas kernels, attend(): pl.pallas_call(functools.partial(attend_kernel, blocks, first, last), out...  4.11 us
    ppermute x2, waiting for transfers between devices, on_device(): near = [shifted('view', count, d)(kv) for d in (2, -2)]  3.61 us
  transfers between devices with their start and end apart: 16, of which 10 were waited for; matrix products, arithmetic and copies ran while one was open for 0% of the time, Pallas kernels for 10%

profile of v3, /device:TPU:8, one launch (start us, length us, event | category | flops | bytes accessed | tf_op | source)
XLA Modules:
  0.0 64.1 jit_solution(17308828291928204002)
XLA Ops:
  0.0 1.6 %collective-permute-start = (bf16[256,1024]{1,0:T(8,128)(2,1)}, bf16[256,1024]{1,0:T(8,128)(2,1)S(1)}, u32[]{:S(2)}, u32[]{:S(2)}) collective-permute-start(bf16[256,1024]{1,0:T(8,128)(2,1)} %o0.1), channel_id=1, source_target_pairs={{0,2},{2,0},{4,6},{6,4},{1,3},{3,1},{5,7},{7,5},{8,10},{10,8},{12,... | collective-permute-start | bytes 1572872 | tf_op jit(solution)/shard_map/ppermute | solution.py:392
  1.6 2.1 %project.1 = (bf16[256,1024]{1,0:T(8,128)(2,1)S(1)}, bf16[512,256]{1,0:T(8,128)(2,1)S(1)}, bf16[128,1024]{1,0:T(8,128)(2,1)S(1)}) custom-call(bf16[256,1024]{1,0:T(8,128)(2,1)} %bitcast.4, bf16[1024,256]{1,0:T(8,128)(2,1)} %wk_hbm.1, bf16[1024,256]{1,0:T(8,128)(2,1)} %wv_hbm.1, bf16[256,1024]{1,0:T(8,128)(2,1)} %o0.1), custom_call_target="tpu_custom_call" | custom-call | flops 1000 | bytes 1000 | tf_op jit(solution)/shard_map/project/pallas_call | solution.py:115
  3.7 1.7 %collective-permute-start.2 = (bf16[512,256]{1,0:T(8,128)(2,1)S(1)}, bf16[512,256]{1,0:T(8,128)(2,1)S(1)}, u32[]{:S(2)}, u32[]{:S(2)}) collective-permute-start(bf16[512,256]{1,0:T(8,128)(2,1)S(1)} %get-tuple-element.20.refs_0_), channel_id=1, source_target_pairs={{0,16},{8,24},{16,32},{24,40},{32,48},{40,56},{48,64},{56,72},{64,... | collective-permute-start | bytes 786440 | tf_op jit(solution)/shard_map/ppermute | solution.py:390
  5.4 0.5 collective-permute-start.1
  5.8 2.3 %collective-permute-start.4 = (bf16[512,256]{1,0:T(8,128)(2,1)S(1)}, bf16[512,256]{1,0:T(8,128)(2,1)S(1)}, u32[]{:S(2)}, u32[]{:S(2)}) collective-permute-start(bf16[512,256]{1,0:T(8,128)(2,1)S(1)} %get-tuple-element.20.refs_0_), channel_id=1, source_target_pairs={{0,32},{8,40},{16,48},{24,56},{32,64},{40,72},{48,80},{56,88},{64,... | collective-permute-start | bytes 786440 | tf_op jit(solution)/shard_map/ppermute | solution.py:391
  8.1 4.1 %collective-permute-start.3 = (bf16[512,256]{1,0:T(8,128)(2,1)S(1)}, bf16[512,256]{1,0:T(8,128)(2,1)S(1)}, u32[]{:S(2)}, u32[]{:S(2)}) collective-permute-start(bf16[512,256]{1,0:T(8,128)(2,1)S(1)} %get-tuple-element.20.refs_0_), channel_id=1, source_target_pairs={{0,224},{8,232},{16,240},{24,248},{32,0},{40,8},{48,16},{56,24},{6... | collective-permute-start | bytes 786440 | tf_op jit(solution)/shard_map/ppermute | solution.py:391
  12.2 1.8 %collective-permute-done.b_ref.o1 = bf16[256,1024]{1,0:T(8,128)(2,1)S(1)} collective-permute-done((bf16[256,1024]{1,0:T(8,128)(2,1)}, bf16[256,1024]{1,0:T(8,128)(2,1)S(1)}, u32[]{:S(2)}, u32[]{:S(2)}) %collective-permute-start) | collective-permute-done | bytes 524320 | tf_op jit(solution)/shard_map/ppermute | solution.py:392
  14.0 2.8 %collective-permute-start.7 = (bf16[1024,256]{1,0:T(8,128)(2,1)S(1)}, bf16[1024,256]{1,0:T(8,128)(2,1)S(1)}, u32[]{:S(2)}, u32[]{:S(2)}) collective-permute-start(bf16[1024,256]{1,0:T(8,128)(2,1)S(1)} %halves.1.after_ref.refs_3_), channel_id=1, source_target_pairs={{0,6},{2,4},{4,2},{6,0},{1,7},{3,5},{5,3},{7,1},{8,14},{10,12},{12... | collective-permute-start | bytes 1572872 | tf_op jit(solution)/shard_map/ppermute | solution.py:396
  16.9 0.7 %biases.1.bias_ref = f32[32,128]{1,0:T(8,128)S(1)} custom-call(s32[2,8]{1,0:T(2,128)S(1)} %bitcast.3, s32[2]{0:T(128)S(1)} %copy-done.5, bf16[1024,256]{1,0:T(8,128)(2,1)S(1)} %halves.1.after_ref.refs_3_), custom_call_target="tpu_custom_call" | custom-call | flops 1000 | bytes 1000 | tf_op jit(solution)/shard_map/biases/pallas_call | solution.py:85
  17.6 0.3 ask.1.q_ref
  17.9 0.1 collective-permute-start.6
  18.0 3.6 %collective-permute-done.1.refs_1_.a_ref = bf16[512,256]{1,0:T(8,128)(2,1)S(1)} collective-permute-done((bf16[512,256]{1,0:T(8,128)(2,1)S(1)}, bf16[512,256]{1,0:T(8,128)(2,1)S(1)}, u32[]{:S(2)}, u32[]{:S(2)}) %collective-permute-start.1) | collective-permute-done | bytes 262176 | tf_op jit(solution)/shard_map/ppermute | solution.py:390
  21.6 1.5 %attend.3 = (f32[512,128]{1,0:T(8,128)S(1)}, f32[4,512]{1,0:T(4,128)S(1)}) custom-call(f32[32,128]{1,0:T(8,128)S(1)} %biases.1.bias_ref, bf16[256,256]{1,0:T(8,128)(2,1)S(1)} %ask.1.q_ref, bf16[512,256]{1,0:T(8,128)(2,1)S(1)} %get-tuple-element.20.refs_0_, bf16[512,256]{1,0:T(8,128)(2,1)S(1)} %collective-permute-done.1.refs_1_.a_ref, ...), custom_call_target="tpu_custom_call" | custom-call | flops 1000 | bytes 1000 | tf_op jit(solution)/shard_map/attend/pallas_call | solution.py:213
  23.2 2.3 %collective-permute-done.4.refs_1_.refs_2_ = bf16[512,256]{1,0:T(8,128)(2,1)S(1)} collective-permute-done((bf16[512,256]{1,0:T(8,128)(2,1)S(1)}, bf16[512,256]{1,0:T(8,128)(2,1)S(1)}, u32[]{:S(2)}, u32[]{:S(2)}) %collective-permute-start.4) | collective-permute-done | bytes 262176 | tf_op jit(solution)/shard_map/ppermute | solution.py:391
  25.6 0.1 collective-permute-start.5
  25.7 1.5 %attend.4 = (f32[512,128]{1,0:T(8,128)S(1)}, f32[4,512]{1,0:T(4,128)S(1)}) custom-call(f32[32,128]{1,0:T(8,128)S(1)} %biases.1.bias_ref, bf16[256,256]{1,0:T(8,128)(2,1)S(1)} %ask.1.q_ref, bf16[512,256]{1,0:T(8,128)(2,1)S(1)} %collective-permute-done.6.refs_0_, bf16[512,256]{1,0:T(8,128)(2,1)S(1)} %collective-permute-done.3.refs_0_.refs_1_, ...), custom_call_target="tpu_custom_call" | custom-call | flops 1000 | bytes 1000 | tf_op jit(solution)/shard_map/attend/pallas_call | solution.py:213
  27.2 0.9 %collective-permute-done.7.refs_3_.a_ref.mine = bf16[1024,256]{1,0:T(8,128)(2,1)S(1)} collective-permute-done((bf16[1024,256]{1,0:T(8,128)(2,1)S(1)}, bf16[1024,256]{1,0:T(8,128)(2,1)S(1)}, u32[]{:S(2)}, u32[]{:S(2)}) %collective-permute-start.7) | collective-permute-done | bytes 524320 | tf_op jit(solution)/shard_map/ppermute | solution.py:396
  28.1 1.1 %attend.5.after_ref.a0 = bf16[256,256]{1,0:T(8,128)(2,1)S(1)} custom-call(f32[32,128]{1,0:T(8,128)S(1)} %biases.1.bias_ref, bf16[256,256]{1,0:T(8,128)(2,1)S(1)} %ask.1.q_ref, bf16[512,256]{1,0:T(8,128)(2,1)S(1)} %collective-permute-done.5.refs_0_, f32[512,128]{1,0:T(8,128)S(1)} %get-tuple-element.23.refs_1_, f32[4,512]{1,0:T(4,128)S(1)} %get-tuple-element.24.refs_2_, ...), custom_call_target="tpu_custom_call" | custom-call | flops 1000 | bytes 1000 | tf_op jit(solution)/shard_map/attend/pallas_call | solution.py:213
  29.3 2.8 %collective-permute-start.10 = (bf16[256,256]{1,0:T(8,128)(2,1)S(1)}, bf16[256,256]{1,0:T(8,128)(2,1)S(1)}, u32[]{:S(2)}, u32[]{:S(2)}) collective-permute-start(bf16[256,256]{1,0:T(8,128)(2,1)S(1)} %attend.5.after_ref.a0), channel_id=1, source_target_pairs={{0,6},{2,4},{4,2},{6,0},{1,7},{3,5},{5,3},{7,1},{8,14},{10,12},{12... | collective-permute-start | bytes 393224 | tf_op jit(solution)/shard_map/ppermute | solution.py:404
  32.2 1.3 %collective-permute-start.8 = (bf16[256,256]{1,0:T(8,128)(2,1)S(1)}, bf16[256,256]{1,0:T(8,128)(2,1)S(1)}, u32[]{:S(2)}, u32[]{:S(2)}) collective-permute-start(bf16[256,256]{1,0:T(8,128)(2,1)S(1)} %attend.5.after_ref.a0), channel_id=1, source_target_pairs={{0,2},{2,0},{4,6},{6,4},{1,3},{3,1},{5,7},{7,5},{8,10},{10,8},{12,... | collective-permute-start | bytes 393224 | tf_op jit(solution)/shard_map/ppermute | solution.py:404
  33.5 4.8 %collective-permute-done.10.a3 = bf16[256,256]{1,0:T(8,128)(2,1)S(1)} collective-permute-done((bf16[256,256]{1,0:T(8,128)(2,1)S(1)}, bf16[256,256]{1,0:T(8,128)(2,1)S(1)}, u32[]{:S(2)}, u32[]{:S(2)}) %collective-permute-start.10) | collective-permute-done | bytes 131104 | tf_op jit(solution)/shard_map/ppermute | solution.py:404
  38.3 1.7 %collective-permute-done.9.a2 = bf16[256,256]{1,0:T(8,128)(2,1)S(1)} collective-permute-done((bf16[256,256]{1,0:T(8,128)(2,1)S(1)}, bf16[256,256]{1,0:T(8,128)(2,1)S(1)}, u32[]{:S(2)}, u32[]{:S(2)}) %collective-permute-start.9) | collective-permute-done | bytes 131104 | tf_op jit(solution)/shard_map/ppermute | solution.py:404
  40.0 2.2 %feed.1 = (f32[64,1024]{1,0:T(8,128)S(1)}, bf16[64,1024]{1,0:T(8,128)(2,1)S(1)}, bf16[64,1024]{1,0:T(8,128)(2,1)S(1)}, bf16[64,1024]{1,0:T(8,128)(2,1)S(1)}) custom-call(bf16[256,1024]{1,0:T(8,128)(2,1)S(1)} %get-tuple-element.18.x_ref, bf16[256,256]{1,0:T(8,128)(2,1)S(1)} %attend.5.after_ref.a0, bf16[256,256]{1,0:T(8,128)(2,1)S(1)} %collective-permute-done.8.a1, ...), custom_call_target="tpu_custom_call" | custom-call | flops 1000 | bytes 1000 | tf_op jit(solution)/shard_map/feed/pallas_call | solution.py:323
  42.2 0.9 %collective-permute-start.12 = (bf16[64,1024]{1,0:T(8,128)(2,1)S(1)}, bf16[64,1024]{1,0:T(8,128)(2,1)S(1)}, u32[]{:S(2)}, u32[]{:S(2)}) collective-permute-start(bf16[64,1024]{1,0:T(8,128)(2,1)S(1)} %get-tuple-element.26), channel_id=1, source_target_pairs={{0,2},{2,0},{4,6},{6,4},{1,3},{3,1},{5,7},{7,5},{8,10},{10,8},{12,... | collective-permute-start | bytes 393224 | tf_op jit(solution)/shard_map/ppermute | solution.py:406
  43.2 3.2 %collective-permute-start.13 = (bf16[64,1024]{1,0:T(8,128)(2,1)S(1)}, bf16[64,1024]{1,0:T(8,128)(2,1)S(1)}, u32[]{:S(2)}, u32[]{:S(2)}) collective-permute-start(bf16[64,1024]{1,0:T(8,128)(2,1)S(1)} %get-tuple-element.27), channel_id=1, source_target_pairs={{0,4},{2,6},{4,0},{6,2},{1,5},{3,7},{5,1},{7,3},{8,12},{10,14},{12... | collective-permute-start | bytes 393224 | tf_op jit(solution)/shard_map/ppermute | solution.py:406
  46.4 0.7 %collective-permute-start.14 = (bf16[64,1024]{1,0:T(8,128)(2,1)S(1)}, bf16[64,1024]{1,0:T(8,128)(2,1)S(1)}, u32[]{:S(2)}, u32[]{:S(2)}) collective-permute-start(bf16[64,1024]{1,0:T(8,128)(2,1)S(1)} %get-tuple-element.28), channel_id=1, source_target_pairs={{0,6},{2,4},{4,2},{6,0},{1,7},{3,5},{5,3},{7,1},{8,14},{10,12},{12... | collective-permute-start | bytes 393224 | tf_op jit(solution)/shard_map/ppermute | solution.py:406
  47.0 1.5 %collective-permute-done.12.r1 = bf16[64,1024]{1,0:T(8,128)(2,1)S(1)} collective-permute-done((bf16[64,1024]{1,0:T(8,128)(2,1)S(1)}, bf16[64,1024]{1,0:T(8,128)(2,1)S(1)}, u32[]{:S(2)}, u32[]{:S(2)}) %collective-permute-start.12) | collective-permute-done | bytes 131104 | tf_op jit(solution)/shard_map/ppermute | solution.py:406
  48.6 3.4 %collective-permute-done.13.r2 = bf16[64,1024]{1,0:T(8,128)(2,1)S(1)} collective-permute-done((bf16[64,1024]{1,0:T(8,128)(2,1)S(1)}, bf16[64,1024]{1,0:T(8,128)(2,1)S(1)}, u32[]{:S(2)}, u32[]{:S(2)}) %collective-permute-start.13) | collective-permute-done | bytes 131104 | tf_op jit(solution)/shard_map/ppermute | solution.py:406
  52.0 1.8 %collective-permute-done.14.r3 = bf16[64,1024]{1,0:T(8,128)(2,1)S(1)} collective-permute-done((bf16[64,1024]{1,0:T(8,128)(2,1)S(1)}, bf16[64,1024]{1,0:T(8,128)(2,1)S(1)}, u32[]{:S(2)}, u32[]{:S(2)}) %collective-permute-start.14) | collective-permute-done | bytes 131104 | tf_op jit(solution)/shard_map/ppermute | solution.py:406
  53.8 7.3 %collective-permute-start.15 = (bf16[32,1024]{1,0:T(8,128)(2,1)S(1)}, bf16[32,1024]{1,0:T(8,128)(2,1)S(1)}, u32[]{:S(2)}, u32[]{:S(2)}) collective-permute-start(bf16[32,1024]{1,0:T(8,128)(2,1)S(1)} %get-tuple-element.30), channel_id=1, source_target_pairs={{0,1},{1,0},{2,3},{3,2},{4,5},{5,4},{6,7},{7,6},{8,9},{9,8},{10,11... | collective-permute-start | bytes 196616 | tf_op jit(solution)/shard_map/ppermute | solution.py:408
  61.7 1.7 %collective-permute-done.15.other_ref = bf16[32,1024]{1,0:T(8,128)(2,1)S(1)} collective-permute-done((bf16[32,1024]{1,0:T(8,128)(2,1)S(1)}, bf16[32,1024]{1,0:T(8,128)(2,1)S(1)}, u32[]{:S(2)}, u32[]{:S(2)}) %collective-permute-start.15) | collective-permute-done | bytes 65568 | tf_op jit(solution)/shard_map/ppermute | solution.py:408
  63.4 0.7 %guide.1 = bf16[32,1024]{1,0:T(8,128)(2,1)} custom-call(f32[1]{0:T(128)S(6)} %copy.11.guidance_ref, f32[32,1024]{1,0:T(8,128)S(1)} %get-tuple-element.29.kept_ref, bf16[32,1024]{1,0:T(8,128)(2,1)S(1)} %collective-permute-done.15.other_ref), custom_call_target="tpu_custom_call" | custom-call | flops 1000 | bytes 1000 | tf_op jit(solution)/shard_map/guide/pallas_call | solution.py:372
  (24 shorter events, 0.3 us)
Async XLA Ops:
  0.0 16.9 %copy-start.5 = (s32[2]{0:T(128)S(1)}, s32[2]{0:T(128)}, u32[]{:S(2)}) copy-start(s32[2]{0:T(128)} %counts_ref.1) | copy-start | bytes 28
  0.0 16.9 %copy-start.4 = (s32[8,2]{0,1:T(2,128)S(1)}, s32[8,2]{0,1:T(2,128)}, u32[]{:S(2)}) copy-start(s32[8,2]{0,1:T(2,128)} %param.11) | copy-start | bytes 196
  0.0 17.6 %copy-start.3 = (bf16[1024,256]{1,0:T(8,128)(2,1)S(1)}, bf16[1024,256]{1,0:T(8,128)(2,1)}, u32[]{:S(2)}) copy-start(bf16[1024,256]{1,0:T(8,128)(2,1)} %wq_ref.1) | copy-start | bytes 1572868
  0.0 14.0 %collective-permute-start = (bf16[256,1024]{1,0:T(8,128)(2,1)}, bf16[256,1024]{1,0:T(8,128)(2,1)S(1)}, u32[]{:S(2)}, u32[]{:S(2)}) collective-permute-start(bf16[256,1024]{1,0:T(8,128)(2,1)} %o0.1), channel_id=1, source_target_pairs={{0,2},{2,0},{4,6},{6,4},{1,3},{3,1},{5,7},{7,5},{8,10},{10,8},{12,... | collective-permute-start | bytes 1572872 | tf_op jit(solution)/shard_map/ppermute | solution.py:392
  3.7 14.2 %collective-permute-start.2 = (bf16[512,256]{1,0:T(8,128)(2,1)S(1)}, bf16[512,256]{1,0:T(8,128)(2,1)S(1)}, u32[]{:S(2)}, u32[]{:S(2)}) collective-permute-start(bf16[512,256]{1,0:T(8,128)(2,1)S(1)} %get-tuple-element.20.refs_0_), channel_id=1, source_target_pairs={{0,16},{8,24},{16,32},{24,40},{32,48},{40,56},{48,64},{56,72},{64,... | collective-permute-start | bytes 786440 | tf_op jit(solution)/shard_map/ppermute | solution.py:390
  5.4 16.3 %collective-permute-start.1 = (bf16[512,256]{1,0:T(8,128)(2,1)S(1)}, bf16[512,256]{1,0:T(8,128)(2,1)S(1)}, u32[]{:S(2)}, u32[]{:S(2)}) collective-permute-start(bf16[512,256]{1,0:T(8,128)(2,1)S(1)} %get-tuple-element.20.refs_0_), channel_id=1, source_target_pairs={{0,240},{8,248},{16,0},{24,8},{32,16},{40,24},{48,32},{56,40},{64,... | collective-permute-start | bytes 786440 | tf_op jit(solution)/shard_map/ppermute | solution.py:390
  5.8 19.7 %collective-permute-start.4 = (bf16[512,256]{1,0:T(8,128)(2,1)S(1)}, bf16[512,256]{1,0:T(8,128)(2,1)S(1)}, u32[]{:S(2)}, u32[]{:S(2)}) collective-permute-start(bf16[512,256]{1,0:T(8,128)(2,1)S(1)} %get-tuple-element.20.refs_0_), channel_id=1, source_target_pairs={{0,32},{8,40},{16,48},{24,56},{32,64},{40,72},{48,80},{56,88},{64,... | collective-permute-start | bytes 786440 | tf_op jit(solution)/shard_map/ppermute | solution.py:391
  8.1 17.4 %collective-permute-start.3 = (bf16[512,256]{1,0:T(8,128)(2,1)S(1)}, bf16[512,256]{1,0:T(8,128)(2,1)S(1)}, u32[]{:S(2)}, u32[]{:S(2)}) collective-permute-start(bf16[512,256]{1,0:T(8,128)(2,1)S(1)} %get-tuple-element.20.refs_0_), channel_id=1, source_target_pairs={{0,224},{8,232},{16,240},{24,248},{32,0},{40,8},{48,16},{56,24},{6... | collective-permute-start | bytes 786440 | tf_op jit(solution)/shard_map/ppermute | solution.py:391
  14.0 14.1 %collective-permute-start.7 = (bf16[1024,256]{1,0:T(8,128)(2,1)S(1)}, bf16[1024,256]{1,0:T(8,128)(2,1)S(1)}, u32[]{:S(2)}, u32[]{:S(2)}) collective-permute-start(bf16[1024,256]{1,0:T(8,128)(2,1)S(1)} %halves.1.after_ref.refs_3_), channel_id=1, source_target_pairs={{0,6},{2,4},{4,2},{6,0},{1,7},{3,5},{5,3},{7,1},{8,14},{10,12},{12... | collective-permute-start | bytes 1572872 | tf_op jit(solution)/shard_map/ppermute | solution.py:396
  17.9 7.7 %collective-permute-start.6 = (bf16[512,256]{1,0:T(8,128)(2,1)S(1)}, bf16[512,256]{1,0:T(8,128)(2,1)S(1)}, u32[]{:S(2)}, u32[]{:S(2)}) collective-permute-start(bf16[512,256]{1,0:T(8,128)(2,1)S(1)} %get-tuple-element.20.refs_0_), channel_id=1, source_target_pairs={{0,8},{8,0},{16,24},{24,16},{32,40},{40,32},{48,56},{56,48},{64,72... | collective-permute-start | bytes 786440 | tf_op jit(solution)/shard_map/ppermute | solution.py:399
  25.5 14.5 %copy-start.2 = (bf16[1024,1024]{1,0:T(8,128)(2,1)S(1)}, bf16[1024,1024]{1,0:T(8,128)(2,1)}, u32[]{:S(2)}) copy-start(bf16[1024,1024]{1,0:T(8,128)(2,1)} %wback_ref.1) | copy-start | bytes 6291460
  25.5 14.5 %copy-start = (bf16[256,1024]{1,0:T(8,128)(2,1)S(1)}, bf16[256,1024]{1,0:T(8,128)(2,1)}, u32[]{:S(2)}) copy-start(bf16[256,1024]{1,0:T(8,128)(2,1)} %o0.1) | copy-start | bytes 1572868
  25.6 14.5 %copy-start.1 = (bf16[1024,1024]{1,0:T(8,128)(2,1)S(1)}, bf16[1024,1024]{1,0:T(8,128)(2,1)}, u32[]{:S(2)}) copy-start(bf16[1024,1024]{1,0:T(8,128)(2,1)} %win_ref.1) | copy-start | bytes 6291460
  25.6 1.7 %collective-permute-start.5 = (bf16[512,256]{1,0:T(8,128)(2,1)S(1)}, bf16[512,256]{1,0:T(8,128)(2,1)S(1)}, u32[]{:S(2)}, u32[]{:S(2)}) collective-permute-start(bf16[512,256]{1,0:T(8,128)(2,1)S(1)} %pick.1), channel_id=1, source_target_pairs={{0,8},{8,0},{16,24},{24,16},{32,40},{40,32},{48,56},{56,48},{64,72... | collective-permute-start | bytes 786440 | tf_op jit(solution)/shard_map/ppermute | solution.py:399
  29.2 10.8 %collective-permute-start.11 = (bf16[1024,256]{1,0:T(8,128)(2,1)S(1)}, bf16[1024,256]{1,0:T(8,128)(2,1)S(1)}, u32[]{:S(2)}, u32[]{:S(2)}) collective-permute-start(bf16[1024,256]{1,0:T(8,128)(2,1)S(1)} %kept_until.1), channel_id=1, source_target_pairs={{0,8},{8,0},{16,24},{24,16},{32,40},{40,32},{48,56},{56,48},{64,72... | collective-permute-start | bytes 1572872 | tf_op jit(solution)/shard_map/ppermute | solution.py:402
  29.3 9.0 %collective-permute-start.10 = (bf16[256,256]{1,0:T(8,128)(2,1)S(1)}, bf16[256,256]{1,0:T(8,128)(2,1)S(1)}, u32[]{:S(2)}, u32[]{:S(2)}) collective-permute-start(bf16[256,256]{1,0:T(8,128)(2,1)S(1)} %attend.5.after_ref.a0), channel_id=1, source_target_pairs={{0,6},{2,4},{4,2},{6,0},{1,7},{3,5},{5,3},{7,1},{8,14},{10,12},{12... | collective-permute-start | bytes 393224 | tf_op jit(solution)/shard_map/ppermute | solution.py:404
  32.2 7.8 %collective-permute-start.9 = (bf16[256,256]{1,0:T(8,128)(2,1)S(1)}, bf16[256,256]{1,0:T(8,128)(2,1)S(1)}, u32[]{:S(2)}, u32[]{:S(2)}) collective-permute-start(bf16[256,256]{1,0:T(8,128)(2,1)S(1)} %attend.5.after_ref.a0), channel_id=1, source_target_pairs={{0,4},{2,6},{4,0},{6,2},{1,5},{3,7},{5,1},{7,3},{8,12},{10,14},{12... | collective-permute-start | bytes 393224 | tf_op jit(solution)/shard_map/ppermute | solution.py:404
  32.2 7.8 %collective-permute-start.8 = (bf16[256,256]{1,0:T(8,128)(2,1)S(1)}, bf16[256,256]{1,0:T(8,128)(2,1)S(1)}, u32[]{:S(2)}, u32[]{:S(2)}) collective-permute-start(bf16[256,256]{1,0:T(8,128)(2,1)S(1)} %attend.5.after_ref.a0), channel_id=1, source_target_pairs={{0,2},{2,0},{4,6},{6,4},{1,3},{3,1},{5,7},{7,5},{8,10},{10,8},{12,... | collective-permute-start | bytes 393224 | tf_op jit(solution)/shard_map/ppermute | solution.py:404
  42.2 6.3 %collective-permute-start.12 = (bf16[64,1024]{1,0:T(8,128)(2,1)S(1)}, bf16[64,1024]{1,0:T(8,128)(2,1)S(1)}, u32[]{:S(2)}, u32[]{:S(2)}) collective-permute-start(bf16[64,1024]{1,0:T(8,128)(2,1)S(1)} %get-tuple-element.26), channel_id=1, source_target_pairs={{0,2},{2,0},{4,6},{6,4},{1,3},{3,1},{5,7},{7,5},{8,10},{10,8},{12,... | collective-permute-start | bytes 393224 | tf_op jit(solution)/shard_map/ppermute | solution.py:406
  43.2 8.8 %collective-permute-start.13 = (bf16[64,1024]{1,0:T(8,128)(2,1)S(1)}, bf16[64,1024]{1,0:T(8,128)(2,1)S(1)}, u32[]{:S(2)}, u32[]{:S(2)}) collective-permute-start(bf16[64,1024]{1,0:T(8,128)(2,1)S(1)} %get-tuple-element.27), channel_id=1, source_target_pairs={{0,4},{2,6},{4,0},{6,2},{1,5},{3,7},{5,1},{7,3},{8,12},{10,14},{12... | collective-permute-start | bytes 393224 | tf_op jit(solution)/shard_map/ppermute | solution.py:406
  46.4 7.4 %collective-permute-start.14 = (bf16[64,1024]{1,0:T(8,128)(2,1)S(1)}, bf16[64,1024]{1,0:T(8,128)(2,1)S(1)}, u32[]{:S(2)}, u32[]{:S(2)}) collective-permute-start(bf16[64,1024]{1,0:T(8,128)(2,1)S(1)} %get-tuple-element.28), channel_id=1, source_target_pairs={{0,6},{2,4},{4,2},{6,0},{1,7},{3,5},{5,3},{7,1},{8,14},{10,12},{12... | collective-permute-start | bytes 393224 | tf_op jit(solution)/shard_map/ppermute | solution.py:406
  53.8 9.6 %collective-permute-start.15 = (bf16[32,1024]{1,0:T(8,128)(2,1)S(1)}, bf16[32,1024]{1,0:T(8,128)(2,1)S(1)}, u32[]{:S(2)}, u32[]{:S(2)}) collective-permute-start(bf16[32,1024]{1,0:T(8,128)(2,1)S(1)} %get-tuple-element.30), channel_id=1, source_target_pairs={{0,1},{1,0},{2,3},{3,2},{4,5},{5,4},{6,7},{7,6},{8,9},{9,8},{10,11... | collective-permute-start | bytes 196616 | tf_op jit(solution)/shard_map/ppermute | solution.py:408

commit v4 on v3

--- a/solution.py
+++ b/solution.py
@@ -25,8 +25,18 @@
     return pltpu.CompilerParams(vmem_limit_bytes=int(mib * 1024 * 1024))
 
 
-def shifted(axis, count, apart):
-    return functools.partial(lax.ppermute, axis_name=axis, perm=[(i, (i - apart) % count) for i in range(count)])
+def matched(count, apart, parity):
+    route = []
+    for low in range(count):
+        if (low // apart) % 2 == parity:
+            high = (low + apart) % count
+            route += [(low, high), (high, low)]
+    return functools.partial(lax.ppermute, axis_name="view", perm=route)
+
+
+def onward(count):
+    route = [(i, (i + 8 - 4 * (i & 4)) % count) for i in range(count)]
+    return functools.partial(lax.ppermute, axis_name="view", perm=route)
 
 
 def flipped(axis, count, bits):
@@ -57,7 +67,8 @@
 def key_views(count):
     me = lax.axis_index("view")
     core = me & 1
-    sources = (me, me + 1 - 2 * core, me + 2, me - 2, me - 1 + 2 * core, me + 4, me - 4)
+    near, far = 2 * (me & 2) - 2, 4 - 2 * (me & 4)
+    sources = (me, me + 1 - 2 * core, me + near, me - near, me - 1 + 2 * core, me + far, me - far)
     return [2 * lax.rem(s + count, count) for s in sources]
 
 
@@ -223,7 +234,8 @@
 
 def pick_kernel(a_ref, b_ref, *refs):
     out_ref = refs[-1]
-    first = lax.axis_index("view") & 1 == 0
+    me = lax.axis_index("view")
+    first = (me & 1) != ((me >> 1) & 1)
 
     @pl.when(first)
     def _():
@@ -246,46 +258,27 @@
     )(a, b, *after)
 
 
-def halves_kernel(a_ref, b_ref, out_ref):
-    half = a_ref.shape[0]
-    block = out_ref.shape[1]
-    rows = pl.ds(pl.multiple_of((lax.axis_index("view") & 1) * half, half), half)
-    for j in range(a_ref.shape[1] // block):
-        columns = slice(j * block, (j + 1) * block)
-        out_ref[2 * j * half : (2 * j + 1) * half] = a_ref[:, columns]
-        out_ref[(2 * j + 1) * half : (2 * j + 2) * half] = b_ref[rows, columns]
-
-
-def halves(a, b):
-    rows, columns = b.shape
-    return pl.pallas_call(
-        halves_kernel,
-        out_shape=held((columns, rows), a.dtype),
-        in_specs=[VMEM, VMEM],
+def stack_kernel(*refs):
+    *piece_refs, _, out_ref = refs
+    at = 0
+    for ref in piece_refs:
+        out_ref[at : at + ref.shape[0]] = ref[...]
+        at += ref.shape[0]
+
+
+def stack(*pieces, after):
+    return pl.pallas_call(
+        stack_kernel,
+        out_shape=held((sum(p.shape[0] for p in pieces), pieces[0].shape[1]), pieces[0].dtype),
+        in_specs=[VMEM] * len(pieces) + [ANY],
         out_specs=VMEM,
         compiler_params=params(2),
         cost_estimate=COST,
-        name="halves",
-    )(a, b)
-
-
-def kept_until_kernel(a_ref, after_ref, out_ref):
-    out_ref[...] = a_ref[...]
-
-
-def kept_until(a, after):
-    return pl.pallas_call(
-        kept_until_kernel,
-        out_shape=held(a.shape, a.dtype),
-        in_specs=[VMEM, ANY],
-        out_specs=VMEM,
-        compiler_params=params(2),
-        cost_estimate=COST,
-        name="kept_until",
-    )(a, after)
-
-
-def feed_kernel(x_ref, a0, a1, a2, a3, o0, o1, mine, pair, win_ref, wback_ref, own_ref, r1, r2, r3):
+        name="stack",
+    )(*pieces, after)
+
+
+def feed_kernel(x_ref, a0, a1, a2, a3, o0, w1, w32, pair, win_ref, wback_ref, own_ref, r1, r2, r3):
     head = lax.axis_index("head")
     rows, width = x_ref.shape
     tok = rows // 2
@@ -299,15 +292,14 @@
                 pieces.append(ref[pl.ds(start, part), columns])
         return jnp.concatenate(pieces, axis=0)
 
-    block = o0.shape[0]
+    half = w1.shape[0]
     core = lax.axis_index("view") & 1
-    attention = dot(turned(a0), o0[...]) + dot(turned(a1), o1[...])
-    parts = []
-    for ref, first, which in ((mine, 0, core), (pair, pair.shape[0] - width, 1 - core)):
-        columns = pl.ds(pl.multiple_of(which * (block // 2), block // 2), block // 2)
-        both = jnp.concatenate([turned(a3, columns), turned(a2, columns)], axis=1)
-        parts.append([dot(both, ref[first + i : first + i + block]) for i in range(0, width, block)])
-    attention = attention + jnp.concatenate([m + p for m, p in zip(*parts)], axis=1)
+    mine = pl.ds(pl.multiple_of(core * half, half), half)
+    theirs = pl.ds(pl.multiple_of((1 - core) * half, half), half)
+    left = jnp.concatenate([turned(a, rows) for a in (a1, a3, a2) for rows in (mine, theirs)], axis=1)
+    own = (w1[...], w32[:half], w32[half:])
+    right = [r for i, w in enumerate(own) for r in (w, pair[i * half : (i + 1) * half])]
+    attention = dot(turned(a0), o0[...]) + dot(left, jnp.concatenate(right, axis=0))
     y = turned(x_ref).astype(jnp.float32) + attention
     normed = (y * lax.rsqrt(jnp.mean(y * y, axis=-1, keepdims=True) + 1e-06)).astype(jnp.bfloat16)
     hidden = jax.nn.gelu(dot(normed, win_ref[...])).astype(jnp.bfloat16)
@@ -387,19 +379,19 @@
 
     x, kv, w_half = project(x, w_key, w_value, w_out)
 
-    near = [shifted("view", count, d)(kv) for d in (2, -2)]
-    far = [shifted("view", count, d)(kv) for d in (4, -4)]
-    w_1 = flipped("head", 4, 1)(w_out)
-    w_01 = halves(w_half, w_1)
-    q = ask(x, w_query, w_01)
-    bias = biases(count, partners.T, counts, w_01)
-    w_32 = flipped("head", 4, 3)(w_01)
-    state = attend(((0, 0, True), (2, 0, False), (3, 0, False)), True, False, bias, q, (kv, *near), (), *(w_01,))
+    near = [matched(count, 2, parity)(kv) for parity in (1, 0)]
+    across = flipped("view", count, 4)(kv)
+    far = (across, onward(count)(across))
+    w_1 = flipped("head", 4, 1)(w_half)
+    w_32 = flipped("head", 4, 3)(stack(w_half, w_1, after=x))
+    q = ask(x, w_query, x)
+    bias = biases(count, partners.T, counts, x)
+    state = attend(((0, 0, True), (2, 0, False), (3, 0, False)), True, False, bias, q, (kv, *near))
     other_core = flipped("view", count, 1)
     other, cross = other_core(kv), other_core(pick(*near, *far, state[1]))
-    state = attend(((1, 0, True), (5, 0, False), (6, 0, False)), False, False, bias, q, (other, *far), state)
-    attended = attend(((4, 0, True),), False, True, bias, q, (cross,), state, w_32)
-    w_pair = flipped("view", count, 1)(kept_until(w_32, attended))
+    state = attend(((1, 0, True), (5, 0, False), (6, 0, False)), False, False, bias, q, (other, *far), state, w_32)
+    attended = attend(((4, 0, True),), False, True, bias, q, (cross,), state)
+    w_pair = other_core(stack(w_1, w_32, after=attended))
 
     pieces = [attended] + [flipped("head", 4, j)(attended) for j in (1, 2, 3)]
     own, *outgoing = feed(x, pieces, (w_out, w_1, w_32, w_pair), w_in, w_back)

time: 64.2 us -> 62.8 us (0.978)
  waiting for transfers between devices: 23.5 us -> 21.5 us
    ppermute x7, waiting for transfers between devices: 8.6 us -> 7.19 us  [the longest x1 3.18 us: on_device(): far = (across, onward(count)(across))]
    ppermute x7, starting transfers between devices: 13 us -> 14.3 us  [the longest x2 6.46 us: on_device(): near = [matched(count, 2, parity)(kv) for parity in (1, 0)]]
    ppermute x1, starting transfers between devices: 7.27 us -> 5.98 us  [on_device(): other = flipped('branch', 2, 1)(sent)]
  transfers between devices with their start and end apart: 16 -> 16, of which waited for: 10 -> 11; matrix products, arithmetic and copies ran while one was open for 0% -> 0% of each run, Pallas kernels for 10% -> 7%
where the time goes in v4:
time: 62.8 us; the launch traced here: 62.7 us
  starting transfers between devices  30 us (48%)
  waiting for transfers between devices  21.5 us (34%)
  Pallas kernels  10.4 us (17%)
  between operations  0.82 us (1%)
    ppermute x2, starting transfers between devices, on_device(): near = [matched(count, 2, parity)(kv) for parity in (1, 0)]  6.46 us
    ppermute x3, waiting for transfers between devices, on_device(): pieces = [attended] + [flipped('head', 4, j)(attended) for j in (1, 2, 3)]  6.33 us
    ppermute x3, waiting for transfers between devices, on_device(): received = [flipped('head', 4, j)(r) for j, r in zip((1, 2, 3), outgoing)]  6.23 us
    ppermute x1, starting transfers between devices, on_device(): other = flipped('branch', 2, 1)(sent)  5.98 us
    ppermute x3, starting transfers between devices, on_device(): pieces = [attended] + [flipped('head', 4, j)(attended) for j in (1, 2, 3)]  4.79 us
    ppermute x3, starting transfers between devices, on_device(): received = [flipped('head', 4, j)(r) for j, r in zip((1, 2, 3), outgoing)]  4.78 us
    pallas_call x3, Pallas kernels, attend(): pl.pallas_call(functools.partial(attend_kernel, blocks, first, last), out...  4.12 us
    ppermute x1, waiting for transfers between devices, on_device(): far = (across, onward(count)(across))  3.18 us
  transfers between devices with their start and end apart: 16, of which 11 were waited for; matrix products, arithmetic and copies ran while one was open for 0% of the time, Pallas kernels for 7%

profile of v4, /device:TPU:8, one launch (start us, length us, event | category | flops | bytes accessed | tf_op | source)
XLA Modules:
  0.0 62.7 jit_solution(5111721556284729386)
XLA Ops:
  0.0 2.2 %project.1 = (bf16[256,1024]{1,0:T(8,128)(2,1)S(1)}, bf16[512,256]{1,0:T(8,128)(2,1)S(1)}, bf16[128,1024]{1,0:T(8,128)(2,1)S(1)}) custom-call(bf16[256,1024]{1,0:T(8,128)(2,1)} %bitcast.4, bf16[1024,256]{1,0:T(8,128)(2,1)} %wk_hbm.1, bf16[1024,256]{1,0:T(8,128)(2,1)} %wv_hbm.1, bf16[256,1024]{1,0:T(8,128)(2,1)} %o0.1), custom_call_target="tpu_custom_call" | custom-call | flops 1000 | bytes 1000 | tf_op jit(solution)/shard_map/project/pallas_call | solution.py:126
  2.2 1.6 %collective-permute-start.6 = (bf16[128,1024]{1,0:T(8,128)(2,1)S(1)}, bf16[128,1024]{1,0:T(8,128)(2,1)S(1)}, u32[]{:S(2)}, u32[]{:S(2)}) collective-permute-start(bf16[128,1024]{1,0:T(8,128)(2,1)S(1)} %get-tuple-element.22.refs_0_), channel_id=1, source_target_pairs={{0,2},{2,0},{4,6},{6,4},{1,3},{3,1},{5,7},{7,5},{8,10},{10,8},{12,... | collective-permute-start | bytes 786440 | tf_op jit(solution)/shard_map/ppermute | solution.py:385
  3.8 2.3 %collective-permute-start.2 = (bf16[512,256]{1,0:T(8,128)(2,1)S(1)}, bf16[512,256]{1,0:T(8,128)(2,1)S(1)}, u32[]{:S(2)}, u32[]{:S(2)}) collective-permute-start(bf16[512,256]{1,0:T(8,128)(2,1)S(1)} %get-tuple-element.19.refs_0_), channel_id=1, source_target_pairs={{0,32},{8,40},{16,48},{24,56},{32,0},{40,8},{48,16},{56,24},{64,96... | collective-permute-start | bytes 786440 | tf_op jit(solution)/shard_map/ppermute | solution.py:383
  6.1 6.5 %collective-permute-start.1 = (bf16[512,256]{1,0:T(8,128)(2,1)S(1)}, bf16[512,256]{1,0:T(8,128)(2,1)S(1)}, u32[]{:S(2)}, u32[]{:S(2)}) collective-permute-start(bf16[512,256]{1,0:T(8,128)(2,1)S(1)} %get-tuple-element.19.refs_0_), channel_id=1, source_target_pairs={{0,16},{16,0},{8,24},{24,8},{32,48},{48,32},{40,56},{56,40},{64,80... | collective-permute-start | bytes 786440 | tf_op jit(solution)/shard_map/ppermute | solution.py:382
  12.6 2.2 %collective-permute-start.7 = (bf16[256,1024]{1,0:T(8,128)(2,1)S(1)}, bf16[256,1024]{1,0:T(8,128)(2,1)S(1)}, u32[]{:S(2)}, u32[]{:S(2)}) collective-permute-start(bf16[256,1024]{1,0:T(8,128)(2,1)S(1)} %stack.2), channel_id=1, source_target_pairs={{0,6},{2,4},{4,2},{6,0},{1,7},{3,5},{5,3},{7,1},{8,14},{10,12},{12... | collective-permute-start | bytes 1572872 | tf_op jit(solution)/shard_map/ppermute | solution.py:386
  14.8 1.7 %collective-permute-start.3 = (bf16[512,256]{1,0:T(8,128)(2,1)S(1)}, bf16[512,256]{1,0:T(8,128)(2,1)S(1)}, u32[]{:S(2)}, u32[]{:S(2)}) collective-permute-start(bf16[512,256]{1,0:T(8,128)(2,1)S(1)} %collective-permute-done.2.refs_0_.refs_1_), channel_id=1, source_target_pairs={{0,64},{8,72},{16,80},{24,88},{32,224},{40,232},{48,240},{56,248},... | collective-permute-start | bytes 786440 | tf_op jit(solution)/shard_map/ppermute | solution.py:384
  16.5 0.3 ask.1.q_ref
  16.9 0.8 %biases.1.bias_ref = f32[32,128]{1,0:T(8,128)S(1)} custom-call(s32[2,8]{1,0:T(2,128)S(1)} %bitcast.3, s32[2]{0:T(128)S(1)} %copy-done.5, bf16[256,1024]{1,0:T(8,128)(2,1)S(1)} %get-tuple-element.18.after_ref.x_ref.refs_2_), custom_call_target="tpu_custom_call" | custom-call | flops 1000 | bytes 1000 | tf_op jit(solution)/shard_map/biases/pallas_call | solution.py:96
  17.6 1.1 %collective-permute-done.refs_1_.a_ref = bf16[512,256]{1,0:T(8,128)(2,1)S(1)} collective-permute-done((bf16[512,256]{1,0:T(8,128)(2,1)S(1)}, bf16[512,256]{1,0:T(8,128)(2,1)S(1)}, u32[]{:S(2)}, u32[]{:S(2)}) %collective-permute-start) | collective-permute-done | bytes 262176 | tf_op jit(solution)/shard_map/ppermute | solution.py:382
  18.7 0.2 collective-permute-done.1.refs_2_.b_ref
  18.9 1.5 %attend.3 = (f32[512,128]{1,0:T(8,128)S(1)}, f32[4,512]{1,0:T(4,128)S(1)}) custom-call(f32[32,128]{1,0:T(8,128)S(1)} %biases.1.bias_ref, bf16[256,256]{1,0:T(8,128)(2,1)S(1)} %ask.1.q_ref, bf16[512,256]{1,0:T(8,128)(2,1)S(1)} %get-tuple-element.19.refs_0_, bf16[512,256]{1,0:T(8,128)(2,1)S(1)} %collective-permute-done.refs_1_.a_ref, ...), custom_call_target="tpu_custom_call" | custom-call | flops 1000 | bytes 1000 | tf_op jit(solution)/shard_map/attend/pallas_call | solution.py:224
  20.4 3.2 %collective-permute-done.3.refs_1_.refs_2_ = bf16[512,256]{1,0:T(8,128)(2,1)S(1)} collective-permute-done((bf16[512,256]{1,0:T(8,128)(2,1)S(1)}, bf16[512,256]{1,0:T(8,128)(2,1)S(1)}, u32[]{:S(2)}, u32[]{:S(2)}) %collective-permute-start.3) | collective-permute-done | bytes 262176 | tf_op jit(solution)/shard_map/ppermute | solution.py:384
  23.6 0.1 collective-permute-start.4
  23.7 2.7 %collective-permute-done.7.refs_5_.refs_1_.w32 = bf16[256,1024]{1,0:T(8,128)(2,1)S(1)} collective-permute-done((bf16[256,1024]{1,0:T(8,128)(2,1)S(1)}, bf16[256,1024]{1,0:T(8,128)(2,1)S(1)}, u32[]{:S(2)}, u32[]{:S(2)}) %collective-permute-start.7) | collective-permute-done | bytes 524320 | tf_op jit(solution)/shard_map/ppermute | solution.py:386
  26.5 1.5 %attend.4 = (f32[512,128]{1,0:T(8,128)S(1)}, f32[4,512]{1,0:T(4,128)S(1)}) custom-call(f32[32,128]{1,0:T(8,128)S(1)} %biases.1.bias_ref, bf16[256,256]{1,0:T(8,128)(2,1)S(1)} %ask.1.q_ref, bf16[512,256]{1,0:T(8,128)(2,1)S(1)} %collective-permute-done.5.refs_0_, bf16[512,256]{1,0:T(8,128)(2,1)S(1)} %collective-permute-done.2.refs_0_.refs_1_, ...), custom_call_target="tpu_custom_call" | custom-call | flops 1000 | bytes 1000 | tf_op jit(solution)/shard_map/attend/pallas_call | solution.py:224
  28.0 1.1 %attend.5.refs_2_.a0 = bf16[256,256]{1,0:T(8,128)(2,1)S(1)} custom-call(f32[32,128]{1,0:T(8,128)S(1)} %biases.1.bias_ref, bf16[256,256]{1,0:T(8,128)(2,1)S(1)} %ask.1.q_ref, bf16[512,256]{1,0:T(8,128)(2,1)S(1)} %collective-permute-done.4.refs_0_, f32[512,128]{1,0:T(8,128)S(1)} %get-tuple-element.23.refs_1_, f32[4,512]{1,0:T(4,128)S(1)} %get-tuple-element.24.refs_2_), custom_call_target="tpu_custom_call" | custom-call | flops 1000 | bytes 1000 | tf_op jit(solution)/shard_map/attend/pallas_call | solution.py:224
  29.1 0.1 collective-permute-start.11
  29.2 2.2 %collective-permute-start.10 = (bf16[256,256]{1,0:T(8,128)(2,1)S(1)}, bf16[256,256]{1,0:T(8,128)(2,1)S(1)}, u32[]{:S(2)}, u32[]{:S(2)}) collective-permute-start(bf16[256,256]{1,0:T(8,128)(2,1)S(1)} %attend.5.refs_2_.a0), channel_id=1, source_target_pairs={{0,6},{2,4},{4,2},{6,0},{1,7},{3,5},{5,3},{7,1},{8,14},{10,12},{12... | collective-permute-start | bytes 393224 | tf_op jit(solution)/shard_map/ppermute | solution.py:396
  31.4 2.6 %collective-permute-start.9 = (bf16[256,256]{1,0:T(8,128)(2,1)S(1)}, bf16[256,256]{1,0:T(8,128)(2,1)S(1)}, u32[]{:S(2)}, u32[]{:S(2)}) collective-permute-start(bf16[256,256]{1,0:T(8,128)(2,1)S(1)} %attend.5.refs_2_.a0), channel_id=1, source_target_pairs={{0,4},{2,6},{4,0},{6,2},{1,5},{3,7},{5,1},{7,3},{8,12},{10,14},{12... | collective-permute-start | bytes 393224 | tf_op jit(solution)/shard_map/ppermute | solution.py:396
  34.0 2.3 %collective-permute-done.10.a3 = bf16[256,256]{1,0:T(8,128)(2,1)S(1)} collective-permute-done((bf16[256,256]{1,0:T(8,128)(2,1)S(1)}, bf16[256,256]{1,0:T(8,128)(2,1)S(1)}, u32[]{:S(2)}, u32[]{:S(2)}) %collective-permute-start.10) | collective-permute-done | bytes 131104 | tf_op jit(solution)/shard_map/ppermute | solution.py:396
  36.4 1.4 %collective-permute-done.8.a1 = bf16[256,256]{1,0:T(8,128)(2,1)S(1)} collective-permute-done((bf16[256,256]{1,0:T(8,128)(2,1)S(1)}, bf16[256,256]{1,0:T(8,128)(2,1)S(1)}, u32[]{:S(2)}, u32[]{:S(2)}) %collective-permute-start.8) | collective-permute-done | bytes 131104 | tf_op jit(solution)/shard_map/ppermute | solution.py:396
  37.8 2.6 %collective-permute-done.9.a2 = bf16[256,256]{1,0:T(8,128)(2,1)S(1)} collective-permute-done((bf16[256,256]{1,0:T(8,128)(2,1)S(1)}, bf16[256,256]{1,0:T(8,128)(2,1)S(1)}, u32[]{:S(2)}, u32[]{:S(2)}) %collective-permute-start.9) | collective-permute-done | bytes 131104 | tf_op jit(solution)/shard_map/ppermute | solution.py:396
  40.4 2.2 %feed.1 = (f32[64,1024]{1,0:T(8,128)S(1)}, bf16[64,1024]{1,0:T(8,128)(2,1)S(1)}, bf16[64,1024]{1,0:T(8,128)(2,1)S(1)}, bf16[64,1024]{1,0:T(8,128)(2,1)S(1)}) custom-call(bf16[256,1024]{1,0:T(8,128)(2,1)S(1)} %get-tuple-element.18.after_ref.x_ref.refs_2_, bf16[256,256]{1,0:T(8,128)(2,1)S(1)} %attend.5.refs_2_.a0, ...), custom_call_target="tpu_custom_call" | custom-call | flops 1000 | bytes 1000 | tf_op jit(solution)/shard_map/feed/pallas_call | solution.py:315
  42.6 0.1 collective-permute-start.12
  42.7 3.5 %collective-permute-start.13 = (bf16[64,1024]{1,0:T(8,128)(2,1)S(1)}, bf16[64,1024]{1,0:T(8,128)(2,1)S(1)}, u32[]{:S(2)}, u32[]{:S(2)}) collective-permute-start(bf16[64,1024]{1,0:T(8,128)(2,1)S(1)} %get-tuple-element.27), channel_id=1, source_target_pairs={{0,4},{2,6},{4,0},{6,2},{1,5},{3,7},{5,1},{7,3},{8,12},{10,14},{12... | collective-permute-start | bytes 393224 | tf_op jit(solution)/shard_map/ppermute | solution.py:398
  46.2 1.1 %collective-permute-start.14 = (bf16[64,1024]{1,0:T(8,128)(2,1)S(1)}, bf16[64,1024]{1,0:T(8,128)(2,1)S(1)}, u32[]{:S(2)}, u32[]{:S(2)}) collective-permute-start(bf16[64,1024]{1,0:T(8,128)(2,1)S(1)} %get-tuple-element.28), channel_id=1, source_target_pairs={{0,6},{2,4},{4,2},{6,0},{1,7},{3,5},{5,3},{7,1},{8,14},{10,12},{12... | collective-permute-start | bytes 393224 | tf_op jit(solution)/shard_map/ppermute | solution.py:398
  47.4 1.4 %collective-permute-done.12.r1 = bf16[64,1024]{1,0:T(8,128)(2,1)S(1)} collective-permute-done((bf16[64,1024]{1,0:T(8,128)(2,1)S(1)}, bf16[64,1024]{1,0:T(8,128)(2,1)S(1)}, u32[]{:S(2)}, u32[]{:S(2)}) %collective-permute-start.12) | collective-permute-done | bytes 131104 | tf_op jit(solution)/shard_map/ppermute | solution.py:398
  48.8 3.0 %collective-permute-done.13.r2 = bf16[64,1024]{1,0:T(8,128)(2,1)S(1)} collective-permute-done((bf16[64,1024]{1,0:T(8,128)(2,1)S(1)}, bf16[64,1024]{1,0:T(8,128)(2,1)S(1)}, u32[]{:S(2)}, u32[]{:S(2)}) %collective-permute-start.13) | collective-permute-done | bytes 131104 | tf_op jit(solution)/shard_map/ppermute | solution.py:398
  51.8 1.8 %collective-permute-done.14.r3 = bf16[64,1024]{1,0:T(8,128)(2,1)S(1)} collective-permute-done((bf16[64,1024]{1,0:T(8,128)(2,1)S(1)}, bf16[64,1024]{1,0:T(8,128)(2,1)S(1)}, u32[]{:S(2)}, u32[]{:S(2)}) %collective-permute-start.14) | collective-permute-done | bytes 131104 | tf_op jit(solution)/shard_map/ppermute | solution.py:398
  53.7 6.0 %collective-permute-start.15 = (bf16[32,1024]{1,0:T(8,128)(2,1)S(1)}, bf16[32,1024]{1,0:T(8,128)(2,1)S(1)}, u32[]{:S(2)}, u32[]{:S(2)}) collective-permute-start(bf16[32,1024]{1,0:T(8,128)(2,1)S(1)} %get-tuple-element.30), channel_id=1, source_target_pairs={{0,1},{1,0},{2,3},{3,2},{4,5},{5,4},{6,7},{7,6},{8,9},{9,8},{10,11... | collective-permute-start | bytes 196616 | tf_op jit(solution)/shard_map/ppermute | solution.py:400
  60.3 1.7 %collective-permute-done.15.other_ref = bf16[32,1024]{1,0:T(8,128)(2,1)S(1)} collective-permute-done((bf16[32,1024]{1,0:T(8,128)(2,1)S(1)}, bf16[32,1024]{1,0:T(8,128)(2,1)S(1)}, u32[]{:S(2)}, u32[]{:S(2)}) %collective-permute-start.15) | collective-permute-done | bytes 65568 | tf_op jit(solution)/shard_map/ppermute | solution.py:400
  62.0 0.7 %guide.1 = bf16[32,1024]{1,0:T(8,128)(2,1)} custom-call(f32[1]{0:T(128)S(6)} %copy.11.guidance_ref, f32[32,1024]{1,0:T(8,128)S(1)} %get-tuple-element.29.kept_ref, bf16[32,1024]{1,0:T(8,128)(2,1)S(1)} %collective-permute-done.15.other_ref), custom_call_target="tpu_custom_call" | custom-call | flops 1000 | bytes 1000 | tf_op jit(solution)/shard_map/guide/pallas_call | solution.py:364
  (24 shorter events, 0.2 us)
Async XLA Ops:
  0.0 16.5 %copy-start.3 = (bf16[1024,256]{1,0:T(8,128)(2,1)S(1)}, bf16[1024,256]{1,0:T(8,128)(2,1)}, u32[]{:S(2)}) copy-start(bf16[1024,256]{1,0:T(8,128)(2,1)} %wq_ref.1) | copy-start | bytes 1572868
  2.2 14.6 %copy-start.4 = (s32[8,2]{0,1:T(2,128)S(1)}, s32[8,2]{0,1:T(2,128)}, u32[]{:S(2)}) copy-start(s32[8,2]{0,1:T(2,128)} %param.11) | copy-start | bytes 196
  2.2 14.6 %copy-start.5 = (s32[2]{0:T(128)S(1)}, s32[2]{0:T(128)}, u32[]{:S(2)}) copy-start(s32[2]{0:T(128)} %counts_ref.1) | copy-start | bytes 28
  2.2 10.3 %collective-permute-start.6 = (bf16[128,1024]{1,0:T(8,128)(2,1)S(1)}, bf16[128,1024]{1,0:T(8,128)(2,1)S(1)}, u32[]{:S(2)}, u32[]{:S(2)}) collective-permute-start(bf16[128,1024]{1,0:T(8,128)(2,1)S(1)} %get-tuple-element.22.refs_0_), channel_id=1, source_target_pairs={{0,2},{2,0},{4,6},{6,4},{1,3},{3,1},{5,7},{7,5},{8,10},{10,8},{12,... | collective-permute-start | bytes 786440 | tf_op jit(solution)/shard_map/ppermute | solution.py:385
  3.8 11.0 %collective-permute-start.2 = (bf16[512,256]{1,0:T(8,128)(2,1)S(1)}, bf16[512,256]{1,0:T(8,128)(2,1)S(1)}, u32[]{:S(2)}, u32[]{:S(2)}) collective-permute-start(bf16[512,256]{1,0:T(8,128)(2,1)S(1)} %get-tuple-element.19.refs_0_), channel_id=1, source_target_pairs={{0,32},{8,40},{16,48},{24,56},{32,0},{40,8},{48,16},{56,24},{64,96... | collective-permute-start | bytes 786440 | tf_op jit(solution)/shard_map/ppermute | solution.py:383
  6.1 12.6 %collective-permute-start = (bf16[512,256]{1,0:T(8,128)(2,1)S(1)}, bf16[512,256]{1,0:T(8,128)(2,1)S(1)}, u32[]{:S(2)}, u32[]{:S(2)}) collective-permute-start(bf16[512,256]{1,0:T(8,128)(2,1)S(1)} %get-tuple-element.19.refs_0_), channel_id=1, source_target_pairs={{16,32},{32,16},{24,40},{40,24},{48,64},{64,48},{56,72},{72,56},{8... | collective-permute-start | bytes 786440 | tf_op jit(solution)/shard_map/ppermute | solution.py:382
  6.1 12.7 %collective-permute-start.1 = (bf16[512,256]{1,0:T(8,128)(2,1)S(1)}, bf16[512,256]{1,0:T(8,128)(2,1)S(1)}, u32[]{:S(2)}, u32[]{:S(2)}) collective-permute-start(bf16[512,256]{1,0:T(8,128)(2,1)S(1)} %get-tuple-element.19.refs_0_), channel_id=1, source_target_pairs={{0,16},{16,0},{8,24},{24,8},{32,48},{48,32},{40,56},{56,40},{64,80... | collective-permute-start | bytes 786440 | tf_op jit(solution)/shard_map/ppermute | solution.py:382
  12.6 13.8 %collective-permute-start.7 = (bf16[256,1024]{1,0:T(8,128)(2,1)S(1)}, bf16[256,1024]{1,0:T(8,128)(2,1)S(1)}, u32[]{:S(2)}, u32[]{:S(2)}) collective-permute-start(bf16[256,1024]{1,0:T(8,128)(2,1)S(1)} %stack.2), channel_id=1, source_target_pairs={{0,6},{2,4},{4,2},{6,0},{1,7},{3,5},{5,3},{7,1},{8,14},{10,12},{12... | collective-permute-start | bytes 1572872 | tf_op jit(solution)/shard_map/ppermute | solution.py:386
  14.8 8.8 %collective-permute-start.3 = (bf16[512,256]{1,0:T(8,128)(2,1)S(1)}, bf16[512,256]{1,0:T(8,128)(2,1)S(1)}, u32[]{:S(2)}, u32[]{:S(2)}) collective-permute-start(bf16[512,256]{1,0:T(8,128)(2,1)S(1)} %collective-permute-done.2.refs_0_.refs_1_), channel_id=1, source_target_pairs={{0,64},{8,72},{16,80},{24,88},{32,224},{40,232},{48,240},{56,248},... | collective-permute-start | bytes 786440 | tf_op jit(solution)/shard_map/ppermute | solution.py:384
  16.5 7.2 %collective-permute-start.5 = (bf16[512,256]{1,0:T(8,128)(2,1)S(1)}, bf16[512,256]{1,0:T(8,128)(2,1)S(1)}, u32[]{:S(2)}, u32[]{:S(2)}) collective-permute-start(bf16[512,256]{1,0:T(8,128)(2,1)S(1)} %get-tuple-element.19.refs_0_), channel_id=1, source_target_pairs={{0,8},{8,0},{16,24},{24,16},{32,40},{40,32},{48,56},{56,48},{64,72... | collective-permute-start | bytes 786440 | tf_op jit(solution)/shard_map/ppermute | solution.py:391
  23.6 16.8 %copy-start.2 = (bf16[1024,1024]{1,0:T(8,128)(2,1)S(1)}, bf16[1024,1024]{1,0:T(8,128)(2,1)}, u32[]{:S(2)}) copy-start(bf16[1024,1024]{1,0:T(8,128)(2,1)} %wback_ref.1) | copy-start | bytes 6291460
  23.6 4.4 %collective-permute-start.4 = (bf16[512,256]{1,0:T(8,128)(2,1)S(1)}, bf16[512,256]{1,0:T(8,128)(2,1)S(1)}, u32[]{:S(2)}, u32[]{:S(2)}) collective-permute-start(bf16[512,256]{1,0:T(8,128)(2,1)S(1)} %pick.1), channel_id=1, source_target_pairs={{0,8},{8,0},{16,24},{24,16},{32,40},{40,32},{48,56},{56,48},{64,72... | collective-permute-start | bytes 786440 | tf_op jit(solution)/shard_map/ppermute | solution.py:391
  26.5 13.9 %copy-start = (bf16[256,1024]{1,0:T(8,128)(2,1)S(1)}, bf16[256,1024]{1,0:T(8,128)(2,1)}, u32[]{:S(2)}) copy-start(bf16[256,1024]{1,0:T(8,128)(2,1)} %o0.1) | copy-start | bytes 1572868
  26.5 13.9 %copy-start.1 = (bf16[1024,1024]{1,0:T(8,128)(2,1)S(1)}, bf16[1024,1024]{1,0:T(8,128)(2,1)}, u32[]{:S(2)}) copy-start(bf16[1024,1024]{1,0:T(8,128)(2,1)} %win_ref.1) | copy-start | bytes 6291460
  29.1 11.2 %collective-permute-start.11 = (bf16[384,1024]{1,0:T(8,128)(2,1)S(1)}, bf16[384,1024]{1,0:T(8,128)(2,1)S(1)}, u32[]{:S(2)}, u32[]{:S(2)}) collective-permute-start(bf16[384,1024]{1,0:T(8,128)(2,1)S(1)} %stack.3), channel_id=1, source_target_pairs={{0,8},{8,0},{16,24},{24,16},{32,40},{40,32},{48,56},{56,48},{64,72... | collective-permute-start | bytes 2359304 | tf_op jit(solution)/shard_map/ppermute | solution.py:394
  29.2 7.1 %collective-permute-start.10 = (bf16[256,256]{1,0:T(8,128)(2,1)S(1)}, bf16[256,256]{1,0:T(8,128)(2,1)S(1)}, u32[]{:S(2)}, u32[]{:S(2)}) collective-permute-start(bf16[256,256]{1,0:T(8,128)(2,1)S(1)} %attend.5.refs_2_.a0), channel_id=1, source_target_pairs={{0,6},{2,4},{4,2},{6,0},{1,7},{3,5},{5,3},{7,1},{8,14},{10,12},{12... | collective-permute-start | bytes 393224 | tf_op jit(solution)/shard_map/ppermute | solution.py:396
  31.4 6.3 %collective-permute-start.8 = (bf16[256,256]{1,0:T(8,128)(2,1)S(1)}, bf16[256,256]{1,0:T(8,128)(2,1)S(1)}, u32[]{:S(2)}, u32[]{:S(2)}) collective-permute-start(bf16[256,256]{1,0:T(8,128)(2,1)S(1)} %attend.5.refs_2_.a0), channel_id=1, source_target_pairs={{0,2},{2,0},{4,6},{6,4},{1,3},{3,1},{5,7},{7,5},{8,10},{10,8},{12,... | collective-permute-start | bytes 393224 | tf_op jit(solution)/shard_map/ppermute | solution.py:396
  31.4 8.9 %collective-permute-start.9 = (bf16[256,256]{1,0:T(8,128)(2,1)S(1)}, bf16[256,256]{1,0:T(8,128)(2,1)S(1)}, u32[]{:S(2)}, u32[]{:S(2)}) collective-permute-start(bf16[256,256]{1,0:T(8,128)(2,1)S(1)} %attend.5.refs_2_.a0), channel_id=1, source_target_pairs={{0,4},{2,6},{4,0},{6,2},{1,5},{3,7},{5,1},{7,3},{8,12},{10,14},{12... | collective-permute-start | bytes 393224 | tf_op jit(solution)/shard_map/ppermute | solution.py:396
  42.6 6.2 %collective-permute-start.12 = (bf16[64,1024]{1,0:T(8,128)(2,1)S(1)}, bf16[64,1024]{1,0:T(8,128)(2,1)S(1)}, u32[]{:S(2)}, u32[]{:S(2)}) collective-permute-start(bf16[64,1024]{1,0:T(8,128)(2,1)S(1)} %get-tuple-element.26), channel_id=1, source_target_pairs={{0,2},{2,0},{4,6},{6,4},{1,3},{3,1},{5,7},{7,5},{8,10},{10,8},{12,... | collective-permute-start | bytes 393224 | tf_op jit(solution)/shard_map/ppermute | solution.py:398
  42.7 9.1 %collective-permute-start.13 = (bf16[64,1024]{1,0:T(8,128)(2,1)S(1)}, bf16[64,1024]{1,0:T(8,128)(2,1)S(1)}, u32[]{:S(2)}, u32[]{:S(2)}) collective-permute-start(bf16[64,1024]{1,0:T(8,128)(2,1)S(1)} %get-tuple-element.27), channel_id=1, source_target_pairs={{0,4},{2,6},{4,0},{6,2},{1,5},{3,7},{5,1},{7,3},{8,12},{10,14},{12... | collective-permute-start | bytes 393224 | tf_op jit(solution)/shard_map/ppermute | solution.py:398
  46.2 7.4 %collective-permute-start.14 = (bf16[64,1024]{1,0:T(8,128)(2,1)S(1)}, bf16[64,1024]{1,0:T(8,128)(2,1)S(1)}, u32[]{:S(2)}, u32[]{:S(2)}) collective-permute-start(bf16[64,1024]{1,0:T(8,128)(2,1)S(1)} %get-tuple-element.28), channel_id=1, source_target_pairs={{0,6},{2,4},{4,2},{6,0},{1,7},{3,5},{5,3},{7,1},{8,14},{10,12},{12... | collective-permute-start | bytes 393224 | tf_op jit(solution)/shard_map/ppermute | solution.py:398
  53.7 8.4 %collective-permute-start.15 = (bf16[32,1024]{1,0:T(8,128)(2,1)S(1)}, bf16[32,1024]{1,0:T(8,128)(2,1)S(1)}, u32[]{:S(2)}, u32[]{:S(2)}) collective-permute-start(bf16[32,1024]{1,0:T(8,128)(2,1)S(1)} %get-tuple-element.30), channel_id=1, source_target_pairs={{0,1},{1,0},{2,3},{3,2},{4,5},{5,4},{6,7},{7,6},{8,9},{9,8},{10,11... | collective-permute-start | bytes 196616 | tf_op jit(solution)/shard_map/ppermute | solution.py:400

commit v5 on v4

--- a/solution.py
+++ b/solution.py
@@ -278,29 +278,51 @@
     )(*pieces, after)
 
 
-def feed_kernel(x_ref, a0, a1, a2, a3, o0, w1, w32, pair, win_ref, wback_ref, own_ref, r1, r2, r3):
+def turned(ref, tok, columns=slice(None)):
     head = lax.axis_index("head")
+    part = tok // 4
+    pieces = []
+    for j in range(4):
+        for view in range(2):
+            start = pl.multiple_of(view * tok + jnp.bitwise_xor(head, j) * part, part)
+            pieces.append(ref[pl.ds(start, part), columns])
+    return jnp.concatenate(pieces, axis=0)
+
+
+def lay_kernel(a0, a1, a2, a3, out_ref):
+    tok = a0.shape[0] // 2
+    block = a0.shape[1]
+    half = block // 2
+    core = lax.axis_index("view") & 1
+    out_ref[:, :block] = turned(a0, tok)
+    for i, a in enumerate((a1, a3, a2)):
+        for k, which in enumerate((core, 1 - core)):
+            at = block * (i + 1) + half * k
+            out_ref[:, at : at + half] = turned(a, tok, pl.ds(pl.multiple_of(which * half, half), half))
+
+
+def lay(*pieces):
+    rows, columns = pieces[0].shape
+    return pl.pallas_call(
+        lay_kernel,
+        out_shape=held((rows, 4 * columns), pieces[0].dtype),
+        in_specs=[VMEM] * 4,
+        out_specs=VMEM,
+        compiler_params=params(4),
+        cost_estimate=pl.CostEstimate(flops=20_000_000_000, bytes_accessed=1000, transcendentals=0),
+        name="lay",
+    )(*pieces)
+
+
+def feed_kernel(x_ref, left_ref, o0, w1, w32, pair, win_ref, wback_ref, own_ref, r1, r2, r3):
     rows, width = x_ref.shape
     tok = rows // 2
     part = tok // 4
-
-    def turned(ref, columns=slice(None)):
-        pieces = []
-        for j in range(4):
-            for view in range(2):
-                start = pl.multiple_of(view * tok + jnp.bitwise_xor(head, j) * part, part)
-                pieces.append(ref[pl.ds(start, part), columns])
-        return jnp.concatenate(pieces, axis=0)
-
     half = w1.shape[0]
-    core = lax.axis_index("view") & 1
-    mine = pl.ds(pl.multiple_of(core * half, half), half)
-    theirs = pl.ds(pl.multiple_of((1 - core) * half, half), half)
-    left = jnp.concatenate([turned(a, rows) for a in (a1, a3, a2) for rows in (mine, theirs)], axis=1)
-    own = (w1[...], w32[:half], w32[half:])
-    right = [r for i, w in enumerate(own) for r in (w, pair[i * half : (i + 1) * half])]
-    attention = dot(turned(a0), o0[...]) + dot(left, jnp.concatenate(right, axis=0))
-    y = turned(x_ref).astype(jnp.float32) + attention
+    blocks = (w1[...], w32[:half], w32[half:])
+    right = [o0[...]] + [r for i, w in enumerate(blocks) for r in (w, pair[i * half : (i + 1) * half])]
+    attention = dot(left_ref[...], jnp.concatenate(right, axis=0))
+    y = turned(x_ref, tok).astype(jnp.float32) + attention
     normed = (y * lax.rsqrt(jnp.mean(y * y, axis=-1, keepdims=True) + 1e-06)).astype(jnp.bfloat16)
     hidden = jax.nn.gelu(dot(normed, win_ref[...])).astype(jnp.bfloat16)
     update = dot(hidden, wback_ref[...])
@@ -309,18 +331,18 @@
         ref[...] = update[2 * part * j : 2 * part * (j + 1)].astype(jnp.bfloat16)
 
 
-def feed(x, attended, w_outs, w_in, w_back):
+def feed(x, left, w_outs, w_in, w_back):
     rows, width = x.shape
     piece = held((rows // 4, width), jnp.bfloat16)
     return pl.pallas_call(
         feed_kernel,
         out_shape=(held((rows // 4, width), jnp.float32), piece, piece, piece),
-        in_specs=[VMEM] * 11,
+        in_specs=[VMEM] * 8,
         out_specs=(VMEM,) * 4,
         compiler_params=params(16),
         cost_estimate=COST,
         name="feed",
-    )(x, *attended, *w_outs, w_in, w_back)
+    )(x, left, *w_outs, w_in, w_back)
 
 
 def gather_kernel(own_ref, r1, r2, r3, kept_ref, sent_ref):
@@ -394,7 +416,7 @@
     w_pair = other_core(stack(w_1, w_32, after=attended))
 
     pieces = [attended] + [flipped("head", 4, j)(attended) for j in (1, 2, 3)]
-    own, *outgoing = feed(x, pieces, (w_out, w_1, w_32, w_pair), w_in, w_back)
+    own, *outgoing = feed(x, lay(*pieces), (w_out, w_1, w_32, w_pair), w_in, w_back)
     received = [flipped("head", 4, j)(r) for j, r in zip((1, 2, 3), outgoing)]
     kept, sent = gather(own, received)
     other = flipped("branch", 2, 1)(sent)

time: 62.8 us -> 61.9 us (0.986)
  the two profiles are of different devices: /device:TPU:8 before, /device:TPU:1 now
where the time goes in v5:
time: 61.9 us; the launch traced here: 61.8 us
  starting transfers between devices  31.8 us (51%)
  waiting for transfers between devices  18.7 us (30%)
  Pallas kernels  10.5 us (17%)
  between operations  0.85 us (1%)
    ppermute x3, waiting for transfers between devices, on_device(): received = [flipped('head', 4, j)(r) for j, r in zip((1, 2, 3), outgoing)]  6.87 us
    ppermute x2, starting transfers between devices, on_device(): other, cross = (other_core(kv), other_core(pick(*near, *far, state[1])))  5.81 us
    ppermute x3, waiting for transfers between devices, on_device(): pieces = [attended] + [flipped('head', 4, j)(attended) for j in (1, 2, 3)]  4.88 us
    ppermute x2, starting transfers between devices, on_device(): near = [matched(count, 2, parity)(kv) for parity in (1, 0)]  4.84 us
    ppermute x1, starting transfers between devices, on_device(): other = flipped('branch', 2, 1)(sent)  4.52 us
    pallas_call x3, Pallas kernels, attend(): pl.pallas_call(functools.partial(attend_kernel, blocks, first, last), out...  4.11 us
    ppermute x1, waiting for transfers between devices, on_device(): far = (across, onward(count)(across))  4.1 us
    ppermute x3, starting transfers between devices, on_device(): pieces = [attended] + [flipped('head', 4, j)(attended) for j in (1, 2, 3)]  3.95 us
  transfers between devices with their start and end apart: 16, of which 8 were waited for; matrix products, arithmetic and copies ran while one was open for 0% of the time, Pallas kernels for 7%

profile of v5, /device:TPU:1, one launch (start us, length us, event | category | flops | bytes accessed | tf_op | source)
XLA Modules:
  0.0 61.8 jit_solution(4941394912082169995)
XLA Ops:
  0.0 2.2 %project.1 = (bf16[256,1024]{1,0:T(8,128)(2,1)S(1)}, bf16[512,256]{1,0:T(8,128)(2,1)S(1)}, bf16[128,1024]{1,0:T(8,128)(2,1)S(1)}) custom-call(bf16[256,1024]{1,0:T(8,128)(2,1)} %bitcast.4, bf16[1024,256]{1,0:T(8,128)(2,1)} %wk_hbm.1, bf16[1024,256]{1,0:T(8,128)(2,1)} %wv_hbm.1, bf16[256,1024]{1,0:T(8,128)(2,1)} %o0.1), custom_call_target="tpu_custom_call" | custom-call | flops 1000 | bytes 1000 | tf_op jit(solution)/shard_map/project/pallas_call | solution.py:126
  2.2 2.1 %collective-permute-start.6 = (bf16[128,1024]{1,0:T(8,128)(2,1)S(1)}, bf16[128,1024]{1,0:T(8,128)(2,1)S(1)}, u32[]{:S(2)}, u32[]{:S(2)}) collective-permute-start(bf16[128,1024]{1,0:T(8,128)(2,1)S(1)} %get-tuple-element.22.refs_0_), channel_id=1, source_target_pairs={{0,2},{2,0},{4,6},{6,4},{1,3},{3,1},{5,7},{7,5},{8,10},{10,8},{12,... | collective-permute-start | bytes 786440 | tf_op jit(solution)/shard_map/ppermute | solution.py:407
  4.4 2.9 %collective-permute-start.2 = (bf16[512,256]{1,0:T(8,128)(2,1)S(1)}, bf16[512,256]{1,0:T(8,128)(2,1)S(1)}, u32[]{:S(2)}, u32[]{:S(2)}) collective-permute-start(bf16[512,256]{1,0:T(8,128)(2,1)S(1)} %get-tuple-element.19.refs_0_), channel_id=1, source_target_pairs={{0,32},{8,40},{16,48},{24,56},{32,0},{40,8},{48,16},{56,24},{64,96... | collective-permute-start | bytes 786440 | tf_op jit(solution)/shard_map/ppermute | solution.py:405
  7.3 4.8 %collective-permute-start = (bf16[512,256]{1,0:T(8,128)(2,1)S(1)}, bf16[512,256]{1,0:T(8,128)(2,1)S(1)}, u32[]{:S(2)}, u32[]{:S(2)}) collective-permute-start(bf16[512,256]{1,0:T(8,128)(2,1)S(1)} %get-tuple-element.19.refs_0_), channel_id=1, source_target_pairs={{16,32},{32,16},{24,40},{40,24},{48,64},{64,48},{56,72},{72,56},{8... | collective-permute-start | bytes 786440 | tf_op jit(solution)/shard_map/ppermute | solution.py:404
  12.2 1.9 %collective-permute-start.7 = (bf16[256,1024]{1,0:T(8,128)(2,1)S(1)}, bf16[256,1024]{1,0:T(8,128)(2,1)S(1)}, u32[]{:S(2)}, u32[]{:S(2)}) collective-permute-start(bf16[256,1024]{1,0:T(8,128)(2,1)S(1)} %stack.2), channel_id=1, source_target_pairs={{0,6},{2,4},{4,2},{6,0},{1,7},{3,5},{5,3},{7,1},{8,14},{10,12},{12... | collective-permute-start | bytes 1572872 | tf_op jit(solution)/shard_map/ppermute | solution.py:408
  14.1 0.6 %collective-permute-start.3 = (bf16[512,256]{1,0:T(8,128)(2,1)S(1)}, bf16[512,256]{1,0:T(8,128)(2,1)S(1)}, u32[]{:S(2)}, u32[]{:S(2)}) collective-permute-start(bf16[512,256]{1,0:T(8,128)(2,1)S(1)} %collective-permute-done.2.refs_0_.refs_1_), channel_id=1, source_target_pairs={{0,64},{8,72},{16,80},{24,88},{32,224},{40,232},{48,240},{56,248},... | collective-permute-start | bytes 786440 | tf_op jit(solution)/shard_map/ppermute | solution.py:406
  14.7 3.9 %collective-permute-start.5 = (bf16[512,256]{1,0:T(8,128)(2,1)S(1)}, bf16[512,256]{1,0:T(8,128)(2,1)S(1)}, u32[]{:S(2)}, u32[]{:S(2)}) collective-permute-start(bf16[512,256]{1,0:T(8,128)(2,1)S(1)} %get-tuple-element.19.refs_0_), channel_id=1, source_target_pairs={{0,8},{8,0},{16,24},{24,16},{32,40},{40,32},{48,56},{56,48},{64,72... | collective-permute-start | bytes 786440 | tf_op jit(solution)/shard_map/ppermute | solution.py:413
  18.6 0.3 ask.1.q_ref
  18.9 0.8 %biases.1.bias_ref = f32[32,128]{1,0:T(8,128)S(1)} custom-call(s32[2,8]{1,0:T(2,128)S(1)} %bitcast.3, s32[2]{0:T(128)S(1)} %copy-done.5, bf16[256,1024]{1,0:T(8,128)(2,1)S(1)} %get-tuple-element.18.after_ref.x_ref.refs_2_), custom_call_target="tpu_custom_call" | custom-call | flops 1000 | bytes 1000 | tf_op jit(solution)/shard_map/biases/pallas_call | solution.py:96
  19.7 0.9 %collective-permute-done.1.refs_2_.b_ref = bf16[512,256]{1,0:T(8,128)(2,1)S(1)} collective-permute-done((bf16[512,256]{1,0:T(8,128)(2,1)S(1)}, bf16[512,256]{1,0:T(8,128)(2,1)S(1)}, u32[]{:S(2)}, u32[]{:S(2)}) %collective-permute-start.1) | collective-permute-done | bytes 262176 | tf_op jit(solution)/shard_map/ppermute | solution.py:404
  20.6 1.5 %attend.3 = (f32[512,128]{1,0:T(8,128)S(1)}, f32[4,512]{1,0:T(4,128)S(1)}) custom-call(f32[32,128]{1,0:T(8,128)S(1)} %biases.1.bias_ref, bf16[256,256]{1,0:T(8,128)(2,1)S(1)} %ask.1.q_ref, bf16[512,256]{1,0:T(8,128)(2,1)S(1)} %get-tuple-element.19.refs_0_, bf16[512,256]{1,0:T(8,128)(2,1)S(1)} %collective-permute-done.refs_1_.a_ref, ...), custom_call_target="tpu_custom_call" | custom-call | flops 1000 | bytes 1000 | tf_op jit(solution)/shard_map/attend/pallas_call | solution.py:224
  22.1 4.1 %collective-permute-done.3.refs_1_.refs_2_ = bf16[512,256]{1,0:T(8,128)(2,1)S(1)} collective-permute-done((bf16[512,256]{1,0:T(8,128)(2,1)S(1)}, bf16[512,256]{1,0:T(8,128)(2,1)S(1)}, u32[]{:S(2)}, u32[]{:S(2)}) %collective-permute-start.3) | collective-permute-done | bytes 262176 | tf_op jit(solution)/shard_map/ppermute | solution.py:406
  26.2 1.9 %collective-permute-start.4 = (bf16[512,256]{1,0:T(8,128)(2,1)S(1)}, bf16[512,256]{1,0:T(8,128)(2,1)S(1)}, u32[]{:S(2)}, u32[]{:S(2)}) collective-permute-start(bf16[512,256]{1,0:T(8,128)(2,1)S(1)} %pick.1), channel_id=1, source_target_pairs={{0,8},{8,0},{16,24},{24,16},{32,40},{40,32},{48,56},{56,48},{64,72... | collective-permute-start | bytes 786440 | tf_op jit(solution)/shard_map/ppermute | solution.py:413
  28.1 1.5 %attend.4 = (f32[512,128]{1,0:T(8,128)S(1)}, f32[4,512]{1,0:T(4,128)S(1)}) custom-call(f32[32,128]{1,0:T(8,128)S(1)} %biases.1.bias_ref, bf16[256,256]{1,0:T(8,128)(2,1)S(1)} %ask.1.q_ref, bf16[512,256]{1,0:T(8,128)(2,1)S(1)} %collective-permute-done.5.refs_0_, bf16[512,256]{1,0:T(8,128)(2,1)S(1)} %collective-permute-done.2.refs_0_.refs_1_, ...), custom_call_target="tpu_custom_call" | custom-call | flops 1000 | bytes 1000 | tf_op jit(solution)/shard_map/attend/pallas_call | solution.py:224
  29.7 1.1 %attend.5.a0.refs_2_ = bf16[256,256]{1,0:T(8,128)(2,1)S(1)} custom-call(f32[32,128]{1,0:T(8,128)S(1)} %biases.1.bias_ref, bf16[256,256]{1,0:T(8,128)(2,1)S(1)} %ask.1.q_ref, bf16[512,256]{1,0:T(8,128)(2,1)S(1)} %collective-permute-done.4.refs_0_, f32[512,128]{1,0:T(8,128)S(1)} %get-tuple-element.23.refs_1_, f32[4,512]{1,0:T(4,128)S(1)} %get-tuple-element.24.refs_2_), custom_call_target="tpu_custom_call" | custom-call | flops 1000 | bytes 1000 | tf_op jit(solution)/shard_map/attend/pallas_call | solution.py:224
  30.7 1.9 %collective-permute-start.10 = (bf16[256,256]{1,0:T(8,128)(2,1)S(1)}, bf16[256,256]{1,0:T(8,128)(2,1)S(1)}, u32[]{:S(2)}, u32[]{:S(2)}) collective-permute-start(bf16[256,256]{1,0:T(8,128)(2,1)S(1)} %attend.5.a0.refs_2_), channel_id=1, source_target_pairs={{0,6},{2,4},{4,2},{6,0},{1,7},{3,5},{5,3},{7,1},{8,14},{10,12},{12... | collective-permute-start | bytes 393224 | tf_op jit(solution)/shard_map/ppermute | solution.py:418
  32.6 0.3 collective-permute-start.8
  33.0 1.7 %collective-permute-start.9 = (bf16[256,256]{1,0:T(8,128)(2,1)S(1)}, bf16[256,256]{1,0:T(8,128)(2,1)S(1)}, u32[]{:S(2)}, u32[]{:S(2)}) collective-permute-start(bf16[256,256]{1,0:T(8,128)(2,1)S(1)} %attend.5.a0.refs_2_), channel_id=1, source_target_pairs={{0,4},{2,6},{4,0},{6,2},{1,5},{3,7},{5,1},{7,3},{8,12},{10,14},{12... | collective-permute-start | bytes 393224 | tf_op jit(solution)/shard_map/ppermute | solution.py:418
  34.8 1.1 %collective-permute-start.11 = (bf16[384,1024]{1,0:T(8,128)(2,1)S(1)}, bf16[384,1024]{1,0:T(8,128)(2,1)S(1)}, u32[]{:S(2)}, u32[]{:S(2)}) collective-permute-start(bf16[384,1024]{1,0:T(8,128)(2,1)S(1)} %stack.3), channel_id=1, source_target_pairs={{0,8},{8,0},{16,24},{24,16},{32,40},{40,32},{48,56},{56,48},{64,72... | collective-permute-start | bytes 2359304 | tf_op jit(solution)/shard_map/ppermute | solution.py:416
  35.9 1.2 %collective-permute-done.10.a3 = bf16[256,256]{1,0:T(8,128)(2,1)S(1)} collective-permute-done((bf16[256,256]{1,0:T(8,128)(2,1)S(1)}, bf16[256,256]{1,0:T(8,128)(2,1)S(1)}, u32[]{:S(2)}, u32[]{:S(2)}) %collective-permute-start.10) | collective-permute-done | bytes 131104 | tf_op jit(solution)/shard_map/ppermute | solution.py:418
  37.1 0.3 collective-permute-done.8.a1
  37.4 3.4 %collective-permute-done.9.a2 = bf16[256,256]{1,0:T(8,128)(2,1)S(1)} collective-permute-done((bf16[256,256]{1,0:T(8,128)(2,1)S(1)}, bf16[256,256]{1,0:T(8,128)(2,1)S(1)}, u32[]{:S(2)}, u32[]{:S(2)}) %collective-permute-start.9) | collective-permute-done | bytes 131104 | tf_op jit(solution)/shard_map/ppermute | solution.py:418
  40.8 0.1 lay.1.left_ref
  41.0 2.2 %feed.1 = (f32[64,1024]{1,0:T(8,128)S(1)}, bf16[64,1024]{1,0:T(8,128)(2,1)S(1)}, bf16[64,1024]{1,0:T(8,128)(2,1)S(1)}, bf16[64,1024]{1,0:T(8,128)(2,1)S(1)}) custom-call(bf16[256,1024]{1,0:T(8,128)(2,1)S(1)} %get-tuple-element.18.after_ref.x_ref.refs_2_, bf16[256,1024]{1,0:T(8,128)(2,1)S(1)} %lay.1.left_ref, bf16[256,1024]{1,0:T(8,128)(2,1)S(1)} %copy-done, ...), custom_call_target="tpu_custom_call" | custom-call | flops 1000 | bytes 1000 | tf_op jit(solution)/shard_map/feed/pallas_call | solution.py:337
  43.2 0.1 collective-permute-start.12
  43.3 3.0 %collective-permute-start.13 = (bf16[64,1024]{1,0:T(8,128)(2,1)S(1)}, bf16[64,1024]{1,0:T(8,128)(2,1)S(1)}, u32[]{:S(2)}, u32[]{:S(2)}) collective-permute-start(bf16[64,1024]{1,0:T(8,128)(2,1)S(1)} %get-tuple-element.27), channel_id=1, source_target_pairs={{0,4},{2,6},{4,0},{6,2},{1,5},{3,7},{5,1},{7,3},{8,12},{10,14},{12... | collective-permute-start | bytes 393224 | tf_op jit(solution)/shard_map/ppermute | solution.py:420
  46.3 0.8 %collective-permute-start.14 = (bf16[64,1024]{1,0:T(8,128)(2,1)S(1)}, bf16[64,1024]{1,0:T(8,128)(2,1)S(1)}, u32[]{:S(2)}, u32[]{:S(2)}) collective-permute-start(bf16[64,1024]{1,0:T(8,128)(2,1)S(1)} %get-tuple-element.28), channel_id=1, source_target_pairs={{0,6},{2,4},{4,2},{6,0},{1,7},{3,5},{5,3},{7,1},{8,14},{10,12},{12... | collective-permute-start | bytes 393224 | tf_op jit(solution)/shard_map/ppermute | solution.py:420
  47.1 4.1 %collective-permute-done.13.r2 = bf16[64,1024]{1,0:T(8,128)(2,1)S(1)} collective-permute-done((bf16[64,1024]{1,0:T(8,128)(2,1)S(1)}, bf16[64,1024]{1,0:T(8,128)(2,1)S(1)}, u32[]{:S(2)}, u32[]{:S(2)}) %collective-permute-start.13) | collective-permute-done | bytes 131104 | tf_op jit(solution)/shard_map/ppermute | solution.py:420
  51.2 2.8 %collective-permute-done.14.r3 = bf16[64,1024]{1,0:T(8,128)(2,1)S(1)} collective-permute-done((bf16[64,1024]{1,0:T(8,128)(2,1)S(1)}, bf16[64,1024]{1,0:T(8,128)(2,1)S(1)}, u32[]{:S(2)}, u32[]{:S(2)}) %collective-permute-start.14) | collective-permute-done | bytes 131104 | tf_op jit(solution)/shard_map/ppermute | solution.py:420
  54.0 4.5 %collective-permute-start.15 = (bf16[32,1024]{1,0:T(8,128)(2,1)S(1)}, bf16[32,1024]{1,0:T(8,128)(2,1)S(1)}, u32[]{:S(2)}, u32[]{:S(2)}) collective-permute-start(bf16[32,1024]{1,0:T(8,128)(2,1)S(1)} %get-tuple-element.30), channel_id=1, source_target_pairs={{0,1},{1,0},{2,3},{3,2},{4,5},{5,4},{6,7},{7,6},{8,9},{9,8},{10,11... | collective-permute-start | bytes 196616 | tf_op jit(solution)/shard_map/ppermute | solution.py:422
  59.2 1.9 %collective-permute-done.15.other_ref = bf16[32,1024]{1,0:T(8,128)(2,1)S(1)} collective-permute-done((bf16[32,1024]{1,0:T(8,128)(2,1)S(1)}, bf16[32,1024]{1,0:T(8,128)(2,1)S(1)}, u32[]{:S(2)}, u32[]{:S(2)}) %collective-permute-start.15) | collective-permute-done | bytes 65568 | tf_op jit(solution)/shard_map/ppermute | solution.py:422
  61.1 0.7 %guide.1 = bf16[32,1024]{1,0:T(8,128)(2,1)} custom-call(f32[1]{0:T(128)S(6)} %copy.11.guidance_ref, f32[32,1024]{1,0:T(8,128)S(1)} %get-tuple-element.29.kept_ref, bf16[32,1024]{1,0:T(8,128)(2,1)S(1)} %collective-permute-done.15.other_ref), custom_call_target="tpu_custom_call" | custom-call | flops 1000 | bytes 1000 | tf_op jit(solution)/shard_map/guide/pallas_call | solution.py:386
  (25 shorter events, 0.2 us)
Async XLA Ops:
  0.0 18.6 %copy-start.3 = (bf16[1024,256]{1,0:T(8,128)(2,1)S(1)}, bf16[1024,256]{1,0:T(8,128)(2,1)}, u32[]{:S(2)}) copy-start(bf16[1024,256]{1,0:T(8,128)(2,1)} %wq_ref.1) | copy-start | bytes 1572868
  2.2 16.7 %copy-start.4 = (s32[8,2]{0,1:T(2,128)S(1)}, s32[8,2]{0,1:T(2,128)}, u32[]{:S(2)}) copy-start(s32[8,2]{0,1:T(2,128)} %param.11) | copy-start | bytes 196
  2.2 16.7 %copy-start.5 = (s32[2]{0:T(128)S(1)}, s32[2]{0:T(128)}, u32[]{:S(2)}) copy-start(s32[2]{0:T(128)} %counts_ref.1) | copy-start | bytes 28
  2.2 9.9 %collective-permute-start.6 = (bf16[128,1024]{1,0:T(8,128)(2,1)S(1)}, bf16[128,1024]{1,0:T(8,128)(2,1)S(1)}, u32[]{:S(2)}, u32[]{:S(2)}) collective-permute-start(bf16[128,1024]{1,0:T(8,128)(2,1)S(1)} %get-tuple-element.22.refs_0_), channel_id=1, source_target_pairs={{0,2},{2,0},{4,6},{6,4},{1,3},{3,1},{5,7},{7,5},{8,10},{10,8},{12,... | collective-permute-start | bytes 786440 | tf_op jit(solution)/shard_map/ppermute | solution.py:407
  4.4 9.7 %collective-permute-start.2 = (bf16[512,256]{1,0:T(8,128)(2,1)S(1)}, bf16[512,256]{1,0:T(8,128)(2,1)S(1)}, u32[]{:S(2)}, u32[]{:S(2)}) collective-permute-start(bf16[512,256]{1,0:T(8,128)(2,1)S(1)} %get-tuple-element.19.refs_0_), channel_id=1, source_target_pairs={{0,32},{8,40},{16,48},{24,56},{32,0},{40,8},{48,16},{56,24},{64,96... | collective-permute-start | bytes 786440 | tf_op jit(solution)/shard_map/ppermute | solution.py:405
  7.3 12.4 %collective-permute-start = (bf16[512,256]{1,0:T(8,128)(2,1)S(1)}, bf16[512,256]{1,0:T(8,128)(2,1)S(1)}, u32[]{:S(2)}, u32[]{:S(2)}) collective-permute-start(bf16[512,256]{1,0:T(8,128)(2,1)S(1)} %get-tuple-element.19.refs_0_), channel_id=1, source_target_pairs={{16,32},{32,16},{24,40},{40,24},{48,64},{64,48},{56,72},{72,56},{8... | collective-permute-start | bytes 786440 | tf_op jit(solution)/shard_map/ppermute | solution.py:404
  12.1 8.5 %collective-permute-start.1 = (bf16[512,256]{1,0:T(8,128)(2,1)S(1)}, bf16[512,256]{1,0:T(8,128)(2,1)S(1)}, u32[]{:S(2)}, u32[]{:S(2)}) collective-permute-start(bf16[512,256]{1,0:T(8,128)(2,1)S(1)} %get-tuple-element.19.refs_0_), channel_id=1, source_target_pairs={{0,16},{16,0},{8,24},{24,8},{32,48},{48,32},{40,56},{56,40},{64,80... | collective-permute-start | bytes 786440 | tf_op jit(solution)/shard_map/ppermute | solution.py:404
  12.2 16.0 %collective-permute-start.7 = (bf16[256,1024]{1,0:T(8,128)(2,1)S(1)}, bf16[256,1024]{1,0:T(8,128)(2,1)S(1)}, u32[]{:S(2)}, u32[]{:S(2)}) collective-permute-start(bf16[256,1024]{1,0:T(8,128)(2,1)S(1)} %stack.2), channel_id=1, source_target_pairs={{0,6},{2,4},{4,2},{6,0},{1,7},{3,5},{5,3},{7,1},{8,14},{10,12},{12... | collective-permute-start | bytes 1572872 | tf_op jit(solution)/shard_map/ppermute | solution.py:408
  14.1 12.1 %collective-permute-start.3 = (bf16[512,256]{1,0:T(8,128)(2,1)S(1)}, bf16[512,256]{1,0:T(8,128)(2,1)S(1)}, u32[]{:S(2)}, u32[]{:S(2)}) collective-permute-start(bf16[512,256]{1,0:T(8,128)(2,1)S(1)} %collective-permute-done.2.refs_0_.refs_1_), channel_id=1, source_target_pairs={{0,64},{8,72},{16,80},{24,88},{32,224},{40,232},{48,240},{56,248},... | collective-permute-start | bytes 786440 | tf_op jit(solution)/shard_map/ppermute | solution.py:406
  14.7 13.4 %collective-permute-start.5 = (bf16[512,256]{1,0:T(8,128)(2,1)S(1)}, bf16[512,256]{1,0:T(8,128)(2,1)S(1)}, u32[]{:S(2)}, u32[]{:S(2)}) collective-permute-start(bf16[512,256]{1,0:T(8,128)(2,1)S(1)} %get-tuple-element.19.refs_0_), channel_id=1, source_target_pairs={{0,8},{8,0},{16,24},{24,16},{32,40},{40,32},{48,56},{56,48},{64,72... | collective-permute-start | bytes 786440 | tf_op jit(solution)/shard_map/ppermute | solution.py:413
  26.2 3.4 %collective-permute-start.4 = (bf16[512,256]{1,0:T(8,128)(2,1)S(1)}, bf16[512,256]{1,0:T(8,128)(2,1)S(1)}, u32[]{:S(2)}, u32[]{:S(2)}) collective-permute-start(bf16[512,256]{1,0:T(8,128)(2,1)S(1)} %pick.1), channel_id=1, source_target_pairs={{0,8},{8,0},{16,24},{24,16},{32,40},{40,32},{48,56},{56,48},{64,72... | collective-permute-start | bytes 786440 | tf_op jit(solution)/shard_map/ppermute | solution.py:413
  30.7 6.4 %collective-permute-start.10 = (bf16[256,256]{1,0:T(8,128)(2,1)S(1)}, bf16[256,256]{1,0:T(8,128)(2,1)S(1)}, u32[]{:S(2)}, u32[]{:S(2)}) collective-permute-start(bf16[256,256]{1,0:T(8,128)(2,1)S(1)} %attend.5.a0.refs_2_), channel_id=1, source_target_pairs={{0,6},{2,4},{4,2},{6,0},{1,7},{3,5},{5,3},{7,1},{8,14},{10,12},{12... | collective-permute-start | bytes 393224 | tf_op jit(solution)/shard_map/ppermute | solution.py:418
  32.6 4.8 %collective-permute-start.8 = (bf16[256,256]{1,0:T(8,128)(2,1)S(1)}, bf16[256,256]{1,0:T(8,128)(2,1)S(1)}, u32[]{:S(2)}, u32[]{:S(2)}) collective-permute-start(bf16[256,256]{1,0:T(8,128)(2,1)S(1)} %attend.5.a0.refs_2_), channel_id=1, source_target_pairs={{0,2},{2,0},{4,6},{6,4},{1,3},{3,1},{5,7},{7,5},{8,10},{10,8},{12,... | collective-permute-start | bytes 393224 | tf_op jit(solution)/shard_map/ppermute | solution.py:418
  33.0 7.8 %collective-permute-start.9 = (bf16[256,256]{1,0:T(8,128)(2,1)S(1)}, bf16[256,256]{1,0:T(8,128)(2,1)S(1)}, u32[]{:S(2)}, u32[]{:S(2)}) collective-permute-start(bf16[256,256]{1,0:T(8,128)(2,1)S(1)} %attend.5.a0.refs_2_), channel_id=1, source_target_pairs={{0,4},{2,6},{4,0},{6,2},{1,5},{3,7},{5,1},{7,3},{8,12},{10,14},{12... | collective-permute-start | bytes 393224 | tf_op jit(solution)/shard_map/ppermute | solution.py:418
  34.7 6.2 %copy-start = (bf16[256,1024]{1,0:T(8,128)(2,1)S(1)}, bf16[256,1024]{1,0:T(8,128)(2,1)}, u32[]{:S(2)}) copy-start(bf16[256,1024]{1,0:T(8,128)(2,1)} %o0.1) | copy-start | bytes 1572868
  34.8 6.2 %copy-start.1 = (bf16[1024,1024]{1,0:T(8,128)(2,1)S(1)}, bf16[1024,1024]{1,0:T(8,128)(2,1)}, u32[]{:S(2)}) copy-start(bf16[1024,1024]{1,0:T(8,128)(2,1)} %win_ref.1) | copy-start | bytes 6291460
  34.8 6.2 %copy-start.2 = (bf16[1024,1024]{1,0:T(8,128)(2,1)S(1)}, bf16[1024,1024]{1,0:T(8,128)(2,1)}, u32[]{:S(2)}) copy-start(bf16[1024,1024]{1,0:T(8,128)(2,1)} %wback_ref.1) | copy-start | bytes 6291460
  34.8 6.1 %collective-permute-start.11 = (bf16[384,1024]{1,0:T(8,128)(2,1)S(1)}, bf16[384,1024]{1,0:T(8,128)(2,1)S(1)}, u32[]{:S(2)}, u32[]{:S(2)}) collective-permute-start(bf16[384,1024]{1,0:T(8,128)(2,1)S(1)} %stack.3), channel_id=1, source_target_pairs={{0,8},{8,0},{16,24},{24,16},{32,40},{40,32},{48,56},{56,48},{64,72... | collective-permute-start | bytes 2359304 | tf_op jit(solution)/shard_map/ppermute | solution.py:416
  43.2 3.9 %collective-permute-start.12 = (bf16[64,1024]{1,0:T(8,128)(2,1)S(1)}, bf16[64,1024]{1,0:T(8,128)(2,1)S(1)}, u32[]{:S(2)}, u32[]{:S(2)}) collective-permute-start(bf16[64,1024]{1,0:T(8,128)(2,1)S(1)} %get-tuple-element.26), channel_id=1, source_target_pairs={{0,2},{2,0},{4,6},{6,4},{1,3},{3,1},{5,7},{7,5},{8,10},{10,8},{12,... | collective-permute-start | bytes 393224 | tf_op jit(solution)/shard_map/ppermute | solution.py:420
  43.3 7.9 %collective-permute-start.13 = (bf16[64,1024]{1,0:T(8,128)(2,1)S(1)}, bf16[64,1024]{1,0:T(8,128)(2,1)S(1)}, u32[]{:S(2)}, u32[]{:S(2)}) collective-permute-start(bf16[64,1024]{1,0:T(8,128)(2,1)S(1)} %get-tuple-element.27), channel_id=1, source_target_pairs={{0,4},{2,6},{4,0},{6,2},{1,5},{3,7},{5,1},{7,3},{8,12},{10,14},{12... | collective-permute-start | bytes 393224 | tf_op jit(solution)/shard_map/ppermute | solution.py:420
  46.3 7.7 %collective-permute-start.14 = (bf16[64,1024]{1,0:T(8,128)(2,1)S(1)}, bf16[64,1024]{1,0:T(8,128)(2,1)S(1)}, u32[]{:S(2)}, u32[]{:S(2)}) collective-permute-start(bf16[64,1024]{1,0:T(8,128)(2,1)S(1)} %get-tuple-element.28), channel_id=1, source_target_pairs={{0,6},{2,4},{4,2},{6,0},{1,7},{3,5},{5,3},{7,1},{8,14},{10,12},{12... | collective-permute-start | bytes 393224 | tf_op jit(solution)/shard_map/ppermute | solution.py:420
  54.0 7.1 %collective-permute-start.15 = (bf16[32,1024]{1,0:T(8,128)(2,1)S(1)}, bf16[32,1024]{1,0:T(8,128)(2,1)S(1)}, u32[]{:S(2)}, u32[]{:S(2)}) collective-permute-start(bf16[32,1024]{1,0:T(8,128)(2,1)S(1)} %get-tuple-element.30), channel_id=1, source_target_pairs={{0,1},{1,0},{2,3},{3,2},{4,5},{5,4},{6,7},{7,6},{8,9},{9,8},{10,11... | collective-permute-start | bytes 196616 | tf_op jit(solution)/shard_map/ppermute | solution.py:422

commit v6 on v5

--- a/solution.py
+++ b/solution.py
@@ -156,9 +156,9 @@
 
 
 def attend_kernel(blocks, first, last, bias_ref, q_ref, *refs):
-    count = len(blocks)
-    kv_refs = refs[:count]
-    refs = refs[count:]
+    refs, kv_refs = list(refs), []
+    for _, part, _ in blocks:
+        kv_refs.append(refs.pop(0) if part is not None else (refs.pop(0), refs.pop(0)))
     if not first:
         held_ref, held_tops_ref = refs[:2]
         refs = refs[2:]
@@ -172,14 +172,15 @@
         apart = jnp.concatenate([jnp.where(lane // HD == h, q, jnp.zeros_like(q)) for h in range(heads)], axis=0)
         scores, biases, values = [], [], []
         for (slot, part, both), kv_ref in zip(blocks, kv_refs):
-            base = part * (rows + columns)
+            base = (part or 0) * (rows + columns)
+            k_ref, v_ref, v_base = (kv_ref, kv_ref, base + rows) if part is not None else (*kv_ref, 0)
             for kvw in (0, 1) if both else (qv,):
                 span = slice(kvw * tok, (kvw + 1) * tok)
-                keys = kv_ref[base + kvw * tok : base + (kvw + 1) * tok]
+                keys = k_ref[base + kvw * tok : base + (kvw + 1) * tok]
                 scores.append(lax.dot_general(keys, apart, NT, preferred_element_type=jnp.float32))
                 row = BIASES * qv + 2 * slot + kvw
                 biases.append(jnp.concatenate([bias_ref[row : row + 1]] * heads, axis=1))
-                values.append(kv_ref[base + rows : base + rows + columns, span])
+                values.append(v_ref[v_base : v_base + columns, span])
         top = functools.reduce(jnp.maximum, [jnp.max(s, axis=0, keepdims=True) + b for s, b in zip(scores, biases)])
         if not first:
             old_top, old_total = held_tops_ref[2 * qv : 2 * qv + 1], held_tops_ref[2 * qv + 1 : 2 * qv + 2]
@@ -233,25 +234,28 @@
 
 
 def pick_kernel(a_ref, b_ref, *refs):
-    out_ref = refs[-1]
+    keys_ref, values_ref = refs[-2:]
+    rows = keys_ref.shape[0]
     me = lax.axis_index("view")
     first = (me & 1) != ((me >> 1) & 1)
 
     @pl.when(first)
     def _():
-        out_ref[...] = a_ref[...]
+        keys_ref[...] = a_ref[:rows]
+        values_ref[...] = a_ref[rows:]
 
     @pl.when(jnp.logical_not(first))
     def _():
-        out_ref[...] = b_ref[...]
+        keys_ref[...] = b_ref[:rows]
+        values_ref[...] = b_ref[rows:]
 
 
 def pick(a, b, *after):
     return pl.pallas_call(
         pick_kernel,
-        out_shape=held(a.shape, a.dtype),
+        out_shape=(held((a.shape[0] // 2, a.shape[1]), a.dtype),) * 2,
         in_specs=[VMEM] * 2 + [ANY] * len(after),
-        out_specs=VMEM,
+        out_specs=(VMEM,) * 2,
         compiler_params=params(2),
         cost_estimate=COST,
         name="pick",
@@ -408,11 +412,12 @@
     w_32 = flipped("head", 4, 3)(stack(w_half, w_1, after=x))
     q = ask(x, w_query, x)
     bias = biases(count, partners.T, counts, x)
-    state = attend(((0, 0, True), (2, 0, False), (3, 0, False)), True, False, bias, q, (kv, *near))
+    state = attend(((0, 0, True),), True, False, bias, q, (kv,))
     other_core = flipped("view", count, 1)
-    other, cross = other_core(kv), other_core(pick(*near, *far, state[1]))
-    state = attend(((1, 0, True), (5, 0, False), (6, 0, False)), False, False, bias, q, (other, *far), state, w_32)
-    attended = attend(((4, 0, True),), False, True, bias, q, (cross,), state)
+    other = other_core(kv)
+    cross = [other_core(p) for p in pick(*near, state[1])]
+    state = attend(((1, 0, True), (2, 0, False), (3, 0, False)), False, False, bias, q, (other, *near), state)
+    attended = attend(((4, None, True), (5, 0, False), (6, 0, False)), False, True, bias, q, (*cross, *far), state)
     w_pair = other_core(stack(w_1, w_32, after=attended))
 
     pieces = [attended] + [flipped("head", 4, j)(attended) for j in (1, 2, 3)]

time: 61.9 us -> 61.1 us (0.987)
  the two profiles are of different devices: /device:TPU:1 before, /device:TPU:24 now
where the time goes in v6:
time: 61.1 us; the launch traced here: 61 us
  starting transfers between devices  26.6 us (44%)
  waiting for transfers between devices  22.9 us (37%)
  Pallas kernels  10.5 us (17%)
  between operations  0.89 us (1%)
    ppermute x3, waiting for transfers between devices, on_device(): pieces = [attended] + [flipped('head', 4, j)(attended) for j in (1, 2, 3)]  7.08 us
    ppermute x3, waiting for transfers between devices, on_device(): received = [flipped('head', 4, j)(r) for j, r in zip((1, 2, 3), outgoing)]  5.5 us
    ppermute x3, starting transfers between devices, on_device(): pieces = [attended] + [flipped('head', 4, j)(attended) for j in (1, 2, 3)]  4.79 us
    ppermute x3, starting transfers between devices, on_device(): received = [flipped('head', 4, j)(r) for j, r in zip((1, 2, 3), outgoing)]  4.78 us
    ppermute x1, waiting for transfers between devices, on_device(): other = flipped('branch', 2, 1)(sent)  4.68 us
    pallas_call x3, Pallas kernels, attend(): pl.pallas_call(functools.partial(attend_kernel, blocks, first, last), out...  4.12 us
    ppermute x1, waiting for transfers between devices, on_device(): across = flipped('view', count, 4)(kv)  3.88 us
    ppermute x2, starting transfers between devices, on_device(): near = [matched(count, 2, parity)(kv) for parity in (1, 0)]  3.54 us
  transfers between devices with their start and end apart: 17, of which 9 were waited for; matrix products, arithmetic and copies ran while one was open for 0% of the time, Pallas kernels for 9%

profile of v6, /device:TPU:24, one launch (start us, length us, event | category | flops | bytes accessed | tf_op | source)
XLA Modules:
  0.0 61.0 jit_solution(5730746027920741090)
XLA Ops:
  0.0 2.2 %project.1 = (bf16[256,1024]{1,0:T(8,128)(2,1)S(1)}, bf16[512,256]{1,0:T(8,128)(2,1)S(1)}, bf16[128,1024]{1,0:T(8,128)(2,1)S(1)}) custom-call(bf16[256,1024]{1,0:T(8,128)(2,1)} %bitcast.4, bf16[1024,256]{1,0:T(8,128)(2,1)} %wk_hbm.1, bf16[1024,256]{1,0:T(8,128)(2,1)} %wv_hbm.1, bf16[256,1024]{1,0:T(8,128)(2,1)} %o0.1), custom_call_target="tpu_custom_call" | custom-call | flops 1000 | bytes 1000 | tf_op jit(solution)/shard_map/project/pallas_call | solution.py:126
  2.2 1.6 %collective-permute-start.10 = (bf16[128,1024]{1,0:T(8,128)(2,1)S(1)}, bf16[128,1024]{1,0:T(8,128)(2,1)S(1)}, u32[]{:S(2)}, u32[]{:S(2)}) collective-permute-start(bf16[128,1024]{1,0:T(8,128)(2,1)S(1)} %get-tuple-element.28.refs_0_), channel_id=1, source_target_pairs={{0,2},{2,0},{4,6},{6,4},{1,3},{3,1},{5,7},{7,5},{8,10},{10,8},{12,... | collective-permute-start | bytes 786440 | tf_op jit(solution)/shard_map/ppermute | solution.py:411
  3.8 1.2 %collective-permute-start.4 = (bf16[512,256]{1,0:T(8,128)(2,1)S(1)}, bf16[512,256]{1,0:T(8,128)(2,1)S(1)}, u32[]{:S(2)}, u32[]{:S(2)}) collective-permute-start(bf16[512,256]{1,0:T(8,128)(2,1)S(1)} %get-tuple-element.21.refs_0_), channel_id=1, source_target_pairs={{0,32},{8,40},{16,48},{24,56},{32,0},{40,8},{48,16},{56,24},{64,96... | collective-permute-start | bytes 786440 | tf_op jit(solution)/shard_map/ppermute | solution.py:409
  5.1 3.5 %collective-permute-start = (bf16[512,256]{1,0:T(8,128)(2,1)S(1)}, bf16[512,256]{1,0:T(8,128)(2,1)S(1)}, u32[]{:S(2)}, u32[]{:S(2)}) collective-permute-start(bf16[512,256]{1,0:T(8,128)(2,1)S(1)} %get-tuple-element.21.refs_0_), channel_id=1, source_target_pairs={{16,32},{32,16},{24,40},{40,24},{48,64},{64,48},{56,72},{72,56},{8... | collective-permute-start | bytes 786440 | tf_op jit(solution)/shard_map/ppermute | solution.py:408
  8.6 1.8 %collective-permute-done.10.refs_1_.refs_0_.w1 = bf16[128,1024]{1,0:T(8,128)(2,1)S(1)} collective-permute-done((bf16[128,1024]{1,0:T(8,128)(2,1)S(1)}, bf16[128,1024]{1,0:T(8,128)(2,1)S(1)}, u32[]{:S(2)}, u32[]{:S(2)}) %collective-permute-start.10) | collective-permute-done | bytes 262176 | tf_op jit(solution)/shard_map/ppermute | solution.py:411
  10.4 2.8 %collective-permute-start.11 = (bf16[256,1024]{1,0:T(8,128)(2,1)S(1)}, bf16[256,1024]{1,0:T(8,128)(2,1)S(1)}, u32[]{:S(2)}, u32[]{:S(2)}) collective-permute-start(bf16[256,1024]{1,0:T(8,128)(2,1)S(1)} %stack.2), channel_id=1, source_target_pairs={{0,6},{2,4},{4,2},{6,0},{1,7},{3,5},{5,3},{7,1},{8,14},{10,12},{12... | collective-permute-start | bytes 1572872 | tf_op jit(solution)/shard_map/ppermute | solution.py:412
  13.3 3.9 %collective-permute-done.4.refs_2_ = bf16[512,256]{1,0:T(8,128)(2,1)S(1)} collective-permute-done((bf16[512,256]{1,0:T(8,128)(2,1)S(1)}, bf16[512,256]{1,0:T(8,128)(2,1)S(1)}, u32[]{:S(2)}, u32[]{:S(2)}) %collective-permute-start.4) | collective-permute-done | bytes 262176 | tf_op jit(solution)/shard_map/ppermute | solution.py:409
  17.1 3.5 %collective-permute-start.5 = (bf16[512,256]{1,0:T(8,128)(2,1)S(1)}, bf16[512,256]{1,0:T(8,128)(2,1)S(1)}, u32[]{:S(2)}, u32[]{:S(2)}) collective-permute-start(bf16[512,256]{1,0:T(8,128)(2,1)S(1)} %collective-permute-done.4.refs_2_), channel_id=1, source_target_pairs={{0,64},{8,72},{16,80},{24,88},{32,224},{40,232},{48,240},{56,248},... | collective-permute-start | bytes 786440 | tf_op jit(solution)/shard_map/ppermute | solution.py:410
  20.7 0.3 ask.1.q_ref
  21.0 0.8 %biases.1.bias_ref = f32[32,128]{1,0:T(8,128)S(1)} custom-call(s32[2,8]{1,0:T(2,128)S(1)} %bitcast.3, s32[2]{0:T(128)S(1)} %copy-done.5, bf16[256,1024]{1,0:T(8,128)(2,1)S(1)} %get-tuple-element.20.after_ref.x_ref.refs_2_), custom_call_target="tpu_custom_call" | custom-call | flops 1000 | bytes 1000 | tf_op jit(solution)/shard_map/biases/pallas_call | solution.py:96
  21.8 1.0 %attend.3 = (f32[512,128]{1,0:T(8,128)S(1)}, f32[4,512]{1,0:T(4,128)S(1)}) custom-call(f32[32,128]{1,0:T(8,128)S(1)} %biases.1.bias_ref, bf16[256,256]{1,0:T(8,128)(2,1)S(1)} %ask.1.q_ref, bf16[512,256]{1,0:T(8,128)(2,1)S(1)} %get-tuple-element.21.refs_0_), custom_call_target="tpu_custom_call" | custom-call | flops 1000 | bytes 1000 | tf_op jit(solution)/shard_map/attend/pallas_call | solution.py:225
  22.8 0.1 collective-permute-start.2
  22.9 0.5 collective-permute-start.3
  23.4 1.5 %attend.4 = (f32[512,128]{1,0:T(8,128)S(1)}, f32[4,512]{1,0:T(4,128)S(1)}) custom-call(f32[32,128]{1,0:T(8,128)S(1)} %biases.1.bias_ref, bf16[256,256]{1,0:T(8,128)(2,1)S(1)} %ask.1.q_ref, bf16[512,256]{1,0:T(8,128)(2,1)S(1)} %collective-permute-done.6.refs_0_, bf16[512,256]{1,0:T(8,128)(2,1)S(1)} %collective-permute-done.a_ref.refs_1_, ...), custom_call_target="tpu_custom_call" | custom-call | flops 1000 | bytes 1000 | tf_op jit(solution)/shard_map/attend/pallas_call | solution.py:225
  25.0 1.6 %attend.5.a0.refs_2_ = bf16[256,256]{1,0:T(8,128)(2,1)S(1)} custom-call(f32[32,128]{1,0:T(8,128)S(1)} %biases.1.bias_ref, bf16[256,256]{1,0:T(8,128)(2,1)S(1)} %ask.1.q_ref, bf16[256,256]{1,0:T(8,128)(2,1)S(1)} %collective-permute-done.2.refs_0_, bf16[256,256]{1,0:T(8,128)(2,1)S(1)} %collective-permute-done.3.refs_1_, ...), custom_call_target="tpu_custom_call" | custom-call | flops 1000 | bytes 1000 | tf_op jit(solution)/shard_map/attend/pallas_call | solution.py:225
  26.6 0.6 %collective-permute-start.7 = (bf16[256,256]{1,0:T(8,128)(2,1)S(1)}, bf16[256,256]{1,0:T(8,128)(2,1)S(1)}, u32[]{:S(2)}, u32[]{:S(2)}) collective-permute-start(bf16[256,256]{1,0:T(8,128)(2,1)S(1)} %attend.5.a0.refs_2_), channel_id=1, source_target_pairs={{0,2},{2,0},{4,6},{6,4},{1,3},{3,1},{5,7},{7,5},{8,10},{10,8},{12,... | collective-permute-start | bytes 393224 | tf_op jit(solution)/shard_map/ppermute | solution.py:423
  27.2 3.0 %collective-permute-start.8 = (bf16[256,256]{1,0:T(8,128)(2,1)S(1)}, bf16[256,256]{1,0:T(8,128)(2,1)S(1)}, u32[]{:S(2)}, u32[]{:S(2)}) collective-permute-start(bf16[256,256]{1,0:T(8,128)(2,1)S(1)} %attend.5.a0.refs_2_), channel_id=1, source_target_pairs={{0,4},{2,6},{4,0},{6,2},{1,5},{3,7},{5,1},{7,3},{8,12},{10,14},{12... | collective-permute-start | bytes 393224 | tf_op jit(solution)/shard_map/ppermute | solution.py:423
  30.2 1.1 %collective-permute-start.9 = (bf16[256,256]{1,0:T(8,128)(2,1)S(1)}, bf16[256,256]{1,0:T(8,128)(2,1)S(1)}, u32[]{:S(2)}, u32[]{:S(2)}) collective-permute-start(bf16[256,256]{1,0:T(8,128)(2,1)S(1)} %attend.5.a0.refs_2_), channel_id=1, source_target_pairs={{0,6},{2,4},{4,2},{6,0},{1,7},{3,5},{5,3},{7,1},{8,14},{10,12},{12... | collective-permute-start | bytes 393224 | tf_op jit(solution)/shard_map/ppermute | solution.py:423
  31.5 0.3 collective-permute-start.12
  31.8 1.3 %collective-permute-done.7.a1 = bf16[256,256]{1,0:T(8,128)(2,1)S(1)} collective-permute-done((bf16[256,256]{1,0:T(8,128)(2,1)S(1)}, bf16[256,256]{1,0:T(8,128)(2,1)S(1)}, u32[]{:S(2)}, u32[]{:S(2)}) %collective-permute-start.7) | collective-permute-done | bytes 131104 | tf_op jit(solution)/shard_map/ppermute | solution.py:423
  33.0 3.6 %collective-permute-done.8.a2 = bf16[256,256]{1,0:T(8,128)(2,1)S(1)} collective-permute-done((bf16[256,256]{1,0:T(8,128)(2,1)S(1)}, bf16[256,256]{1,0:T(8,128)(2,1)S(1)}, u32[]{:S(2)}, u32[]{:S(2)}) %collective-permute-start.8) | collective-permute-done | bytes 131104 | tf_op jit(solution)/shard_map/ppermute | solution.py:423
  36.6 2.2 %collective-permute-done.9.a3 = bf16[256,256]{1,0:T(8,128)(2,1)S(1)} collective-permute-done((bf16[256,256]{1,0:T(8,128)(2,1)S(1)}, bf16[256,256]{1,0:T(8,128)(2,1)S(1)}, u32[]{:S(2)}, u32[]{:S(2)}) %collective-permute-start.9) | collective-permute-done | bytes 131104 | tf_op jit(solution)/shard_map/ppermute | solution.py:423
  38.8 0.1 lay.1.left_ref
  39.0 2.2 %feed.1 = (f32[64,1024]{1,0:T(8,128)S(1)}, bf16[64,1024]{1,0:T(8,128)(2,1)S(1)}, bf16[64,1024]{1,0:T(8,128)(2,1)S(1)}, bf16[64,1024]{1,0:T(8,128)(2,1)S(1)}) custom-call(bf16[256,1024]{1,0:T(8,128)(2,1)S(1)} %get-tuple-element.20.after_ref.x_ref.refs_2_, bf16[256,1024]{1,0:T(8,128)(2,1)S(1)} %lay.1.left_ref, bf16[256,1024]{1,0:T(8,128)(2,1)S(1)} %copy-done, ...), custom_call_target="tpu_custom_call" | custom-call | flops 1000 | bytes 1000 | tf_op jit(solution)/shard_map/feed/pallas_call | solution.py:341
  41.3 2.6 %collective-permute-start.14 = (bf16[64,1024]{1,0:T(8,128)(2,1)S(1)}, bf16[64,1024]{1,0:T(8,128)(2,1)S(1)}, u32[]{:S(2)}, u32[]{:S(2)}) collective-permute-start(bf16[64,1024]{1,0:T(8,128)(2,1)S(1)} %get-tuple-element.31), channel_id=1, source_target_pairs={{0,4},{2,6},{4,0},{6,2},{1,5},{3,7},{5,1},{7,3},{8,12},{10,14},{12... | collective-permute-start | bytes 393224 | tf_op jit(solution)/shard_map/ppermute | solution.py:425
  43.9 2.1 %collective-permute-start.15 = (bf16[64,1024]{1,0:T(8,128)(2,1)S(1)}, bf16[64,1024]{1,0:T(8,128)(2,1)S(1)}, u32[]{:S(2)}, u32[]{:S(2)}) collective-permute-start(bf16[64,1024]{1,0:T(8,128)(2,1)S(1)} %get-tuple-element.32), channel_id=1, source_target_pairs={{0,6},{2,4},{4,2},{6,0},{1,7},{3,5},{5,3},{7,1},{8,14},{10,12},{12... | collective-permute-start | bytes 393224 | tf_op jit(solution)/shard_map/ppermute | solution.py:425
  46.0 1.6 %collective-permute-done.13.r1 = bf16[64,1024]{1,0:T(8,128)(2,1)S(1)} collective-permute-done((bf16[64,1024]{1,0:T(8,128)(2,1)S(1)}, bf16[64,1024]{1,0:T(8,128)(2,1)S(1)}, u32[]{:S(2)}, u32[]{:S(2)}) %collective-permute-start.13) | collective-permute-done | bytes 131104 | tf_op jit(solution)/shard_map/ppermute | solution.py:425
  47.6 2.1 %collective-permute-done.14.r2 = bf16[64,1024]{1,0:T(8,128)(2,1)S(1)} collective-permute-done((bf16[64,1024]{1,0:T(8,128)(2,1)S(1)}, bf16[64,1024]{1,0:T(8,128)(2,1)S(1)}, u32[]{:S(2)}, u32[]{:S(2)}) %collective-permute-start.14) | collective-permute-done | bytes 131104 | tf_op jit(solution)/shard_map/ppermute | solution.py:425
  49.6 1.8 %collective-permute-done.15.r3 = bf16[64,1024]{1,0:T(8,128)(2,1)S(1)} collective-permute-done((bf16[64,1024]{1,0:T(8,128)(2,1)S(1)}, bf16[64,1024]{1,0:T(8,128)(2,1)S(1)}, u32[]{:S(2)}, u32[]{:S(2)}) %collective-permute-start.15) | collective-permute-done | bytes 131104 | tf_op jit(solution)/shard_map/ppermute | solution.py:425
  51.6 3.5 %collective-permute-start.16 = (bf16[32,1024]{1,0:T(8,128)(2,1)S(1)}, bf16[32,1024]{1,0:T(8,128)(2,1)S(1)}, u32[]{:S(2)}, u32[]{:S(2)}) collective-permute-start(bf16[32,1024]{1,0:T(8,128)(2,1)S(1)} %get-tuple-element.34), channel_id=1, source_target_pairs={{0,1},{1,0},{2,3},{3,2},{4,5},{5,4},{6,7},{7,6},{8,9},{9,8},{10,11... | collective-permute-start | bytes 196616 | tf_op jit(solution)/shard_map/ppermute | solution.py:427
  55.7 4.7 %collective-permute-done.16.other_ref = bf16[32,1024]{1,0:T(8,128)(2,1)S(1)} collective-permute-done((bf16[32,1024]{1,0:T(8,128)(2,1)S(1)}, bf16[32,1024]{1,0:T(8,128)(2,1)S(1)}, u32[]{:S(2)}, u32[]{:S(2)}) %collective-permute-start.16) | collective-permute-done | bytes 65568 | tf_op jit(solution)/shard_map/ppermute | solution.py:427
  60.4 0.7 %guide.1 = bf16[32,1024]{1,0:T(8,128)(2,1)} custom-call(f32[1]{0:T(128)S(6)} %copy.11.guidance_ref, f32[32,1024]{1,0:T(8,128)S(1)} %get-tuple-element.33.kept_ref, bf16[32,1024]{1,0:T(8,128)(2,1)S(1)} %collective-permute-done.16.other_ref), custom_call_target="tpu_custom_call" | custom-call | flops 1000 | bytes 1000 | tf_op jit(solution)/shard_map/guide/pallas_call | solution.py:390
  (27 shorter events, 0.3 us)
Async XLA Ops:
  0.0 20.7 %copy-start.3 = (bf16[1024,256]{1,0:T(8,128)(2,1)S(1)}, bf16[1024,256]{1,0:T(8,128)(2,1)}, u32[]{:S(2)}) copy-start(bf16[1024,256]{1,0:T(8,128)(2,1)} %wq_ref.1) | copy-start | bytes 1572868
  2.2 18.8 %copy-start.4 = (s32[8,2]{0,1:T(2,128)S(1)}, s32[8,2]{0,1:T(2,128)}, u32[]{:S(2)}) copy-start(s32[8,2]{0,1:T(2,128)} %param.11) | copy-start | bytes 196
  2.2 18.8 %copy-start.5 = (s32[2]{0:T(128)S(1)}, s32[2]{0:T(128)}, u32[]{:S(2)}) copy-start(s32[2]{0:T(128)} %counts_ref.1) | copy-start | bytes 28
  2.2 8.1 %collective-permute-start.10 = (bf16[128,1024]{1,0:T(8,128)(2,1)S(1)}, bf16[128,1024]{1,0:T(8,128)(2,1)S(1)}, u32[]{:S(2)}, u32[]{:S(2)}) collective-permute-start(bf16[128,1024]{1,0:T(8,128)(2,1)S(1)} %get-tuple-element.28.refs_0_), channel_id=1, source_target_pairs={{0,2},{2,0},{4,6},{6,4},{1,3},{3,1},{5,7},{7,5},{8,10},{10,8},{12,... | collective-permute-start | bytes 786440 | tf_op jit(solution)/shard_map/ppermute | solution.py:411
  3.8 13.3 %collective-permute-start.4 = (bf16[512,256]{1,0:T(8,128)(2,1)S(1)}, bf16[512,256]{1,0:T(8,128)(2,1)S(1)}, u32[]{:S(2)}, u32[]{:S(2)}) collective-permute-start(bf16[512,256]{1,0:T(8,128)(2,1)S(1)} %get-tuple-element.21.refs_0_), channel_id=1, source_target_pairs={{0,32},{8,40},{16,48},{24,56},{32,0},{40,8},{48,16},{56,24},{64,96... | collective-permute-start | bytes 786440 | tf_op jit(solution)/shard_map/ppermute | solution.py:409
  5.1 17.7 %collective-permute-start = (bf16[512,256]{1,0:T(8,128)(2,1)S(1)}, bf16[512,256]{1,0:T(8,128)(2,1)S(1)}, u32[]{:S(2)}, u32[]{:S(2)}) collective-permute-start(bf16[512,256]{1,0:T(8,128)(2,1)S(1)} %get-tuple-element.21.refs_0_), channel_id=1, source_target_pairs={{16,32},{32,16},{24,40},{40,24},{48,64},{64,48},{56,72},{72,56},{8... | collective-permute-start | bytes 786440 | tf_op jit(solution)/shard_map/ppermute | solution.py:408
  8.6 14.2 %collective-permute-start.1 = (bf16[512,256]{1,0:T(8,128)(2,1)S(1)}, bf16[512,256]{1,0:T(8,128)(2,1)S(1)}, u32[]{:S(2)}, u32[]{:S(2)}) collective-permute-start(bf16[512,256]{1,0:T(8,128)(2,1)S(1)} %get-tuple-element.21.refs_0_), channel_id=1, source_target_pairs={{0,16},{16,0},{8,24},{24,8},{32,48},{48,32},{40,56},{56,40},{64,80... | collective-permute-start | bytes 786440 | tf_op jit(solution)/shard_map/ppermute | solution.py:408
  10.4 21.0 %collective-permute-start.11 = (bf16[256,1024]{1,0:T(8,128)(2,1)S(1)}, bf16[256,1024]{1,0:T(8,128)(2,1)S(1)}, u32[]{:S(2)}, u32[]{:S(2)}) collective-permute-start(bf16[256,1024]{1,0:T(8,128)(2,1)S(1)} %stack.2), channel_id=1, source_target_pairs={{0,6},{2,4},{4,2},{6,0},{1,7},{3,5},{5,3},{7,1},{8,14},{10,12},{12... | collective-permute-start | bytes 1572872 | tf_op jit(solution)/shard_map/ppermute | solution.py:412
  13.3 10.2 %collective-permute-start.6 = (bf16[512,256]{1,0:T(8,128)(2,1)S(1)}, bf16[512,256]{1,0:T(8,128)(2,1)S(1)}, u32[]{:S(2)}, u32[]{:S(2)}) collective-permute-start(bf16[512,256]{1,0:T(8,128)(2,1)S(1)} %get-tuple-element.21.refs_0_), channel_id=1, source_target_pairs={{0,8},{8,0},{16,24},{24,16},{32,40},{40,32},{48,56},{56,48},{64,72... | collective-permute-start | bytes 786440 | tf_op jit(solution)/shard_map/ppermute | solution.py:417
  17.1 7.8 %collective-permute-start.5 = (bf16[512,256]{1,0:T(8,128)(2,1)S(1)}, bf16[512,256]{1,0:T(8,128)(2,1)S(1)}, u32[]{:S(2)}, u32[]{:S(2)}) collective-permute-start(bf16[512,256]{1,0:T(8,128)(2,1)S(1)} %collective-permute-done.4.refs_2_), channel_id=1, source_target_pairs={{0,64},{8,72},{16,80},{24,88},{32,224},{40,232},{48,240},{56,248},... | collective-permute-start | bytes 786440 | tf_op jit(solution)/shard_map/ppermute | solution.py:410
  22.8 2.1 %collective-permute-start.2 = (bf16[256,256]{1,0:T(8,128)(2,1)S(1)}, bf16[256,256]{1,0:T(8,128)(2,1)S(1)}, u32[]{:S(2)}, u32[]{:S(2)}) collective-permute-start(bf16[256,256]{1,0:T(8,128)(2,1)S(1)} %get-tuple-element.23), channel_id=1, source_target_pairs={{0,8},{8,0},{16,24},{24,16},{32,40},{40,32},{48,56},{56,48},{64,72... | collective-permute-start | bytes 393224 | tf_op jit(solution)/shard_map/ppermute | solution.py:418
  22.9 2.0 %collective-permute-start.3 = (bf16[256,256]{1,0:T(8,128)(2,1)S(1)}, bf16[256,256]{1,0:T(8,128)(2,1)S(1)}, u32[]{:S(2)}, u32[]{:S(2)}) collective-permute-start(bf16[256,256]{1,0:T(8,128)(2,1)S(1)} %get-tuple-element.24), channel_id=1, source_target_pairs={{0,8},{8,0},{16,24},{24,16},{32,40},{40,32},{48,56},{56,48},{64,72... | collective-permute-start | bytes 393224 | tf_op jit(solution)/shard_map/ppermute | solution.py:418
  26.6 6.4 %collective-permute-start.7 = (bf16[256,256]{1,0:T(8,128)(2,1)S(1)}, bf16[256,256]{1,0:T(8,128)(2,1)S(1)}, u32[]{:S(2)}, u32[]{:S(2)}) collective-permute-start(bf16[256,256]{1,0:T(8,128)(2,1)S(1)} %attend.5.a0.refs_2_), channel_id=1, source_target_pairs={{0,2},{2,0},{4,6},{6,4},{1,3},{3,1},{5,7},{7,5},{8,10},{10,8},{12,... | collective-permute-start | bytes 393224 | tf_op jit(solution)/shard_map/ppermute | solution.py:423
  27.2 9.4 %collective-permute-start.8 = (bf16[256,256]{1,0:T(8,128)(2,1)S(1)}, bf16[256,256]{1,0:T(8,128)(2,1)S(1)}, u32[]{:S(2)}, u32[]{:S(2)}) collective-permute-start(bf16[256,256]{1,0:T(8,128)(2,1)S(1)} %attend.5.a0.refs_2_), channel_id=1, source_target_pairs={{0,4},{2,6},{4,0},{6,2},{1,5},{3,7},{5,1},{7,3},{8,12},{10,14},{12... | collective-permute-start | bytes 393224 | tf_op jit(solution)/shard_map/ppermute | solution.py:423
  30.2 8.6 %collective-permute-start.9 = (bf16[256,256]{1,0:T(8,128)(2,1)S(1)}, bf16[256,256]{1,0:T(8,128)(2,1)S(1)}, u32[]{:S(2)}, u32[]{:S(2)}) collective-permute-start(bf16[256,256]{1,0:T(8,128)(2,1)S(1)} %attend.5.a0.refs_2_), channel_id=1, source_target_pairs={{0,6},{2,4},{4,2},{6,0},{1,7},{3,5},{5,3},{7,1},{8,14},{10,12},{12... | collective-permute-start | bytes 393224 | tf_op jit(solution)/shard_map/ppermute | solution.py:423
  31.5 7.5 %copy-start = (bf16[256,1024]{1,0:T(8,128)(2,1)S(1)}, bf16[256,1024]{1,0:T(8,128)(2,1)}, u32[]{:S(2)}) copy-start(bf16[256,1024]{1,0:T(8,128)(2,1)} %o0.1) | copy-start | bytes 1572868
  31.5 7.5 %copy-start.1 = (bf16[1024,1024]{1,0:T(8,128)(2,1)S(1)}, bf16[1024,1024]{1,0:T(8,128)(2,1)}, u32[]{:S(2)}) copy-start(bf16[1024,1024]{1,0:T(8,128)(2,1)} %win_ref.1) | copy-start | bytes 6291460
  31.5 7.5 %copy-start.2 = (bf16[1024,1024]{1,0:T(8,128)(2,1)S(1)}, bf16[1024,1024]{1,0:T(8,128)(2,1)}, u32[]{:S(2)}) copy-start(bf16[1024,1024]{1,0:T(8,128)(2,1)} %wback_ref.1) | copy-start | bytes 6291460
  31.5 7.5 %collective-permute-start.12 = (bf16[384,1024]{1,0:T(8,128)(2,1)S(1)}, bf16[384,1024]{1,0:T(8,128)(2,1)S(1)}, u32[]{:S(2)}, u32[]{:S(2)}) collective-permute-start(bf16[384,1024]{1,0:T(8,128)(2,1)S(1)} %stack.3), channel_id=1, source_target_pairs={{0,8},{8,0},{16,24},{24,16},{32,40},{40,32},{48,56},{56,48},{64,72... | collective-permute-start | bytes 2359304 | tf_op jit(solution)/shard_map/ppermute | solution.py:421
  41.2 6.4 %collective-permute-start.13 = (bf16[64,1024]{1,0:T(8,128)(2,1)S(1)}, bf16[64,1024]{1,0:T(8,128)(2,1)S(1)}, u32[]{:S(2)}, u32[]{:S(2)}) collective-permute-start(bf16[64,1024]{1,0:T(8,128)(2,1)S(1)} %get-tuple-element.30), channel_id=1, source_target_pairs={{0,2},{2,0},{4,6},{6,4},{1,3},{3,1},{5,7},{7,5},{8,10},{10,8},{12,... | collective-permute-start | bytes 393224 | tf_op jit(solution)/shard_map/ppermute | solution.py:425
  41.3 8.3 %collective-permute-start.14 = (bf16[64,1024]{1,0:T(8,128)(2,1)S(1)}, bf16[64,1024]{1,0:T(8,128)(2,1)S(1)}, u32[]{:S(2)}, u32[]{:S(2)}) collective-permute-start(bf16[64,1024]{1,0:T(8,128)(2,1)S(1)} %get-tuple-element.31), channel_id=1, source_target_pairs={{0,4},{2,6},{4,0},{6,2},{1,5},{3,7},{5,1},{7,3},{8,12},{10,14},{12... | collective-permute-start | bytes 393224 | tf_op jit(solution)/shard_map/ppermute | solution.py:425
  43.9 7.6 %collective-permute-start.15 = (bf16[64,1024]{1,0:T(8,128)(2,1)S(1)}, bf16[64,1024]{1,0:T(8,128)(2,1)S(1)}, u32[]{:S(2)}, u32[]{:S(2)}) collective-permute-start(bf16[64,1024]{1,0:T(8,128)(2,1)S(1)} %get-tuple-element.32), channel_id=1, source_target_pairs={{0,6},{2,4},{4,2},{6,0},{1,7},{3,5},{5,3},{7,1},{8,14},{10,12},{12... | collective-permute-start | bytes 393224 | tf_op jit(solution)/shard_map/ppermute | solution.py:425
  51.6 8.8 %collective-permute-start.16 = (bf16[32,1024]{1,0:T(8,128)(2,1)S(1)}, bf16[32,1024]{1,0:T(8,128)(2,1)S(1)}, u32[]{:S(2)}, u32[]{:S(2)}) collective-permute-start(bf16[32,1024]{1,0:T(8,128)(2,1)S(1)} %get-tuple-element.34), channel_id=1, source_target_pairs={{0,1},{1,0},{2,3},{3,2},{4,5},{5,4},{6,7},{7,6},{8,9},{9,8},{10,11... | collective-permute-start | bytes 196616 | tf_op jit(solution)/shard_map/ppermute | solution.py:427

commit v7 on v6

--- a/solution.py
+++ b/solution.py
@@ -262,24 +262,24 @@
     )(a, b, *after)
 
 
-def stack_kernel(*refs):
-    *piece_refs, _, out_ref = refs
+def stack_kernel(pieces, *refs):
+    out_ref = refs[-1]
     at = 0
-    for ref in piece_refs:
+    for ref in refs[:pieces]:
         out_ref[at : at + ref.shape[0]] = ref[...]
         at += ref.shape[0]
 
 
-def stack(*pieces, after):
-    return pl.pallas_call(
-        stack_kernel,
+def stack(*pieces, after=()):
+    return pl.pallas_call(
+        functools.partial(stack_kernel, len(pieces)),
         out_shape=held((sum(p.shape[0] for p in pieces), pieces[0].shape[1]), pieces[0].dtype),
-        in_specs=[VMEM] * len(pieces) + [ANY],
+        in_specs=[VMEM] * len(pieces) + [ANY] * len(after),
         out_specs=VMEM,
         compiler_params=params(2),
         cost_estimate=COST,
         name="stack",
-    )(*pieces, after)
+    )(*pieces, *after)
 
 
 def turned(ref, tok, columns=slice(None)):
@@ -409,16 +409,16 @@
     across = flipped("view", count, 4)(kv)
     far = (across, onward(count)(across))
     w_1 = flipped("head", 4, 1)(w_half)
-    w_32 = flipped("head", 4, 3)(stack(w_half, w_1, after=x))
     q = ask(x, w_query, x)
     bias = biases(count, partners.T, counts, x)
     state = attend(((0, 0, True),), True, False, bias, q, (kv,))
+    w_32 = flipped("head", 4, 3)(stack(w_half, w_1, after=(bias, q)))
     other_core = flipped("view", count, 1)
     other = other_core(kv)
     cross = [other_core(p) for p in pick(*near, state[1])]
     state = attend(((1, 0, True), (2, 0, False), (3, 0, False)), False, False, bias, q, (other, *near), state)
     attended = attend(((4, None, True), (5, 0, False), (6, 0, False)), False, True, bias, q, (*cross, *far), state)
-    w_pair = other_core(stack(w_1, w_32, after=attended))
+    w_pair = other_core(stack(w_1, w_32, after=(attended,)))
 
     pieces = [attended] + [flipped("head", 4, j)(attended) for j in (1, 2, 3)]
     own, *outgoing = feed(x, lay(*pieces), (w_out, w_1, w_32, w_pair), w_in, w_back)

time: 61.1 us -> 61.1 us (level)
  the two profiles are of different devices: /device:TPU:24 before, /device:TPU:8 now
where the time goes in v7:
time: 61.1 us; the launch traced here: 61 us
  starting transfers between devices  25.2 us (41%)
  waiting for transfers between devices  24.4 us (40%)
  Pallas kernels  10.5 us (17%)
  between operations  0.87 us (1%)
    ppermute x3, waiting for transfers between devices, on_device(): received = [flipped('head', 4, j)(r) for j, r in zip((1, 2, 3), outgoing)]  6.53 us
    ppermute x2, starting transfers between devices, on_device(): near = [matched(count, 2, parity)(kv) for parity in (1, 0)]  6.46 us
    ppermute x1, waiting for transfers between devices, on_device(): other = flipped('branch', 2, 1)(sent)  5.92 us
    ppermute x1, waiting for transfers between devices, on_device(): far = (across, onward(count)(across))  5.38 us
    ppermute x3, waiting for transfers between devices, on_device(): pieces = [attended] + [flipped('head', 4, j)(attended) for j in (1, 2, 3)]  5.15 us
    ppermute x3, starting transfers between devices, on_device(): pieces = [attended] + [flipped('head', 4, j)(attended) for j in (1, 2, 3)]  4.79 us
    ppermute x3, starting transfers between devices, on_device(): received = [flipped('head', 4, j)(r) for j, r in zip((1, 2, 3), outgoing)]  4.78 us
    pallas_call x3, Pallas kernels, attend(): pl.pallas_call(functools.partial(attend_kernel, blocks, first, last), out...  4.11 us
  transfers between devices with their start and end apart: 17, of which 10 were waited for; matrix products, arithmetic and copies ran while one was open for 0% of the time, Pallas kernels for 9%

profile of v7, /device:TPU:8, one launch (start us, length us, event | category | flops | bytes accessed | tf_op | source)
XLA Modules:
  0.0 61.0 jit_solution(15554876307544861332)
XLA Ops:
  0.0 2.2 %project.1 = (bf16[256,1024]{1,0:T(8,128)(2,1)S(1)}, bf16[512,256]{1,0:T(8,128)(2,1)S(1)}, bf16[128,1024]{1,0:T(8,128)(2,1)S(1)}) custom-call(bf16[256,1024]{1,0:T(8,128)(2,1)} %bitcast.4, bf16[1024,256]{1,0:T(8,128)(2,1)} %wk_hbm.1, bf16[1024,256]{1,0:T(8,128)(2,1)} %wv_hbm.1, bf16[256,1024]{1,0:T(8,128)(2,1)} %o0.1), custom_call_target="tpu_custom_call" | custom-call | flops 1000 | bytes 1000 | tf_op jit(solution)/shard_map/project/pallas_call | solution.py:126
  2.2 1.6 %collective-permute-start.10 = (bf16[128,1024]{1,0:T(8,128)(2,1)S(1)}, bf16[128,1024]{1,0:T(8,128)(2,1)S(1)}, u32[]{:S(2)}, u32[]{:S(2)}) collective-permute-start(bf16[128,1024]{1,0:T(8,128)(2,1)S(1)} %get-tuple-element.28.refs_0_), channel_id=1, source_target_pairs={{0,2},{2,0},{4,6},{6,4},{1,3},{3,1},{5,7},{7,5},{8,10},{10,8},{12,... | collective-permute-start | bytes 786440 | tf_op jit(solution)/shard_map/ppermute | solution.py:411
  3.8 2.3 %collective-permute-start.4 = (bf16[512,256]{1,0:T(8,128)(2,1)S(1)}, bf16[512,256]{1,0:T(8,128)(2,1)S(1)}, u32[]{:S(2)}, u32[]{:S(2)}) collective-permute-start(bf16[512,256]{1,0:T(8,128)(2,1)S(1)} %get-tuple-element.21.refs_0_), channel_id=1, source_target_pairs={{0,32},{8,40},{16,48},{24,56},{32,0},{40,8},{48,16},{56,24},{64,96... | collective-permute-start | bytes 786440 | tf_op jit(solution)/shard_map/ppermute | solution.py:409
  6.1 6.5 %collective-permute-start.1 = (bf16[512,256]{1,0:T(8,128)(2,1)S(1)}, bf16[512,256]{1,0:T(8,128)(2,1)S(1)}, u32[]{:S(2)}, u32[]{:S(2)}) collective-permute-start(bf16[512,256]{1,0:T(8,128)(2,1)S(1)} %get-tuple-element.21.refs_0_), channel_id=1, source_target_pairs={{0,16},{16,0},{8,24},{24,8},{32,48},{48,32},{40,56},{56,40},{64,80... | collective-permute-start | bytes 786440 | tf_op jit(solution)/shard_map/ppermute | solution.py:408
  12.6 0.3 ask.1.q_ref.refs_3_
  12.9 0.8 %biases.1.bias_ref.refs_2_ = f32[32,128]{1,0:T(8,128)S(1)} custom-call(s32[2,8]{1,0:T(2,128)S(1)} %bitcast.3, s32[2]{0:T(128)S(1)} %copy-done.5, bf16[256,1024]{1,0:T(8,128)(2,1)S(1)} %get-tuple-element.20.after_ref.x_ref), custom_call_target="tpu_custom_call" | custom-call | flops 1000 | bytes 1000 | tf_op jit(solution)/shard_map/biases/pallas_call | solution.py:96
  13.7 2.2 %collective-permute-start.11 = (bf16[256,1024]{1,0:T(8,128)(2,1)S(1)}, bf16[256,1024]{1,0:T(8,128)(2,1)S(1)}, u32[]{:S(2)}, u32[]{:S(2)}) collective-permute-start(bf16[256,1024]{1,0:T(8,128)(2,1)S(1)} %stack.2), channel_id=1, source_target_pairs={{0,6},{2,4},{4,2},{6,0},{1,7},{3,5},{5,3},{7,1},{8,14},{10,12},{12... | collective-permute-start | bytes 1572872 | tf_op jit(solution)/shard_map/ppermute | solution.py:415
  15.9 0.6 collective-permute-start.5
  16.5 1.0 %attend.3 = (f32[512,128]{1,0:T(8,128)S(1)}, f32[4,512]{1,0:T(4,128)S(1)}) custom-call(f32[32,128]{1,0:T(8,128)S(1)} %biases.1.bias_ref.refs_2_, bf16[256,256]{1,0:T(8,128)(2,1)S(1)} %ask.1.q_ref.refs_3_, bf16[512,256]{1,0:T(8,128)(2,1)S(1)} %get-tuple-element.21.refs_0_), custom_call_target="tpu_custom_call" | custom-call | flops 1000 | bytes 1000 | tf_op jit(solution)/shard_map/attend/pallas_call | solution.py:225
  17.5 1.2 %collective-permute-done.a_ref.refs_1_ = bf16[512,256]{1,0:T(8,128)(2,1)S(1)} collective-permute-done((bf16[512,256]{1,0:T(8,128)(2,1)S(1)}, bf16[512,256]{1,0:T(8,128)(2,1)S(1)}, u32[]{:S(2)}, u32[]{:S(2)}) %collective-permute-start) | collective-permute-done | bytes 262176 | tf_op jit(solution)/shard_map/ppermute | solution.py:408
  18.7 0.2 collective-permute-done.1.b_ref.refs_2_
  19.0 0.5 collective-permute-start.3
  19.5 1.5 %attend.4 = (f32[512,128]{1,0:T(8,128)S(1)}, f32[4,512]{1,0:T(4,128)S(1)}) custom-call(f32[32,128]{1,0:T(8,128)S(1)} %biases.1.bias_ref.refs_2_, bf16[256,256]{1,0:T(8,128)(2,1)S(1)} %ask.1.q_ref.refs_3_, bf16[512,256]{1,0:T(8,128)(2,1)S(1)} %collective-permute-done.6.refs_0_, bf16[512,256]{1,0:T(8,128)(2,1)S(1)} %collective-permute-done.a_ref.refs_1_, ...), custom_call_target="tpu_custom_call" | custom-call | flops 1000 | bytes 1000 | tf_op jit(solution)/shard_map/attend/pallas_call | solution.py:225
  21.0 5.4 %collective-permute-done.5.refs_3_ = bf16[512,256]{1,0:T(8,128)(2,1)S(1)} collective-permute-done((bf16[512,256]{1,0:T(8,128)(2,1)S(1)}, bf16[512,256]{1,0:T(8,128)(2,1)S(1)}, u32[]{:S(2)}, u32[]{:S(2)}) %collective-permute-start.5) | collective-permute-done | bytes 262176 | tf_op jit(solution)/shard_map/ppermute | solution.py:410
  26.4 1.6 %attend.5.a0.refs_2_ = bf16[256,256]{1,0:T(8,128)(2,1)S(1)} custom-call(f32[32,128]{1,0:T(8,128)S(1)} %biases.1.bias_ref.refs_2_, bf16[256,256]{1,0:T(8,128)(2,1)S(1)} %ask.1.q_ref.refs_3_, bf16[256,256]{1,0:T(8,128)(2,1)S(1)} %collective-permute-done.2.refs_0_, bf16[256,256]{1,0:T(8,128)(2,1)S(1)} %collective-permute-done.3.refs_1_, ...), custom_call_target="tpu_custom_call" | custom-call | flops 1000 | bytes 1000 | tf_op jit(solution)/shard_map/attend/pallas_call | solution.py:225
  28.0 0.7 %collective-permute-start.7 = (bf16[256,256]{1,0:T(8,128)(2,1)S(1)}, bf16[256,256]{1,0:T(8,128)(2,1)S(1)}, u32[]{:S(2)}, u32[]{:S(2)}) collective-permute-start(bf16[256,256]{1,0:T(8,128)(2,1)S(1)} %attend.5.a0.refs_2_), channel_id=1, source_target_pairs={{0,2},{2,0},{4,6},{6,4},{1,3},{3,1},{5,7},{7,5},{8,10},{10,8},{12,... | collective-permute-start | bytes 393224 | tf_op jit(solution)/shard_map/ppermute | solution.py:423
  28.7 2.0 %collective-permute-start.8 = (bf16[256,256]{1,0:T(8,128)(2,1)S(1)}, bf16[256,256]{1,0:T(8,128)(2,1)S(1)}, u32[]{:S(2)}, u32[]{:S(2)}) collective-permute-start(bf16[256,256]{1,0:T(8,128)(2,1)S(1)} %attend.5.a0.refs_2_), channel_id=1, source_target_pairs={{0,4},{2,6},{4,0},{6,2},{1,5},{3,7},{5,1},{7,3},{8,12},{10,14},{12... | collective-permute-start | bytes 393224 | tf_op jit(solution)/shard_map/ppermute | solution.py:423
  30.7 2.1 %collective-permute-start.9 = (bf16[256,256]{1,0:T(8,128)(2,1)S(1)}, bf16[256,256]{1,0:T(8,128)(2,1)S(1)}, u32[]{:S(2)}, u32[]{:S(2)}) collective-permute-start(bf16[256,256]{1,0:T(8,128)(2,1)S(1)} %attend.5.a0.refs_2_), channel_id=1, source_target_pairs={{0,6},{2,4},{4,2},{6,0},{1,7},{3,5},{5,3},{7,1},{8,14},{10,12},{12... | collective-permute-start | bytes 393224 | tf_op jit(solution)/shard_map/ppermute | solution.py:423
  32.9 0.3 collective-permute-start.12
  33.2 1.3 %collective-permute-done.7.a1 = bf16[256,256]{1,0:T(8,128)(2,1)S(1)} collective-permute-done((bf16[256,256]{1,0:T(8,128)(2,1)S(1)}, bf16[256,256]{1,0:T(8,128)(2,1)S(1)}, u32[]{:S(2)}, u32[]{:S(2)}) %collective-permute-start.7) | collective-permute-done | bytes 131104 | tf_op jit(solution)/shard_map/ppermute | solution.py:423
  34.5 2.1 %collective-permute-done.8.a2 = bf16[256,256]{1,0:T(8,128)(2,1)S(1)} collective-permute-done((bf16[256,256]{1,0:T(8,128)(2,1)S(1)}, bf16[256,256]{1,0:T(8,128)(2,1)S(1)}, u32[]{:S(2)}, u32[]{:S(2)}) %collective-permute-start.8) | collective-permute-done | bytes 131104 | tf_op jit(solution)/shard_map/ppermute | solution.py:423
  36.6 1.8 %collective-permute-done.9.a3 = bf16[256,256]{1,0:T(8,128)(2,1)S(1)} collective-permute-done((bf16[256,256]{1,0:T(8,128)(2,1)S(1)}, bf16[256,256]{1,0:T(8,128)(2,1)S(1)}, u32[]{:S(2)}, u32[]{:S(2)}) %collective-permute-start.9) | collective-permute-done | bytes 131104 | tf_op jit(solution)/shard_map/ppermute | solution.py:423
  38.3 0.1 lay.1.left_ref
  38.5 2.2 %feed.1 = (f32[64,1024]{1,0:T(8,128)S(1)}, bf16[64,1024]{1,0:T(8,128)(2,1)S(1)}, bf16[64,1024]{1,0:T(8,128)(2,1)S(1)}, bf16[64,1024]{1,0:T(8,128)(2,1)S(1)}) custom-call(bf16[256,1024]{1,0:T(8,128)(2,1)S(1)} %get-tuple-element.20.after_ref.x_ref, bf16[256,1024]{1,0:T(8,128)(2,1)S(1)} %lay.1.left_ref, bf16[256,1024]{1,0:T(8,128)(2,1)S(1)} %copy-done, ...), custom_call_target="tpu_custom_call" | custom-call | flops 1000 | bytes 1000 | tf_op jit(solution)/shard_map/feed/pallas_call | solution.py:341
  40.8 3.9 %collective-permute-start.14 = (bf16[64,1024]{1,0:T(8,128)(2,1)S(1)}, bf16[64,1024]{1,0:T(8,128)(2,1)S(1)}, u32[]{:S(2)}, u32[]{:S(2)}) collective-permute-start(bf16[64,1024]{1,0:T(8,128)(2,1)S(1)} %get-tuple-element.31), channel_id=1, source_target_pairs={{0,4},{2,6},{4,0},{6,2},{1,5},{3,7},{5,1},{7,3},{8,12},{10,14},{12... | collective-permute-start | bytes 393224 | tf_op jit(solution)/shard_map/ppermute | solution.py:425
  44.7 0.7 %collective-permute-start.15 = (bf16[64,1024]{1,0:T(8,128)(2,1)S(1)}, bf16[64,1024]{1,0:T(8,128)(2,1)S(1)}, u32[]{:S(2)}, u32[]{:S(2)}) collective-permute-start(bf16[64,1024]{1,0:T(8,128)(2,1)S(1)} %get-tuple-element.32), channel_id=1, source_target_pairs={{0,6},{2,4},{4,2},{6,0},{1,7},{3,5},{5,3},{7,1},{8,14},{10,12},{12... | collective-permute-start | bytes 393224 | tf_op jit(solution)/shard_map/ppermute | solution.py:425
  45.5 1.4 %collective-permute-done.13.r1 = bf16[64,1024]{1,0:T(8,128)(2,1)S(1)} collective-permute-done((bf16[64,1024]{1,0:T(8,128)(2,1)S(1)}, bf16[64,1024]{1,0:T(8,128)(2,1)S(1)}, u32[]{:S(2)}, u32[]{:S(2)}) %collective-permute-start.13) | collective-permute-done | bytes 131104 | tf_op jit(solution)/shard_map/ppermute | solution.py:425
  46.9 3.4 %collective-permute-done.14.r2 = bf16[64,1024]{1,0:T(8,128)(2,1)S(1)} collective-permute-done((bf16[64,1024]{1,0:T(8,128)(2,1)S(1)}, bf16[64,1024]{1,0:T(8,128)(2,1)S(1)}, u32[]{:S(2)}, u32[]{:S(2)}) %collective-permute-start.14) | collective-permute-done | bytes 131104 | tf_op jit(solution)/shard_map/ppermute | solution.py:425
  50.3 1.7 %collective-permute-done.15.r3 = bf16[64,1024]{1,0:T(8,128)(2,1)S(1)} collective-permute-done((bf16[64,1024]{1,0:T(8,128)(2,1)S(1)}, bf16[64,1024]{1,0:T(8,128)(2,1)S(1)}, u32[]{:S(2)}, u32[]{:S(2)}) %collective-permute-start.15) | collective-permute-done | bytes 131104 | tf_op jit(solution)/shard_map/ppermute | solution.py:425
  52.1 1.7 %collective-permute-start.16 = (bf16[32,1024]{1,0:T(8,128)(2,1)S(1)}, bf16[32,1024]{1,0:T(8,128)(2,1)S(1)}, u32[]{:S(2)}, u32[]{:S(2)}) collective-permute-start(bf16[32,1024]{1,0:T(8,128)(2,1)S(1)} %get-tuple-element.34), channel_id=1, source_target_pairs={{0,1},{1,0},{2,3},{3,2},{4,5},{5,4},{6,7},{7,6},{8,9},{9,8},{10,11... | collective-permute-start | bytes 196616 | tf_op jit(solution)/shard_map/ppermute | solution.py:427
  54.4 5.9 %collective-permute-done.16.other_ref = bf16[32,1024]{1,0:T(8,128)(2,1)S(1)} collective-permute-done((bf16[32,1024]{1,0:T(8,128)(2,1)S(1)}, bf16[32,1024]{1,0:T(8,128)(2,1)S(1)}, u32[]{:S(2)}, u32[]{:S(2)}) %collective-permute-start.16) | collective-permute-done | bytes 65568 | tf_op jit(solution)/shard_map/ppermute | solution.py:427
  60.3 0.7 %guide.1 = bf16[32,1024]{1,0:T(8,128)(2,1)} custom-call(f32[1]{0:T(128)S(6)} %copy.11.guidance_ref, f32[32,1024]{1,0:T(8,128)S(1)} %get-tuple-element.33.kept_ref, bf16[32,1024]{1,0:T(8,128)(2,1)S(1)} %collective-permute-done.16.other_ref), custom_call_target="tpu_custom_call" | custom-call | flops 1000 | bytes 1000 | tf_op jit(solution)/shard_map/guide/pallas_call | solution.py:390
  (27 shorter events, 0.4 us)
Async XLA Ops:
  0.0 12.6 %copy-start.3 = (bf16[1024,256]{1,0:T(8,128)(2,1)S(1)}, bf16[1024,256]{1,0:T(8,128)(2,1)}, u32[]{:S(2)}) copy-start(bf16[1024,256]{1,0:T(8,128)(2,1)} %wq_ref.1) | copy-start | bytes 1572868
  0.0 12.9 %copy-start.4 = (s32[8,2]{0,1:T(2,128)S(1)}, s32[8,2]{0,1:T(2,128)}, u32[]{:S(2)}) copy-start(s32[8,2]{0,1:T(2,128)} %param.11) | copy-start | bytes 196
  0.0 12.9 %copy-start.5 = (s32[2]{0:T(128)S(1)}, s32[2]{0:T(128)}, u32[]{:S(2)}) copy-start(s32[2]{0:T(128)} %counts_ref.1) | copy-start | bytes 28
  2.2 11.4 %collective-permute-start.10 = (bf16[128,1024]{1,0:T(8,128)(2,1)S(1)}, bf16[128,1024]{1,0:T(8,128)(2,1)S(1)}, u32[]{:S(2)}, u32[]{:S(2)}) collective-permute-start(bf16[128,1024]{1,0:T(8,128)(2,1)S(1)} %get-tuple-element.28.refs_0_), channel_id=1, source_target_pairs={{0,2},{2,0},{4,6},{6,4},{1,3},{3,1},{5,7},{7,5},{8,10},{10,8},{12,... | collective-permute-start | bytes 786440 | tf_op jit(solution)/shard_map/ppermute | solution.py:411
  3.8 12.1 %collective-permute-start.4 = (bf16[512,256]{1,0:T(8,128)(2,1)S(1)}, bf16[512,256]{1,0:T(8,128)(2,1)S(1)}, u32[]{:S(2)}, u32[]{:S(2)}) collective-permute-start(bf16[512,256]{1,0:T(8,128)(2,1)S(1)} %get-tuple-element.21.refs_0_), channel_id=1, source_target_pairs={{0,32},{8,40},{16,48},{24,56},{32,0},{40,8},{48,16},{56,24},{64,96... | collective-permute-start | bytes 786440 | tf_op jit(solution)/shard_map/ppermute | solution.py:409
  6.1 12.6 %collective-permute-start = (bf16[512,256]{1,0:T(8,128)(2,1)S(1)}, bf16[512,256]{1,0:T(8,128)(2,1)S(1)}, u32[]{:S(2)}, u32[]{:S(2)}) collective-permute-start(bf16[512,256]{1,0:T(8,128)(2,1)S(1)} %get-tuple-element.21.refs_0_), channel_id=1, source_target_pairs={{16,32},{32,16},{24,40},{40,24},{48,64},{64,48},{56,72},{72,56},{8... | collective-permute-start | bytes 786440 | tf_op jit(solution)/shard_map/ppermute | solution.py:408
  6.1 12.7 %collective-permute-start.1 = (bf16[512,256]{1,0:T(8,128)(2,1)S(1)}, bf16[512,256]{1,0:T(8,128)(2,1)S(1)}, u32[]{:S(2)}, u32[]{:S(2)}) collective-permute-start(bf16[512,256]{1,0:T(8,128)(2,1)S(1)} %get-tuple-element.21.refs_0_), channel_id=1, source_target_pairs={{0,16},{16,0},{8,24},{24,8},{32,48},{48,32},{40,56},{56,40},{64,80... | collective-permute-start | bytes 786440 | tf_op jit(solution)/shard_map/ppermute | solution.py:408
  13.7 19.1 %collective-permute-start.11 = (bf16[256,1024]{1,0:T(8,128)(2,1)S(1)}, bf16[256,1024]{1,0:T(8,128)(2,1)S(1)}, u32[]{:S(2)}, u32[]{:S(2)}) collective-permute-start(bf16[256,1024]{1,0:T(8,128)(2,1)S(1)} %stack.2), channel_id=1, source_target_pairs={{0,6},{2,4},{4,2},{6,0},{1,7},{3,5},{5,3},{7,1},{8,14},{10,12},{12... | collective-permute-start | bytes 1572872 | tf_op jit(solution)/shard_map/ppermute | solution.py:415
  15.9 3.6 %collective-permute-start.6 = (bf16[512,256]{1,0:T(8,128)(2,1)S(1)}, bf16[512,256]{1,0:T(8,128)(2,1)S(1)}, u32[]{:S(2)}, u32[]{:S(2)}) collective-permute-start(bf16[512,256]{1,0:T(8,128)(2,1)S(1)} %get-tuple-element.21.refs_0_), channel_id=1, source_target_pairs={{0,8},{8,0},{16,24},{24,16},{32,40},{40,32},{48,56},{56,48},{64,72... | collective-permute-start | bytes 786440 | tf_op jit(solution)/shard_map/ppermute | solution.py:417
  15.9 10.5 %collective-permute-start.5 = (bf16[512,256]{1,0:T(8,128)(2,1)S(1)}, bf16[512,256]{1,0:T(8,128)(2,1)S(1)}, u32[]{:S(2)}, u32[]{:S(2)}) collective-permute-start(bf16[512,256]{1,0:T(8,128)(2,1)S(1)} %collective-permute-done.4.refs_2_), channel_id=1, source_target_pairs={{0,64},{8,72},{16,80},{24,88},{32,224},{40,232},{48,240},{56,248},... | collective-permute-start | bytes 786440 | tf_op jit(solution)/shard_map/ppermute | solution.py:410
  18.9 2.1 %collective-permute-start.2 = (bf16[256,256]{1,0:T(8,128)(2,1)S(1)}, bf16[256,256]{1,0:T(8,128)(2,1)S(1)}, u32[]{:S(2)}, u32[]{:S(2)}) collective-permute-start(bf16[256,256]{1,0:T(8,128)(2,1)S(1)} %get-tuple-element.23), channel_id=1, source_target_pairs={{0,8},{8,0},{16,24},{24,16},{32,40},{40,32},{48,56},{56,48},{64,72... | collective-permute-start | bytes 393224 | tf_op jit(solution)/shard_map/ppermute | solution.py:418
  19.0 2.0 %collective-permute-start.3 = (bf16[256,256]{1,0:T(8,128)(2,1)S(1)}, bf16[256,256]{1,0:T(8,128)(2,1)S(1)}, u32[]{:S(2)}, u32[]{:S(2)}) collective-permute-start(bf16[256,256]{1,0:T(8,128)(2,1)S(1)} %get-tuple-element.24), channel_id=1, source_target_pairs={{0,8},{8,0},{16,24},{24,16},{32,40},{40,32},{48,56},{56,48},{64,72... | collective-permute-start | bytes 393224 | tf_op jit(solution)/shard_map/ppermute | solution.py:418
  28.0 6.5 %collective-permute-start.7 = (bf16[256,256]{1,0:T(8,128)(2,1)S(1)}, bf16[256,256]{1,0:T(8,128)(2,1)S(1)}, u32[]{:S(2)}, u32[]{:S(2)}) collective-permute-start(bf16[256,256]{1,0:T(8,128)(2,1)S(1)} %attend.5.a0.refs_2_), channel_id=1, source_target_pairs={{0,2},{2,0},{4,6},{6,4},{1,3},{3,1},{5,7},{7,5},{8,10},{10,8},{12,... | collective-permute-start | bytes 393224 | tf_op jit(solution)/shard_map/ppermute | solution.py:423
  28.7 7.9 %collective-permute-start.8 = (bf16[256,256]{1,0:T(8,128)(2,1)S(1)}, bf16[256,256]{1,0:T(8,128)(2,1)S(1)}, u32[]{:S(2)}, u32[]{:S(2)}) collective-permute-start(bf16[256,256]{1,0:T(8,128)(2,1)S(1)} %attend.5.a0.refs_2_), channel_id=1, source_target_pairs={{0,4},{2,6},{4,0},{6,2},{1,5},{3,7},{5,1},{7,3},{8,12},{10,14},{12... | collective-permute-start | bytes 393224 | tf_op jit(solution)/shard_map/ppermute | solution.py:423
  30.7 7.6 %collective-permute-start.9 = (bf16[256,256]{1,0:T(8,128)(2,1)S(1)}, bf16[256,256]{1,0:T(8,128)(2,1)S(1)}, u32[]{:S(2)}, u32[]{:S(2)}) collective-permute-start(bf16[256,256]{1,0:T(8,128)(2,1)S(1)} %attend.5.a0.refs_2_), channel_id=1, source_target_pairs={{0,6},{2,4},{4,2},{6,0},{1,7},{3,5},{5,3},{7,1},{8,14},{10,12},{12... | collective-permute-start | bytes 393224 | tf_op jit(solution)/shard_map/ppermute | solution.py:423
  32.9 5.6 %copy-start = (bf16[256,1024]{1,0:T(8,128)(2,1)S(1)}, bf16[256,1024]{1,0:T(8,128)(2,1)}, u32[]{:S(2)}) copy-start(bf16[256,1024]{1,0:T(8,128)(2,1)} %o0.1) | copy-start | bytes 1572868
  32.9 5.6 %copy-start.1 = (bf16[1024,1024]{1,0:T(8,128)(2,1)S(1)}, bf16[1024,1024]{1,0:T(8,128)(2,1)}, u32[]{:S(2)}) copy-start(bf16[1024,1024]{1,0:T(8,128)(2,1)} %win_ref.1) | copy-start | bytes 6291460
  32.9 5.6 %copy-start.2 = (bf16[1024,1024]{1,0:T(8,128)(2,1)S(1)}, bf16[1024,1024]{1,0:T(8,128)(2,1)}, u32[]{:S(2)}) copy-start(bf16[1024,1024]{1,0:T(8,128)(2,1)} %wback_ref.1) | copy-start | bytes 6291460
  32.9 5.6 %collective-permute-start.12 = (bf16[384,1024]{1,0:T(8,128)(2,1)S(1)}, bf16[384,1024]{1,0:T(8,128)(2,1)S(1)}, u32[]{:S(2)}, u32[]{:S(2)}) collective-permute-start(bf16[384,1024]{1,0:T(8,128)(2,1)S(1)} %stack.3), channel_id=1, source_target_pairs={{0,8},{8,0},{16,24},{24,16},{32,40},{40,32},{48,56},{56,48},{64,72... | collective-permute-start | bytes 2359304 | tf_op jit(solution)/shard_map/ppermute | solution.py:421
  40.7 6.2 %collective-permute-start.13 = (bf16[64,1024]{1,0:T(8,128)(2,1)S(1)}, bf16[64,1024]{1,0:T(8,128)(2,1)S(1)}, u32[]{:S(2)}, u32[]{:S(2)}) collective-permute-start(bf16[64,1024]{1,0:T(8,128)(2,1)S(1)} %get-tuple-element.30), channel_id=1, source_target_pairs={{0,2},{2,0},{4,6},{6,4},{1,3},{3,1},{5,7},{7,5},{8,10},{10,8},{12,... | collective-permute-start | bytes 393224 | tf_op jit(solution)/shard_map/ppermute | solution.py:425
  40.8 9.5 %collective-permute-start.14 = (bf16[64,1024]{1,0:T(8,128)(2,1)S(1)}, bf16[64,1024]{1,0:T(8,128)(2,1)S(1)}, u32[]{:S(2)}, u32[]{:S(2)}) collective-permute-start(bf16[64,1024]{1,0:T(8,128)(2,1)S(1)} %get-tuple-element.31), channel_id=1, source_target_pairs={{0,4},{2,6},{4,0},{6,2},{1,5},{3,7},{5,1},{7,3},{8,12},{10,14},{12... | collective-permute-start | bytes 393224 | tf_op jit(solution)/shard_map/ppermute | solution.py:425
  44.7 7.3 %collective-permute-start.15 = (bf16[64,1024]{1,0:T(8,128)(2,1)S(1)}, bf16[64,1024]{1,0:T(8,128)(2,1)S(1)}, u32[]{:S(2)}, u32[]{:S(2)}) collective-permute-start(bf16[64,1024]{1,0:T(8,128)(2,1)S(1)} %get-tuple-element.32), channel_id=1, source_target_pairs={{0,6},{2,4},{4,2},{6,0},{1,7},{3,5},{5,3},{7,1},{8,14},{10,12},{12... | collective-permute-start | bytes 393224 | tf_op jit(solution)/shard_map/ppermute | solution.py:425
  52.1 8.3 %collective-permute-start.16 = (bf16[32,1024]{1,0:T(8,128)(2,1)S(1)}, bf16[32,1024]{1,0:T(8,128)(2,1)S(1)}, u32[]{:S(2)}, u32[]{:S(2)}) collective-permute-start(bf16[32,1024]{1,0:T(8,128)(2,1)S(1)} %get-tuple-element.34), channel_id=1, source_target_pairs={{0,1},{1,0},{2,3},{3,2},{4,5},{5,4},{6,7},{7,6},{8,9},{9,8},{10,11... | collective-permute-start | bytes 196616 | tf_op jit(solution)/shard_map/ppermute | solution.py:427

commit v8 on v7

--- a/solution.py
+++ b/solution.py
@@ -10,7 +10,6 @@
 HD = 64
 ROUNDS = 8
 BIASES = 16
-DIAGONAL = (2, 3, 5, 6)
 MASKED = -1e30
 LOG2E = 1.4426950408889634
 
@@ -73,30 +72,25 @@
 
 
 def bias_kernel(count, partners_ref, counts_ref, after_ref, bias_ref):
-    bias_ref[...] = jnp.zeros_like(bias_ref)
-    firsts = key_views(count)
+    row = lax.broadcasted_iota(jnp.int32, (BIASES, bias_ref.shape[1]), 0)
+    keys = row & 1
+    for slot, first in enumerate(key_views(count)):
+        keys = keys + jnp.where(row >> 1 == slot, first, 0)
     for qv in range(2):
-        used = counts_ref[qv]
-        named = [jnp.where(r < used, partners_ref[qv, r], -1) for r in range(ROUNDS)]
-        for slot, first in enumerate(firsts):
-            for kvw in range(2):
-                if (slot in DIAGONAL or slot == 0) and (kvw == qv) == (slot == 0):
-                    continue
-                times = sum((n == first + kvw).astype(jnp.int32) for n in named)
-                row = BIASES * qv + 2 * slot + kvw
-                bias_ref[row : row + 1] = jnp.full((1, bias_ref.shape[1]), times.astype(jnp.float32))
-    times = bias_ref[...]
-    bias_ref[...] = jnp.where(times > 0, jnp.log2(jnp.maximum(times, 1.0)), MASKED)
-    for qv in range(2):
-        row = BIASES * qv + qv
-        bias_ref[row : row + 1] = jnp.zeros((1, bias_ref.shape[1]), jnp.float32)
+        used = counts_ref[0:1, qv : qv + 1]
+        times = jnp.where(row == qv, 1, 0)
+        for r in range(ROUNDS):
+            named = jnp.where(r < used, partners_ref[qv : qv + 1, r : r + 1], -1)
+            times = times + jnp.where(keys == named, 1, 0)
+        bias = jnp.log2(jnp.maximum(times, 1).astype(jnp.float32))
+        bias_ref[BIASES * qv : BIASES * (qv + 1)] = jnp.where(times > 0, bias, MASKED)
 
 
 def biases(count, partners, counts, after):
     return pl.pallas_call(
         functools.partial(bias_kernel, count),
         out_shape=held((2 * BIASES, 2 * HD), jnp.float32),
-        in_specs=[SMEM, SMEM, ANY],
+        in_specs=[VMEM, VMEM, ANY],
         out_specs=VMEM,
         compiler_params=params(2),
         cost_estimate=COST,
@@ -410,7 +404,7 @@
     far = (across, onward(count)(across))
     w_1 = flipped("head", 4, 1)(w_half)
     q = ask(x, w_query, x)
-    bias = biases(count, partners.T, counts, x)
+    bias = biases(count, partners.T, counts[None], x)
     state = attend(((0, 0, True),), True, False, bias, q, (kv,))
     w_32 = flipped("head", 4, 3)(stack(w_half, w_1, after=(bias, q)))
     other_core = flipped("view", count, 1)

time: 61.1 us -> 60.5 us (level)
  starting transfers between devices: 25.2 us -> 26.6 us
  waiting for transfers between devices: 24.4 us -> 23 us
    ppermute x1, starting transfers between devices: 1.69 us -> 2.46 us  [on_device(): other = flipped('branch', 2, 1)(sent)]
  transfers between devices with their start and end apart: 17 -> 17, of which waited for: 10 -> 10; matrix products, arithmetic and copies ran while one was open for 0% -> 0% of each run, Pallas kernels for 9% -> 8%
where the time goes in v8:
time: 60.5 us; the launch traced here: 60.4 us
  starting transfers between devices  26.6 us (44%)
  waiting for transfers between devices  23 us (38%)
  Pallas kernels  9.91 us (16%)
  between operations  0.87 us (1%)
    ppermute x3, waiting for transfers between devices, on_device(): received = [flipped('head', 4, j)(r) for j, r in zip((1, 2, 3), outgoing)]  6.59 us
    ppermute x2, starting transfers between devices, on_device(): near = [matched(count, 2, parity)(kv) for parity in (1, 0)]  6.46 us
    ppermute x1, waiting for transfers between devices, on_device(): other = flipped('branch', 2, 1)(sent)  5.34 us
    ppermute x3, waiting for transfers between devices, on_device(): pieces = [attended] + [flipped('head', 4, j)(attended) for j in (1, 2, 3)]  4.91 us
    ppermute x1, waiting for transfers between devices, on_device(): far = (across, onward(count)(across))  4.8 us
    ppermute x3, starting transfers between devices, on_device(): pieces = [attended] + [flipped('head', 4, j)(attended) for j in (1, 2, 3)]  4.79 us
    ppermute x3, starting transfers between devices, on_device(): received = [flipped('head', 4, j)(r) for j, r in zip((1, 2, 3), outgoing)]  4.78 us
    pallas_call x3, Pallas kernels, attend(): pl.pallas_call(functools.partial(attend_kernel, blocks, first, last), out...  4.11 us
  transfers between devices with their start and end apart: 17, of which 10 were waited for; matrix products, arithmetic and copies ran while one was open for 0% of the time, Pallas kernels for 8%

profile of v8, /device:TPU:8, one launch (start us, length us, event | category | flops | bytes accessed | tf_op | source)
XLA Modules:
  0.0 60.4 jit_solution(11484053537312510076)
XLA Ops:
  0.0 2.2 %project.1 = (bf16[256,1024]{1,0:T(8,128)(2,1)S(1)}, bf16[512,256]{1,0:T(8,128)(2,1)S(1)}, bf16[128,1024]{1,0:T(8,128)(2,1)S(1)}) custom-call(bf16[256,1024]{1,0:T(8,128)(2,1)} %bitcast.6, bf16[1024,256]{1,0:T(8,128)(2,1)} %wk_hbm.1, bf16[1024,256]{1,0:T(8,128)(2,1)} %wv_hbm.1, bf16[256,1024]{1,0:T(8,128)(2,1)} %o0.1), custom_call_target="tpu_custom_call" | custom-call | flops 1000 | bytes 1000 | tf_op jit(solution)/shard_map/project/pallas_call | solution.py:120
  2.2 1.6 %collective-permute-start.10 = (bf16[128,1024]{1,0:T(8,128)(2,1)S(1)}, bf16[128,1024]{1,0:T(8,128)(2,1)S(1)}, u32[]{:S(2)}, u32[]{:S(2)}) collective-permute-start(bf16[128,1024]{1,0:T(8,128)(2,1)S(1)} %get-tuple-element.28.refs_0_), channel_id=1, source_target_pairs={{0,2},{2,0},{4,6},{6,4},{1,3},{3,1},{5,7},{7,5},{8,10},{10,8},{12,... | collective-permute-start | bytes 786440 | tf_op jit(solution)/shard_map/ppermute | solution.py:405
  3.8 2.3 %collective-permute-start.4 = (bf16[512,256]{1,0:T(8,128)(2,1)S(1)}, bf16[512,256]{1,0:T(8,128)(2,1)S(1)}, u32[]{:S(2)}, u32[]{:S(2)}) collective-permute-start(bf16[512,256]{1,0:T(8,128)(2,1)S(1)} %get-tuple-element.21.refs_0_), channel_id=1, source_target_pairs={{0,32},{8,40},{16,48},{24,56},{32,0},{40,8},{48,16},{56,24},{64,96... | collective-permute-start | bytes 786440 | tf_op jit(solution)/shard_map/ppermute | solution.py:403
  6.1 6.5 %collective-permute-start.1 = (bf16[512,256]{1,0:T(8,128)(2,1)S(1)}, bf16[512,256]{1,0:T(8,128)(2,1)S(1)}, u32[]{:S(2)}, u32[]{:S(2)}) collective-permute-start(bf16[512,256]{1,0:T(8,128)(2,1)S(1)} %get-tuple-element.21.refs_0_), channel_id=1, source_target_pairs={{0,16},{16,0},{8,24},{24,8},{32,48},{48,32},{40,56},{56,40},{64,80... | collective-permute-start | bytes 786440 | tf_op jit(solution)/shard_map/ppermute | solution.py:402
  12.6 0.3 ask.1.q_ref.refs_3_
  12.9 0.2 biases.1.bias_ref.refs_2_
  13.1 2.2 %collective-permute-start.11 = (bf16[256,1024]{1,0:T(8,128)(2,1)S(1)}, bf16[256,1024]{1,0:T(8,128)(2,1)S(1)}, u32[]{:S(2)}, u32[]{:S(2)}) collective-permute-start(bf16[256,1024]{1,0:T(8,128)(2,1)S(1)} %stack.2), channel_id=1, source_target_pairs={{0,6},{2,4},{4,2},{6,0},{1,7},{3,5},{5,3},{7,1},{8,14},{10,12},{12... | collective-permute-start | bytes 1572872 | tf_op jit(solution)/shard_map/ppermute | solution.py:409
  15.3 1.2 %collective-permute-start.5 = (bf16[512,256]{1,0:T(8,128)(2,1)S(1)}, bf16[512,256]{1,0:T(8,128)(2,1)S(1)}, u32[]{:S(2)}, u32[]{:S(2)}) collective-permute-start(bf16[512,256]{1,0:T(8,128)(2,1)S(1)} %collective-permute-done.4.refs_2_), channel_id=1, source_target_pairs={{0,64},{8,72},{16,80},{24,88},{32,224},{40,232},{48,240},{56,248},... | collective-permute-start | bytes 786440 | tf_op jit(solution)/shard_map/ppermute | solution.py:404
  16.5 1.0 %attend.3 = (f32[512,128]{1,0:T(8,128)S(1)}, f32[4,512]{1,0:T(4,128)S(1)}) custom-call(f32[32,128]{1,0:T(8,128)S(1)} %biases.1.bias_ref.refs_2_, bf16[256,256]{1,0:T(8,128)(2,1)S(1)} %ask.1.q_ref.refs_3_, bf16[512,256]{1,0:T(8,128)(2,1)S(1)} %get-tuple-element.21.refs_0_), custom_call_target="tpu_custom_call" | custom-call | flops 1000 | bytes 1000 | tf_op jit(solution)/shard_map/attend/pallas_call | solution.py:219
  17.5 1.2 %collective-permute-done.a_ref.refs_1_ = bf16[512,256]{1,0:T(8,128)(2,1)S(1)} collective-permute-done((bf16[512,256]{1,0:T(8,128)(2,1)S(1)}, bf16[512,256]{1,0:T(8,128)(2,1)S(1)}, u32[]{:S(2)}, u32[]{:S(2)}) %collective-permute-start) | collective-permute-done | bytes 262176 | tf_op jit(solution)/shard_map/ppermute | solution.py:402
  18.7 0.2 collective-permute-done.1.b_ref.refs_2_
  19.0 0.5 collective-permute-start.3
  19.5 1.5 %attend.4 = (f32[512,128]{1,0:T(8,128)S(1)}, f32[4,512]{1,0:T(4,128)S(1)}) custom-call(f32[32,128]{1,0:T(8,128)S(1)} %biases.1.bias_ref.refs_2_, bf16[256,256]{1,0:T(8,128)(2,1)S(1)} %ask.1.q_ref.refs_3_, bf16[512,256]{1,0:T(8,128)(2,1)S(1)} %collective-permute-done.6.refs_0_, bf16[512,256]{1,0:T(8,128)(2,1)S(1)} %collective-permute-done.a_ref.refs_1_, ...), custom_call_target="tpu_custom_call" | custom-call | flops 1000 | bytes 1000 | tf_op jit(solution)/shard_map/attend/pallas_call | solution.py:219
  21.0 4.8 %collective-permute-done.5.refs_3_ = bf16[512,256]{1,0:T(8,128)(2,1)S(1)} collective-permute-done((bf16[512,256]{1,0:T(8,128)(2,1)S(1)}, bf16[512,256]{1,0:T(8,128)(2,1)S(1)}, u32[]{:S(2)}, u32[]{:S(2)}) %collective-permute-start.5) | collective-permute-done | bytes 262176 | tf_op jit(solution)/shard_map/ppermute | solution.py:404
  25.8 1.6 %attend.5.a0.refs_2_ = bf16[256,256]{1,0:T(8,128)(2,1)S(1)} custom-call(f32[32,128]{1,0:T(8,128)S(1)} %biases.1.bias_ref.refs_2_, bf16[256,256]{1,0:T(8,128)(2,1)S(1)} %ask.1.q_ref.refs_3_, bf16[256,256]{1,0:T(8,128)(2,1)S(1)} %collective-permute-done.2.refs_0_, bf16[256,256]{1,0:T(8,128)(2,1)S(1)} %collective-permute-done.3.refs_1_, ...), custom_call_target="tpu_custom_call" | custom-call | flops 1000 | bytes 1000 | tf_op jit(solution)/shard_map/attend/pallas_call | solution.py:219
  27.4 0.7 %collective-permute-start.7 = (bf16[256,256]{1,0:T(8,128)(2,1)S(1)}, bf16[256,256]{1,0:T(8,128)(2,1)S(1)}, u32[]{:S(2)}, u32[]{:S(2)}) collective-permute-start(bf16[256,256]{1,0:T(8,128)(2,1)S(1)} %attend.5.a0.refs_2_), channel_id=1, source_target_pairs={{0,2},{2,0},{4,6},{6,4},{1,3},{3,1},{5,7},{7,5},{8,10},{10,8},{12,... | collective-permute-start | bytes 393224 | tf_op jit(solution)/shard_map/ppermute | solution.py:417
  28.1 2.0 %collective-permute-start.8 = (bf16[256,256]{1,0:T(8,128)(2,1)S(1)}, bf16[256,256]{1,0:T(8,128)(2,1)S(1)}, u32[]{:S(2)}, u32[]{:S(2)}) collective-permute-start(bf16[256,256]{1,0:T(8,128)(2,1)S(1)} %attend.5.a0.refs_2_), channel_id=1, source_target_pairs={{0,4},{2,6},{4,0},{6,2},{1,5},{3,7},{5,1},{7,3},{8,12},{10,14},{12... | collective-permute-start | bytes 393224 | tf_op jit(solution)/shard_map/ppermute | solution.py:417
  30.1 2.1 %collective-permute-start.9 = (bf16[256,256]{1,0:T(8,128)(2,1)S(1)}, bf16[256,256]{1,0:T(8,128)(2,1)S(1)}, u32[]{:S(2)}, u32[]{:S(2)}) collective-permute-start(bf16[256,256]{1,0:T(8,128)(2,1)S(1)} %attend.5.a0.refs_2_), channel_id=1, source_target_pairs={{0,6},{2,4},{4,2},{6,0},{1,7},{3,5},{5,3},{7,1},{8,14},{10,12},{12... | collective-permute-start | bytes 393224 | tf_op jit(solution)/shard_map/ppermute | solution.py:417
  32.3 0.3 collective-permute-start.12
  32.6 1.3 %collective-permute-done.7.a1 = bf16[256,256]{1,0:T(8,128)(2,1)S(1)} collective-permute-done((bf16[256,256]{1,0:T(8,128)(2,1)S(1)}, bf16[256,256]{1,0:T(8,128)(2,1)S(1)}, u32[]{:S(2)}, u32[]{:S(2)}) %collective-permute-start.7) | collective-permute-done | bytes 131104 | tf_op jit(solution)/shard_map/ppermute | solution.py:417
  33.9 2.0 %collective-permute-done.8.a2 = bf16[256,256]{1,0:T(8,128)(2,1)S(1)} collective-permute-done((bf16[256,256]{1,0:T(8,128)(2,1)S(1)}, bf16[256,256]{1,0:T(8,128)(2,1)S(1)}, u32[]{:S(2)}, u32[]{:S(2)}) %collective-permute-start.8) | collective-permute-done | bytes 131104 | tf_op jit(solution)/shard_map/ppermute | solution.py:417
  36.0 1.5 %collective-permute-done.9.a3 = bf16[256,256]{1,0:T(8,128)(2,1)S(1)} collective-permute-done((bf16[256,256]{1,0:T(8,128)(2,1)S(1)}, bf16[256,256]{1,0:T(8,128)(2,1)S(1)}, u32[]{:S(2)}, u32[]{:S(2)}) %collective-permute-start.9) | collective-permute-done | bytes 131104 | tf_op jit(solution)/shard_map/ppermute | solution.py:417
  37.5 0.1 lay.1.left_ref
  37.7 2.2 %feed.1 = (f32[64,1024]{1,0:T(8,128)S(1)}, bf16[64,1024]{1,0:T(8,128)(2,1)S(1)}, bf16[64,1024]{1,0:T(8,128)(2,1)S(1)}, bf16[64,1024]{1,0:T(8,128)(2,1)S(1)}) custom-call(bf16[256,1024]{1,0:T(8,128)(2,1)S(1)} %get-tuple-element.20.after_ref.x_ref, bf16[256,1024]{1,0:T(8,128)(2,1)S(1)} %lay.1.left_ref, bf16[256,1024]{1,0:T(8,128)(2,1)S(1)} %copy-done, ...), custom_call_target="tpu_custom_call" | custom-call | flops 1000 | bytes 1000 | tf_op jit(solution)/shard_map/feed/pallas_call | solution.py:335
  40.0 4.1 %collective-permute-start.14 = (bf16[64,1024]{1,0:T(8,128)(2,1)S(1)}, bf16[64,1024]{1,0:T(8,128)(2,1)S(1)}, u32[]{:S(2)}, u32[]{:S(2)}) collective-permute-start(bf16[64,1024]{1,0:T(8,128)(2,1)S(1)} %get-tuple-element.31), channel_id=1, source_target_pairs={{0,4},{2,6},{4,0},{6,2},{1,5},{3,7},{5,1},{7,3},{8,12},{10,14},{12... | collective-permute-start | bytes 393224 | tf_op jit(solution)/shard_map/ppermute | solution.py:419
  44.0 0.6 %collective-permute-start.15 = (bf16[64,1024]{1,0:T(8,128)(2,1)S(1)}, bf16[64,1024]{1,0:T(8,128)(2,1)S(1)}, u32[]{:S(2)}, u32[]{:S(2)}) collective-permute-start(bf16[64,1024]{1,0:T(8,128)(2,1)S(1)} %get-tuple-element.32), channel_id=1, source_target_pairs={{0,6},{2,4},{4,2},{6,0},{1,7},{3,5},{5,3},{7,1},{8,14},{10,12},{12... | collective-permute-start | bytes 393224 | tf_op jit(solution)/shard_map/ppermute | solution.py:419
  44.7 1.4 %collective-permute-done.13.r1 = bf16[64,1024]{1,0:T(8,128)(2,1)S(1)} collective-permute-done((bf16[64,1024]{1,0:T(8,128)(2,1)S(1)}, bf16[64,1024]{1,0:T(8,128)(2,1)S(1)}, u32[]{:S(2)}, u32[]{:S(2)}) %collective-permute-start.13) | collective-permute-done | bytes 131104 | tf_op jit(solution)/shard_map/ppermute | solution.py:419
  46.1 3.4 %collective-permute-done.14.r2 = bf16[64,1024]{1,0:T(8,128)(2,1)S(1)} collective-permute-done((bf16[64,1024]{1,0:T(8,128)(2,1)S(1)}, bf16[64,1024]{1,0:T(8,128)(2,1)S(1)}, u32[]{:S(2)}, u32[]{:S(2)}) %collective-permute-start.14) | collective-permute-done | bytes 131104 | tf_op jit(solution)/shard_map/ppermute | solution.py:419
  49.5 1.7 %collective-permute-done.15.r3 = bf16[64,1024]{1,0:T(8,128)(2,1)S(1)} collective-permute-done((bf16[64,1024]{1,0:T(8,128)(2,1)S(1)}, bf16[64,1024]{1,0:T(8,128)(2,1)S(1)}, u32[]{:S(2)}, u32[]{:S(2)}) %collective-permute-start.15) | collective-permute-done | bytes 131104 | tf_op jit(solution)/shard_map/ppermute | solution.py:419
  51.3 2.5 %collective-permute-start.16 = (bf16[32,1024]{1,0:T(8,128)(2,1)S(1)}, bf16[32,1024]{1,0:T(8,128)(2,1)S(1)}, u32[]{:S(2)}, u32[]{:S(2)}) collective-permute-start(bf16[32,1024]{1,0:T(8,128)(2,1)S(1)} %get-tuple-element.34), channel_id=1, source_target_pairs={{0,1},{1,0},{2,3},{3,2},{4,5},{5,4},{6,7},{7,6},{8,9},{9,8},{10,11... | collective-permute-start | bytes 196616 | tf_op jit(solution)/shard_map/ppermute | solution.py:421
  54.4 5.3 %collective-permute-done.16.other_ref = bf16[32,1024]{1,0:T(8,128)(2,1)S(1)} collective-permute-done((bf16[32,1024]{1,0:T(8,128)(2,1)S(1)}, bf16[32,1024]{1,0:T(8,128)(2,1)S(1)}, u32[]{:S(2)}, u32[]{:S(2)}) %collective-permute-start.16) | collective-permute-done | bytes 65568 | tf_op jit(solution)/shard_map/ppermute | solution.py:421
  59.8 0.7 %guide.1 = bf16[32,1024]{1,0:T(8,128)(2,1)} custom-call(f32[1]{0:T(128)S(6)} %copy.11.guidance_ref, f32[32,1024]{1,0:T(8,128)S(1)} %get-tuple-element.33.kept_ref, bf16[32,1024]{1,0:T(8,128)(2,1)S(1)} %collective-permute-done.16.other_ref), custom_call_target="tpu_custom_call" | custom-call | flops 1000 | bytes 1000 | tf_op jit(solution)/shard_map/guide/pallas_call | solution.py:384
  (27 shorter events, 0.4 us)
Async XLA Ops:
  0.0 12.6 %copy-start.3 = (bf16[1024,256]{1,0:T(8,128)(2,1)S(1)}, bf16[1024,256]{1,0:T(8,128)(2,1)}, u32[]{:S(2)}) copy-start(bf16[1024,256]{1,0:T(8,128)(2,1)} %wq_ref.1) | copy-start | bytes 1572868
  0.0 12.9 %copy-start.4 = (s32[8,2]{0,1:T(2,128)S(1)}, s32[8,2]{0,1:T(2,128)}, u32[]{:S(2)}) copy-start(s32[8,2]{0,1:T(2,128)} %param.11) | copy-start | bytes 196
  0.0 12.9 %copy-start.5 = (s32[2]{0:T(128)S(1)}, s32[2]{0:T(128)}, u32[]{:S(2)}) copy-start(s32[2]{0:T(128)} %param.12) | copy-start | bytes 28
  2.2 10.8 %collective-permute-start.10 = (bf16[128,1024]{1,0:T(8,128)(2,1)S(1)}, bf16[128,1024]{1,0:T(8,128)(2,1)S(1)}, u32[]{:S(2)}, u32[]{:S(2)}) collective-permute-start(bf16[128,1024]{1,0:T(8,128)(2,1)S(1)} %get-tuple-element.28.refs_0_), channel_id=1, source_target_pairs={{0,2},{2,0},{4,6},{6,4},{1,3},{3,1},{5,7},{7,5},{8,10},{10,8},{12,... | collective-permute-start | bytes 786440 | tf_op jit(solution)/shard_map/ppermute | solution.py:405
  3.8 11.5 %collective-permute-start.4 = (bf16[512,256]{1,0:T(8,128)(2,1)S(1)}, bf16[512,256]{1,0:T(8,128)(2,1)S(1)}, u32[]{:S(2)}, u32[]{:S(2)}) collective-permute-start(bf16[512,256]{1,0:T(8,128)(2,1)S(1)} %get-tuple-element.21.refs_0_), channel_id=1, source_target_pairs={{0,32},{8,40},{16,48},{24,56},{32,0},{40,8},{48,16},{56,24},{64,96... | collective-permute-start | bytes 786440 | tf_op jit(solution)/shard_map/ppermute | solution.py:403
  6.1 12.6 %collective-permute-start = (bf16[512,256]{1,0:T(8,128)(2,1)S(1)}, bf16[512,256]{1,0:T(8,128)(2,1)S(1)}, u32[]{:S(2)}, u32[]{:S(2)}) collective-permute-start(bf16[512,256]{1,0:T(8,128)(2,1)S(1)} %get-tuple-element.21.refs_0_), channel_id=1, source_target_pairs={{16,32},{32,16},{24,40},{40,24},{48,64},{64,48},{56,72},{72,56},{8... | collective-permute-start | bytes 786440 | tf_op jit(solution)/shard_map/ppermute | solution.py:402
  6.1 12.7 %collective-permute-start.1 = (bf16[512,256]{1,0:T(8,128)(2,1)S(1)}, bf16[512,256]{1,0:T(8,128)(2,1)S(1)}, u32[]{:S(2)}, u32[]{:S(2)}) collective-permute-start(bf16[512,256]{1,0:T(8,128)(2,1)S(1)} %get-tuple-element.21.refs_0_), channel_id=1, source_target_pairs={{0,16},{16,0},{8,24},{24,8},{32,48},{48,32},{40,56},{56,40},{64,80... | collective-permute-start | bytes 786440 | tf_op jit(solution)/shard_map/ppermute | solution.py:402
  13.1 19.1 %collective-permute-start.11 = (bf16[256,1024]{1,0:T(8,128)(2,1)S(1)}, bf16[256,1024]{1,0:T(8,128)(2,1)S(1)}, u32[]{:S(2)}, u32[]{:S(2)}) collective-permute-start(bf16[256,1024]{1,0:T(8,128)(2,1)S(1)} %stack.2), channel_id=1, source_target_pairs={{0,6},{2,4},{4,2},{6,0},{1,7},{3,5},{5,3},{7,1},{8,14},{10,12},{12... | collective-permute-start | bytes 1572872 | tf_op jit(solution)/shard_map/ppermute | solution.py:409
  15.3 4.2 %collective-permute-start.6 = (bf16[512,256]{1,0:T(8,128)(2,1)S(1)}, bf16[512,256]{1,0:T(8,128)(2,1)S(1)}, u32[]{:S(2)}, u32[]{:S(2)}) collective-permute-start(bf16[512,256]{1,0:T(8,128)(2,1)S(1)} %get-tuple-element.21.refs_0_), channel_id=1, source_target_pairs={{0,8},{8,0},{16,24},{24,16},{32,40},{40,32},{48,56},{56,48},{64,72... | collective-permute-start | bytes 786440 | tf_op jit(solution)/shard_map/ppermute | solution.py:411
  15.3 10.5 %collective-permute-start.5 = (bf16[512,256]{1,0:T(8,128)(2,1)S(1)}, bf16[512,256]{1,0:T(8,128)(2,1)S(1)}, u32[]{:S(2)}, u32[]{:S(2)}) collective-permute-start(bf16[512,256]{1,0:T(8,128)(2,1)S(1)} %collective-permute-done.4.refs_2_), channel_id=1, source_target_pairs={{0,64},{8,72},{16,80},{24,88},{32,224},{40,232},{48,240},{56,248},... | collective-permute-start | bytes 786440 | tf_op jit(solution)/shard_map/ppermute | solution.py:404
  18.9 2.1 %collective-permute-start.2 = (bf16[256,256]{1,0:T(8,128)(2,1)S(1)}, bf16[256,256]{1,0:T(8,128)(2,1)S(1)}, u32[]{:S(2)}, u32[]{:S(2)}) collective-permute-start(bf16[256,256]{1,0:T(8,128)(2,1)S(1)} %get-tuple-element.23), channel_id=1, source_target_pairs={{0,8},{8,0},{16,24},{24,16},{32,40},{40,32},{48,56},{56,48},{64,72... | collective-permute-start | bytes 393224 | tf_op jit(solution)/shard_map/ppermute | solution.py:412
  19.0 2.0 %collective-permute-start.3 = (bf16[256,256]{1,0:T(8,128)(2,1)S(1)}, bf16[256,256]{1,0:T(8,128)(2,1)S(1)}, u32[]{:S(2)}, u32[]{:S(2)}) collective-permute-start(bf16[256,256]{1,0:T(8,128)(2,1)S(1)} %get-tuple-element.24), channel_id=1, source_target_pairs={{0,8},{8,0},{16,24},{24,16},{32,40},{40,32},{48,56},{56,48},{64,72... | collective-permute-start | bytes 393224 | tf_op jit(solution)/shard_map/ppermute | solution.py:412
  27.4 6.5 %collective-permute-start.7 = (bf16[256,256]{1,0:T(8,128)(2,1)S(1)}, bf16[256,256]{1,0:T(8,128)(2,1)S(1)}, u32[]{:S(2)}, u32[]{:S(2)}) collective-permute-start(bf16[256,256]{1,0:T(8,128)(2,1)S(1)} %attend.5.a0.refs_2_), channel_id=1, source_target_pairs={{0,2},{2,0},{4,6},{6,4},{1,3},{3,1},{5,7},{7,5},{8,10},{10,8},{12,... | collective-permute-start | bytes 393224 | tf_op jit(solution)/shard_map/ppermute | solution.py:417
  28.1 7.8 %collective-permute-start.8 = (bf16[256,256]{1,0:T(8,128)(2,1)S(1)}, bf16[256,256]{1,0:T(8,128)(2,1)S(1)}, u32[]{:S(2)}, u32[]{:S(2)}) collective-permute-start(bf16[256,256]{1,0:T(8,128)(2,1)S(1)} %attend.5.a0.refs_2_), channel_id=1, source_target_pairs={{0,4},{2,6},{4,0},{6,2},{1,5},{3,7},{5,1},{7,3},{8,12},{10,14},{12... | collective-permute-start | bytes 393224 | tf_op jit(solution)/shard_map/ppermute | solution.py:417
  30.1 7.4 %collective-permute-start.9 = (bf16[256,256]{1,0:T(8,128)(2,1)S(1)}, bf16[256,256]{1,0:T(8,128)(2,1)S(1)}, u32[]{:S(2)}, u32[]{:S(2)}) collective-permute-start(bf16[256,256]{1,0:T(8,128)(2,1)S(1)} %attend.5.a0.refs_2_), channel_id=1, source_target_pairs={{0,6},{2,4},{4,2},{6,0},{1,7},{3,5},{5,3},{7,1},{8,14},{10,12},{12... | collective-permute-start | bytes 393224 | tf_op jit(solution)/shard_map/ppermute | solution.py:417
  32.3 5.4 %copy-start = (bf16[256,1024]{1,0:T(8,128)(2,1)S(1)}, bf16[256,1024]{1,0:T(8,128)(2,1)}, u32[]{:S(2)}) copy-start(bf16[256,1024]{1,0:T(8,128)(2,1)} %o0.1) | copy-start | bytes 1572868
  32.3 5.4 %copy-start.1 = (bf16[1024,1024]{1,0:T(8,128)(2,1)S(1)}, bf16[1024,1024]{1,0:T(8,128)(2,1)}, u32[]{:S(2)}) copy-start(bf16[1024,1024]{1,0:T(8,128)(2,1)} %win_ref.1) | copy-start | bytes 6291460
  32.3 5.4 %copy-start.2 = (bf16[1024,1024]{1,0:T(8,128)(2,1)S(1)}, bf16[1024,1024]{1,0:T(8,128)(2,1)}, u32[]{:S(2)}) copy-start(bf16[1024,1024]{1,0:T(8,128)(2,1)} %wback_ref.1) | copy-start | bytes 6291460
  32.3 5.3 %collective-permute-start.12 = (bf16[384,1024]{1,0:T(8,128)(2,1)S(1)}, bf16[384,1024]{1,0:T(8,128)(2,1)S(1)}, u32[]{:S(2)}, u32[]{:S(2)}) collective-permute-start(bf16[384,1024]{1,0:T(8,128)(2,1)S(1)} %stack.3), channel_id=1, source_target_pairs={{0,8},{8,0},{16,24},{24,16},{32,40},{40,32},{48,56},{56,48},{64,72... | collective-permute-start | bytes 2359304 | tf_op jit(solution)/shard_map/ppermute | solution.py:415
  39.9 6.2 %collective-permute-start.13 = (bf16[64,1024]{1,0:T(8,128)(2,1)S(1)}, bf16[64,1024]{1,0:T(8,128)(2,1)S(1)}, u32[]{:S(2)}, u32[]{:S(2)}) collective-permute-start(bf16[64,1024]{1,0:T(8,128)(2,1)S(1)} %get-tuple-element.30), channel_id=1, source_target_pairs={{0,2},{2,0},{4,6},{6,4},{1,3},{3,1},{5,7},{7,5},{8,10},{10,8},{12,... | collective-permute-start | bytes 393224 | tf_op jit(solution)/shard_map/ppermute | solution.py:419
  40.0 9.6 %collective-permute-start.14 = (bf16[64,1024]{1,0:T(8,128)(2,1)S(1)}, bf16[64,1024]{1,0:T(8,128)(2,1)S(1)}, u32[]{:S(2)}, u32[]{:S(2)}) collective-permute-start(bf16[64,1024]{1,0:T(8,128)(2,1)S(1)} %get-tuple-element.31), channel_id=1, source_target_pairs={{0,4},{2,6},{4,0},{6,2},{1,5},{3,7},{5,1},{7,3},{8,12},{10,14},{12... | collective-permute-start | bytes 393224 | tf_op jit(solution)/shard_map/ppermute | solution.py:419
  44.0 7.2 %collective-permute-start.15 = (bf16[64,1024]{1,0:T(8,128)(2,1)S(1)}, bf16[64,1024]{1,0:T(8,128)(2,1)S(1)}, u32[]{:S(2)}, u32[]{:S(2)}) collective-permute-start(bf16[64,1024]{1,0:T(8,128)(2,1)S(1)} %get-tuple-element.32), channel_id=1, source_target_pairs={{0,6},{2,4},{4,2},{6,0},{1,7},{3,5},{5,3},{7,1},{8,14},{10,12},{12... | collective-permute-start | bytes 393224 | tf_op jit(solution)/shard_map/ppermute | solution.py:419
  51.3 8.5 %collective-permute-start.16 = (bf16[32,1024]{1,0:T(8,128)(2,1)S(1)}, bf16[32,1024]{1,0:T(8,128)(2,1)S(1)}, u32[]{:S(2)}, u32[]{:S(2)}) collective-permute-start(bf16[32,1024]{1,0:T(8,128)(2,1)S(1)} %get-tuple-element.34), channel_id=1, source_target_pairs={{0,1},{1,0},{2,3},{3,2},{4,5},{5,4},{6,7},{7,6},{8,9},{9,8},{10,11... | collective-permute-start | bytes 196616 | tf_op jit(solution)/shard_map/ppermute | solution.py:421

commit v9 on v8

--- a/solution.py
+++ b/solution.py
@@ -184,6 +184,7 @@
         total = jnp.sum(functools.reduce(jnp.add, weights), axis=0, keepdims=True)
         if not first:
             total = total + scale * old_total
+        inverse = 1.0 / total
         rounded = jnp.concatenate([w.astype(jnp.bfloat16) for w in weights], axis=0)
         values = jnp.concatenate(values, axis=1)
         finished = []
@@ -196,7 +197,7 @@
                 if not first:
                     blended = blended + scale[:, lanes] * held_ref[at]
                 if last:
-                    finished.append(blended / total[:, lanes])
+                    finished.append(blended * inverse[:, lanes])
                 else:
                     refs[0][at] = blended
         if last:

time: 60.5 us -> 60.5 us (level)
  no operation moved by 1% of the time
where the time goes in v9:
time: 60.5 us; the launch traced here: 60.4 us
  starting transfers between devices  26.6 us (44%)
  waiting for transfers between devices  23 us (38%)
  Pallas kernels  9.91 us (16%)
  between operations  0.87 us (1%)
    ppermute x3, waiting for transfers between devices, on_device(): received = [flipped('head', 4, j)(r) for j, r in zip((1, 2, 3), outgoing)]  6.59 us
    ppermute x2, starting transfers between devices, on_device(): near = [matched(count, 2, parity)(kv) for parity in (1, 0)]  6.46 us
    ppermute x1, waiting for transfers between devices, on_device(): other = flipped('branch', 2, 1)(sent)  5.35 us
    ppermute x3, waiting for transfers between devices, on_device(): pieces = [attended] + [flipped('head', 4, j)(attended) for j in (1, 2, 3)]  4.91 us
    ppermute x1, waiting for transfers between devices, on_device(): far = (across, onward(count)(across))  4.8 us
    ppermute x3, starting transfers between devices, on_device(): pieces = [attended] + [flipped('head', 4, j)(attended) for j in (1, 2, 3)]  4.79 us
    ppermute x3, starting transfers between devices, on_device(): received = [flipped('head', 4, j)(r) for j, r in zip((1, 2, 3), outgoing)]  4.78 us
    pallas_call x3, Pallas kernels, attend(): pl.pallas_call(functools.partial(attend_kernel, blocks, first, last), out...  4.11 us
  transfers between devices with their start and end apart: 17, of which 10 were waited for; matrix products, arithmetic and copies ran while one was open for 0% of the time, Pallas kernels for 8%

profile of v9, /device:TPU:8, one launch (start us, length us, event | category | flops | bytes accessed | tf_op | source)
XLA Modules:
  0.0 60.4 jit_solution(7046449843348785921)
XLA Ops:
  0.0 2.2 %project.1 = (bf16[256,1024]{1,0:T(8,128)(2,1)S(1)}, bf16[512,256]{1,0:T(8,128)(2,1)S(1)}, bf16[128,1024]{1,0:T(8,128)(2,1)S(1)}) custom-call(bf16[256,1024]{1,0:T(8,128)(2,1)} %bitcast.6, bf16[1024,256]{1,0:T(8,128)(2,1)} %wk_hbm.1, bf16[1024,256]{1,0:T(8,128)(2,1)} %wv_hbm.1, bf16[256,1024]{1,0:T(8,128)(2,1)} %o0.1), custom_call_target="tpu_custom_call" | custom-call | flops 1000 | bytes 1000 | tf_op jit(solution)/shard_map/project/pallas_call | solution.py:120
  2.2 1.6 %collective-permute-start.10 = (bf16[128,1024]{1,0:T(8,128)(2,1)S(1)}, bf16[128,1024]{1,0:T(8,128)(2,1)S(1)}, u32[]{:S(2)}, u32[]{:S(2)}) collective-permute-start(bf16[128,1024]{1,0:T(8,128)(2,1)S(1)} %get-tuple-element.28.refs_0_), channel_id=1, source_target_pairs={{0,2},{2,0},{4,6},{6,4},{1,3},{3,1},{5,7},{7,5},{8,10},{10,8},{12,... | collective-permute-start | bytes 786440 | tf_op jit(solution)/shard_map/ppermute | solution.py:406
  3.8 2.3 %collective-permute-start.4 = (bf16[512,256]{1,0:T(8,128)(2,1)S(1)}, bf16[512,256]{1,0:T(8,128)(2,1)S(1)}, u32[]{:S(2)}, u32[]{:S(2)}) collective-permute-start(bf16[512,256]{1,0:T(8,128)(2,1)S(1)} %get-tuple-element.21.refs_0_), channel_id=1, source_target_pairs={{0,32},{8,40},{16,48},{24,56},{32,0},{40,8},{48,16},{56,24},{64,96... | collective-permute-start | bytes 786440 | tf_op jit(solution)/shard_map/ppermute | solution.py:404
  6.1 6.5 %collective-permute-start.1 = (bf16[512,256]{1,0:T(8,128)(2,1)S(1)}, bf16[512,256]{1,0:T(8,128)(2,1)S(1)}, u32[]{:S(2)}, u32[]{:S(2)}) collective-permute-start(bf16[512,256]{1,0:T(8,128)(2,1)S(1)} %get-tuple-element.21.refs_0_), channel_id=1, source_target_pairs={{0,16},{16,0},{8,24},{24,8},{32,48},{48,32},{40,56},{56,40},{64,80... | collective-permute-start | bytes 786440 | tf_op jit(solution)/shard_map/ppermute | solution.py:403
  12.6 0.3 ask.1.q_ref.refs_3_
  12.9 0.2 biases.1.bias_ref.refs_2_
  13.1 2.2 %collective-permute-start.11 = (bf16[256,1024]{1,0:T(8,128)(2,1)S(1)}, bf16[256,1024]{1,0:T(8,128)(2,1)S(1)}, u32[]{:S(2)}, u32[]{:S(2)}) collective-permute-start(bf16[256,1024]{1,0:T(8,128)(2,1)S(1)} %stack.2), channel_id=1, source_target_pairs={{0,6},{2,4},{4,2},{6,0},{1,7},{3,5},{5,3},{7,1},{8,14},{10,12},{12... | collective-permute-start | bytes 1572872 | tf_op jit(solution)/shard_map/ppermute | solution.py:410
  15.3 1.2 %collective-permute-start.5 = (bf16[512,256]{1,0:T(8,128)(2,1)S(1)}, bf16[512,256]{1,0:T(8,128)(2,1)S(1)}, u32[]{:S(2)}, u32[]{:S(2)}) collective-permute-start(bf16[512,256]{1,0:T(8,128)(2,1)S(1)} %collective-permute-done.4.refs_2_), channel_id=1, source_target_pairs={{0,64},{8,72},{16,80},{24,88},{32,224},{40,232},{48,240},{56,248},... | collective-permute-start | bytes 786440 | tf_op jit(solution)/shard_map/ppermute | solution.py:405
  16.5 1.0 %attend.3 = (f32[512,128]{1,0:T(8,128)S(1)}, f32[4,512]{1,0:T(4,128)S(1)}) custom-call(f32[32,128]{1,0:T(8,128)S(1)} %biases.1.bias_ref.refs_2_, bf16[256,256]{1,0:T(8,128)(2,1)S(1)} %ask.1.q_ref.refs_3_, bf16[512,256]{1,0:T(8,128)(2,1)S(1)} %get-tuple-element.21.refs_0_), custom_call_target="tpu_custom_call" | custom-call | flops 1000 | bytes 1000 | tf_op jit(solution)/shard_map/attend/pallas_call | solution.py:220
  17.5 1.2 %collective-permute-done.a_ref.refs_1_ = bf16[512,256]{1,0:T(8,128)(2,1)S(1)} collective-permute-done((bf16[512,256]{1,0:T(8,128)(2,1)S(1)}, bf16[512,256]{1,0:T(8,128)(2,1)S(1)}, u32[]{:S(2)}, u32[]{:S(2)}) %collective-permute-start) | collective-permute-done | bytes 262176 | tf_op jit(solution)/shard_map/ppermute | solution.py:403
  18.7 0.2 collective-permute-done.1.b_ref.refs_2_
  19.0 0.5 collective-permute-start.3
  19.5 1.5 %attend.4 = (f32[512,128]{1,0:T(8,128)S(1)}, f32[4,512]{1,0:T(4,128)S(1)}) custom-call(f32[32,128]{1,0:T(8,128)S(1)} %biases.1.bias_ref.refs_2_, bf16[256,256]{1,0:T(8,128)(2,1)S(1)} %ask.1.q_ref.refs_3_, bf16[512,256]{1,0:T(8,128)(2,1)S(1)} %collective-permute-done.6.refs_0_, bf16[512,256]{1,0:T(8,128)(2,1)S(1)} %collective-permute-done.a_ref.refs_1_, ...), custom_call_target="tpu_custom_call" | custom-call | flops 1000 | bytes 1000 | tf_op jit(solution)/shard_map/attend/pallas_call | solution.py:220
  21.0 4.8 %collective-permute-done.5.refs_3_ = bf16[512,256]{1,0:T(8,128)(2,1)S(1)} collective-permute-done((bf16[512,256]{1,0:T(8,128)(2,1)S(1)}, bf16[512,256]{1,0:T(8,128)(2,1)S(1)}, u32[]{:S(2)}, u32[]{:S(2)}) %collective-permute-start.5) | collective-permute-done | bytes 262176 | tf_op jit(solution)/shard_map/ppermute | solution.py:405
  25.8 1.6 %attend.5.a0.refs_2_ = bf16[256,256]{1,0:T(8,128)(2,1)S(1)} custom-call(f32[32,128]{1,0:T(8,128)S(1)} %biases.1.bias_ref.refs_2_, bf16[256,256]{1,0:T(8,128)(2,1)S(1)} %ask.1.q_ref.refs_3_, bf16[256,256]{1,0:T(8,128)(2,1)S(1)} %collective-permute-done.2.refs_0_, bf16[256,256]{1,0:T(8,128)(2,1)S(1)} %collective-permute-done.3.refs_1_, ...), custom_call_target="tpu_custom_call" | custom-call | flops 1000 | bytes 1000 | tf_op jit(solution)/shard_map/attend/pallas_call | solution.py:220
  27.4 0.7 %collective-permute-start.7 = (bf16[256,256]{1,0:T(8,128)(2,1)S(1)}, bf16[256,256]{1,0:T(8,128)(2,1)S(1)}, u32[]{:S(2)}, u32[]{:S(2)}) collective-permute-start(bf16[256,256]{1,0:T(8,128)(2,1)S(1)} %attend.5.a0.refs_2_), channel_id=1, source_target_pairs={{0,2},{2,0},{4,6},{6,4},{1,3},{3,1},{5,7},{7,5},{8,10},{10,8},{12,... | collective-permute-start | bytes 393224 | tf_op jit(solution)/shard_map/ppermute | solution.py:418
  28.1 2.0 %collective-permute-start.8 = (bf16[256,256]{1,0:T(8,128)(2,1)S(1)}, bf16[256,256]{1,0:T(8,128)(2,1)S(1)}, u32[]{:S(2)}, u32[]{:S(2)}) collective-permute-start(bf16[256,256]{1,0:T(8,128)(2,1)S(1)} %attend.5.a0.refs_2_), channel_id=1, source_target_pairs={{0,4},{2,6},{4,0},{6,2},{1,5},{3,7},{5,1},{7,3},{8,12},{10,14},{12... | collective-permute-start | bytes 393224 | tf_op jit(solution)/shard_map/ppermute | solution.py:418
  30.1 2.1 %collective-permute-start.9 = (bf16[256,256]{1,0:T(8,128)(2,1)S(1)}, bf16[256,256]{1,0:T(8,128)(2,1)S(1)}, u32[]{:S(2)}, u32[]{:S(2)}) collective-permute-start(bf16[256,256]{1,0:T(8,128)(2,1)S(1)} %attend.5.a0.refs_2_), channel_id=1, source_target_pairs={{0,6},{2,4},{4,2},{6,0},{1,7},{3,5},{5,3},{7,1},{8,14},{10,12},{12... | collective-permute-start | bytes 393224 | tf_op jit(solution)/shard_map/ppermute | solution.py:418
  32.3 0.3 collective-permute-start.12
  32.6 1.3 %collective-permute-done.7.a1 = bf16[256,256]{1,0:T(8,128)(2,1)S(1)} collective-permute-done((bf16[256,256]{1,0:T(8,128)(2,1)S(1)}, bf16[256,256]{1,0:T(8,128)(2,1)S(1)}, u32[]{:S(2)}, u32[]{:S(2)}) %collective-permute-start.7) | collective-permute-done | bytes 131104 | tf_op jit(solution)/shard_map/ppermute | solution.py:418
  33.9 2.0 %collective-permute-done.8.a2 = bf16[256,256]{1,0:T(8,128)(2,1)S(1)} collective-permute-done((bf16[256,256]{1,0:T(8,128)(2,1)S(1)}, bf16[256,256]{1,0:T(8,128)(2,1)S(1)}, u32[]{:S(2)}, u32[]{:S(2)}) %collective-permute-start.8) | collective-permute-done | bytes 131104 | tf_op jit(solution)/shard_map/ppermute | solution.py:418
  36.0 1.5 %collective-permute-done.9.a3 = bf16[256,256]{1,0:T(8,128)(2,1)S(1)} collective-permute-done((bf16[256,256]{1,0:T(8,128)(2,1)S(1)}, bf16[256,256]{1,0:T(8,128)(2,1)S(1)}, u32[]{:S(2)}, u32[]{:S(2)}) %collective-permute-start.9) | collective-permute-done | bytes 131104 | tf_op jit(solution)/shard_map/ppermute | solution.py:418
  37.5 0.1 lay.1.left_ref
  37.7 2.2 %feed.1 = (f32[64,1024]{1,0:T(8,128)S(1)}, bf16[64,1024]{1,0:T(8,128)(2,1)S(1)}, bf16[64,1024]{1,0:T(8,128)(2,1)S(1)}, bf16[64,1024]{1,0:T(8,128)(2,1)S(1)}) custom-call(bf16[256,1024]{1,0:T(8,128)(2,1)S(1)} %get-tuple-element.20.after_ref.x_ref, bf16[256,1024]{1,0:T(8,128)(2,1)S(1)} %lay.1.left_ref, bf16[256,1024]{1,0:T(8,128)(2,1)S(1)} %copy-done, ...), custom_call_target="tpu_custom_call" | custom-call | flops 1000 | bytes 1000 | tf_op jit(solution)/shard_map/feed/pallas_call | solution.py:336
  40.0 4.0 %collective-permute-start.14 = (bf16[64,1024]{1,0:T(8,128)(2,1)S(1)}, bf16[64,1024]{1,0:T(8,128)(2,1)S(1)}, u32[]{:S(2)}, u32[]{:S(2)}) collective-permute-start(bf16[64,1024]{1,0:T(8,128)(2,1)S(1)} %get-tuple-element.31), channel_id=1, source_target_pairs={{0,4},{2,6},{4,0},{6,2},{1,5},{3,7},{5,1},{7,3},{8,12},{10,14},{12... | collective-permute-start | bytes 393224 | tf_op jit(solution)/shard_map/ppermute | solution.py:420
  44.0 0.6 %collective-permute-start.15 = (bf16[64,1024]{1,0:T(8,128)(2,1)S(1)}, bf16[64,1024]{1,0:T(8,128)(2,1)S(1)}, u32[]{:S(2)}, u32[]{:S(2)}) collective-permute-start(bf16[64,1024]{1,0:T(8,128)(2,1)S(1)} %get-tuple-element.32), channel_id=1, source_target_pairs={{0,6},{2,4},{4,2},{6,0},{1,7},{3,5},{5,3},{7,1},{8,14},{10,12},{12... | collective-permute-start | bytes 393224 | tf_op jit(solution)/shard_map/ppermute | solution.py:420
  44.7 1.4 %collective-permute-done.13.r1 = bf16[64,1024]{1,0:T(8,128)(2,1)S(1)} collective-permute-done((bf16[64,1024]{1,0:T(8,128)(2,1)S(1)}, bf16[64,1024]{1,0:T(8,128)(2,1)S(1)}, u32[]{:S(2)}, u32[]{:S(2)}) %collective-permute-start.13) | collective-permute-done | bytes 131104 | tf_op jit(solution)/shard_map/ppermute | solution.py:420
  46.1 3.4 %collective-permute-done.14.r2 = bf16[64,1024]{1,0:T(8,128)(2,1)S(1)} collective-permute-done((bf16[64,1024]{1,0:T(8,128)(2,1)S(1)}, bf16[64,1024]{1,0:T(8,128)(2,1)S(1)}, u32[]{:S(2)}, u32[]{:S(2)}) %collective-permute-start.14) | collective-permute-done | bytes 131104 | tf_op jit(solution)/shard_map/ppermute | solution.py:420
  49.5 1.7 %collective-permute-done.15.r3 = bf16[64,1024]{1,0:T(8,128)(2,1)S(1)} collective-permute-done((bf16[64,1024]{1,0:T(8,128)(2,1)S(1)}, bf16[64,1024]{1,0:T(8,128)(2,1)S(1)}, u32[]{:S(2)}, u32[]{:S(2)}) %collective-permute-start.15) | collective-permute-done | bytes 131104 | tf_op jit(solution)/shard_map/ppermute | solution.py:420
  51.3 2.5 %collective-permute-start.16 = (bf16[32,1024]{1,0:T(8,128)(2,1)S(1)}, bf16[32,1024]{1,0:T(8,128)(2,1)S(1)}, u32[]{:S(2)}, u32[]{:S(2)}) collective-permute-start(bf16[32,1024]{1,0:T(8,128)(2,1)S(1)} %get-tuple-element.34), channel_id=1, source_target_pairs={{0,1},{1,0},{2,3},{3,2},{4,5},{5,4},{6,7},{7,6},{8,9},{9,8},{10,11... | collective-permute-start | bytes 196616 | tf_op jit(solution)/shard_map/ppermute | solution.py:422
  54.4 5.4 %collective-permute-done.16.other_ref = bf16[32,1024]{1,0:T(8,128)(2,1)S(1)} collective-permute-done((bf16[32,1024]{1,0:T(8,128)(2,1)S(1)}, bf16[32,1024]{1,0:T(8,128)(2,1)S(1)}, u32[]{:S(2)}, u32[]{:S(2)}) %collective-permute-start.16) | collective-permute-done | bytes 65568 | tf_op jit(solution)/shard_map/ppermute | solution.py:422
  59.8 0.7 %guide.1 = bf16[32,1024]{1,0:T(8,128)(2,1)} custom-call(f32[1]{0:T(128)S(6)} %copy.11.guidance_ref, f32[32,1024]{1,0:T(8,128)S(1)} %get-tuple-element.33.kept_ref, bf16[32,1024]{1,0:T(8,128)(2,1)S(1)} %collective-permute-done.16.other_ref), custom_call_target="tpu_custom_call" | custom-call | flops 1000 | bytes 1000 | tf_op jit(solution)/shard_map/guide/pallas_call | solution.py:385
  (27 shorter events, 0.4 us)
Async XLA Ops:
  0.0 12.6 %copy-start.3 = (bf16[1024,256]{1,0:T(8,128)(2,1)S(1)}, bf16[1024,256]{1,0:T(8,128)(2,1)}, u32[]{:S(2)}) copy-start(bf16[1024,256]{1,0:T(8,128)(2,1)} %wq_ref.1) | copy-start | bytes 1572868
  0.0 12.9 %copy-start.4 = (s32[8,2]{0,1:T(2,128)S(1)}, s32[8,2]{0,1:T(2,128)}, u32[]{:S(2)}) copy-start(s32[8,2]{0,1:T(2,128)} %param.11) | copy-start | bytes 196
  0.0 12.9 %copy-start.5 = (s32[2]{0:T(128)S(1)}, s32[2]{0:T(128)}, u32[]{:S(2)}) copy-start(s32[2]{0:T(128)} %param.12) | copy-start | bytes 28
  2.2 10.8 %collective-permute-start.10 = (bf16[128,1024]{1,0:T(8,128)(2,1)S(1)}, bf16[128,1024]{1,0:T(8,128)(2,1)S(1)}, u32[]{:S(2)}, u32[]{:S(2)}) collective-permute-start(bf16[128,1024]{1,0:T(8,128)(2,1)S(1)} %get-tuple-element.28.refs_0_), channel_id=1, source_target_pairs={{0,2},{2,0},{4,6},{6,4},{1,3},{3,1},{5,7},{7,5},{8,10},{10,8},{12,... | collective-permute-start | bytes 786440 | tf_op jit(solution)/shard_map/ppermute | solution.py:406
  3.8 11.5 %collective-permute-start.4 = (bf16[512,256]{1,0:T(8,128)(2,1)S(1)}, bf16[512,256]{1,0:T(8,128)(2,1)S(1)}, u32[]{:S(2)}, u32[]{:S(2)}) collective-permute-start(bf16[512,256]{1,0:T(8,128)(2,1)S(1)} %get-tuple-element.21.refs_0_), channel_id=1, source_target_pairs={{0,32},{8,40},{16,48},{24,56},{32,0},{40,8},{48,16},{56,24},{64,96... | collective-permute-start | bytes 786440 | tf_op jit(solution)/shard_map/ppermute | solution.py:404
  6.1 12.6 %collective-permute-start = (bf16[512,256]{1,0:T(8,128)(2,1)S(1)}, bf16[512,256]{1,0:T(8,128)(2,1)S(1)}, u32[]{:S(2)}, u32[]{:S(2)}) collective-permute-start(bf16[512,256]{1,0:T(8,128)(2,1)S(1)} %get-tuple-element.21.refs_0_), channel_id=1, source_target_pairs={{16,32},{32,16},{24,40},{40,24},{48,64},{64,48},{56,72},{72,56},{8... | collective-permute-start | bytes 786440 | tf_op jit(solution)/shard_map/ppermute | solution.py:403
  6.1 12.7 %collective-permute-start.1 = (bf16[512,256]{1,0:T(8,128)(2,1)S(1)}, bf16[512,256]{1,0:T(8,128)(2,1)S(1)}, u32[]{:S(2)}, u32[]{:S(2)}) collective-permute-start(bf16[512,256]{1,0:T(8,128)(2,1)S(1)} %get-tuple-element.21.refs_0_), channel_id=1, source_target_pairs={{0,16},{16,0},{8,24},{24,8},{32,48},{48,32},{40,56},{56,40},{64,80... | collective-permute-start | bytes 786440 | tf_op jit(solution)/shard_map/ppermute | solution.py:403
  13.1 19.1 %collective-permute-start.11 = (bf16[256,1024]{1,0:T(8,128)(2,1)S(1)}, bf16[256,1024]{1,0:T(8,128)(2,1)S(1)}, u32[]{:S(2)}, u32[]{:S(2)}) collective-permute-start(bf16[256,1024]{1,0:T(8,128)(2,1)S(1)} %stack.2), channel_id=1, source_target_pairs={{0,6},{2,4},{4,2},{6,0},{1,7},{3,5},{5,3},{7,1},{8,14},{10,12},{12... | collective-permute-start | bytes 1572872 | tf_op jit(solution)/shard_map/ppermute | solution.py:410
  15.3 4.2 %collective-permute-start.6 = (bf16[512,256]{1,0:T(8,128)(2,1)S(1)}, bf16[512,256]{1,0:T(8,128)(2,1)S(1)}, u32[]{:S(2)}, u32[]{:S(2)}) collective-permute-start(bf16[512,256]{1,0:T(8,128)(2,1)S(1)} %get-tuple-element.21.refs_0_), channel_id=1, source_target_pairs={{0,8},{8,0},{16,24},{24,16},{32,40},{40,32},{48,56},{56,48},{64,72... | collective-permute-start | bytes 786440 | tf_op jit(solution)/shard_map/ppermute | solution.py:412
  15.3 10.5 %collective-permute-start.5 = (bf16[512,256]{1,0:T(8,128)(2,1)S(1)}, bf16[512,256]{1,0:T(8,128)(2,1)S(1)}, u32[]{:S(2)}, u32[]{:S(2)}) collective-permute-start(bf16[512,256]{1,0:T(8,128)(2,1)S(1)} %collective-permute-done.4.refs_2_), channel_id=1, source_target_pairs={{0,64},{8,72},{16,80},{24,88},{32,224},{40,232},{48,240},{56,248},... | collective-permute-start | bytes 786440 | tf_op jit(solution)/shard_map/ppermute | solution.py:405
  18.9 2.1 %collective-permute-start.2 = (bf16[256,256]{1,0:T(8,128)(2,1)S(1)}, bf16[256,256]{1,0:T(8,128)(2,1)S(1)}, u32[]{:S(2)}, u32[]{:S(2)}) collective-permute-start(bf16[256,256]{1,0:T(8,128)(2,1)S(1)} %get-tuple-element.23), channel_id=1, source_target_pairs={{0,8},{8,0},{16,24},{24,16},{32,40},{40,32},{48,56},{56,48},{64,72... | collective-permute-start | bytes 393224 | tf_op jit(solution)/shard_map/ppermute | solution.py:413
  19.0 2.0 %collective-permute-start.3 = (bf16[256,256]{1,0:T(8,128)(2,1)S(1)}, bf16[256,256]{1,0:T(8,128)(2,1)S(1)}, u32[]{:S(2)}, u32[]{:S(2)}) collective-permute-start(bf16[256,256]{1,0:T(8,128)(2,1)S(1)} %get-tuple-element.24), channel_id=1, source_target_pairs={{0,8},{8,0},{16,24},{24,16},{32,40},{40,32},{48,56},{56,48},{64,72... | collective-permute-start | bytes 393224 | tf_op jit(solution)/shard_map/ppermute | solution.py:413
  27.4 6.5 %collective-permute-start.7 = (bf16[256,256]{1,0:T(8,128)(2,1)S(1)}, bf16[256,256]{1,0:T(8,128)(2,1)S(1)}, u32[]{:S(2)}, u32[]{:S(2)}) collective-permute-start(bf16[256,256]{1,0:T(8,128)(2,1)S(1)} %attend.5.a0.refs_2_), channel_id=1, source_target_pairs={{0,2},{2,0},{4,6},{6,4},{1,3},{3,1},{5,7},{7,5},{8,10},{10,8},{12,... | collective-permute-start | bytes 393224 | tf_op jit(solution)/shard_map/ppermute | solution.py:418
  28.1 7.8 %collective-permute-start.8 = (bf16[256,256]{1,0:T(8,128)(2,1)S(1)}, bf16[256,256]{1,0:T(8,128)(2,1)S(1)}, u32[]{:S(2)}, u32[]{:S(2)}) collective-permute-start(bf16[256,256]{1,0:T(8,128)(2,1)S(1)} %attend.5.a0.refs_2_), channel_id=1, source_target_pairs={{0,4},{2,6},{4,0},{6,2},{1,5},{3,7},{5,1},{7,3},{8,12},{10,14},{12... | collective-permute-start | bytes 393224 | tf_op jit(solution)/shard_map/ppermute | solution.py:418
  30.1 7.4 %collective-permute-start.9 = (bf16[256,256]{1,0:T(8,128)(2,1)S(1)}, bf16[256,256]{1,0:T(8,128)(2,1)S(1)}, u32[]{:S(2)}, u32[]{:S(2)}) collective-permute-start(bf16[256,256]{1,0:T(8,128)(2,1)S(1)} %attend.5.a0.refs_2_), channel_id=1, source_target_pairs={{0,6},{2,4},{4,2},{6,0},{1,7},{3,5},{5,3},{7,1},{8,14},{10,12},{12... | collective-permute-start | bytes 393224 | tf_op jit(solution)/shard_map/ppermute | solution.py:418
  32.3 5.4 %copy-start = (bf16[256,1024]{1,0:T(8,128)(2,1)S(1)}, bf16[256,1024]{1,0:T(8,128)(2,1)}, u32[]{:S(2)}) copy-start(bf16[256,1024]{1,0:T(8,128)(2,1)} %o0.1) | copy-start | bytes 1572868
  32.3 5.4 %copy-start.1 = (bf16[1024,1024]{1,0:T(8,128)(2,1)S(1)}, bf16[1024,1024]{1,0:T(8,128)(2,1)}, u32[]{:S(2)}) copy-start(bf16[1024,1024]{1,0:T(8,128)(2,1)} %win_ref.1) | copy-start | bytes 6291460
  32.3 5.4 %copy-start.2 = (bf16[1024,1024]{1,0:T(8,128)(2,1)S(1)}, bf16[1024,1024]{1,0:T(8,128)(2,1)}, u32[]{:S(2)}) copy-start(bf16[1024,1024]{1,0:T(8,128)(2,1)} %wback_ref.1) | copy-start | bytes 6291460
  32.3 5.3 %collective-permute-start.12 = (bf16[384,1024]{1,0:T(8,128)(2,1)S(1)}, bf16[384,1024]{1,0:T(8,128)(2,1)S(1)}, u32[]{:S(2)}, u32[]{:S(2)}) collective-permute-start(bf16[384,1024]{1,0:T(8,128)(2,1)S(1)} %stack.3), channel_id=1, source_target_pairs={{0,8},{8,0},{16,24},{24,16},{32,40},{40,32},{48,56},{56,48},{64,72... | collective-permute-start | bytes 2359304 | tf_op jit(solution)/shard_map/ppermute | solution.py:416
  39.9 6.2 %collective-permute-start.13 = (bf16[64,1024]{1,0:T(8,128)(2,1)S(1)}, bf16[64,1024]{1,0:T(8,128)(2,1)S(1)}, u32[]{:S(2)}, u32[]{:S(2)}) collective-permute-start(bf16[64,1024]{1,0:T(8,128)(2,1)S(1)} %get-tuple-element.30), channel_id=1, source_target_pairs={{0,2},{2,0},{4,6},{6,4},{1,3},{3,1},{5,7},{7,5},{8,10},{10,8},{12,... | collective-permute-start | bytes 393224 | tf_op jit(solution)/shard_map/ppermute | solution.py:420
  40.0 9.5 %collective-permute-start.14 = (bf16[64,1024]{1,0:T(8,128)(2,1)S(1)}, bf16[64,1024]{1,0:T(8,128)(2,1)S(1)}, u32[]{:S(2)}, u32[]{:S(2)}) collective-permute-start(bf16[64,1024]{1,0:T(8,128)(2,1)S(1)} %get-tuple-element.31), channel_id=1, source_target_pairs={{0,4},{2,6},{4,0},{6,2},{1,5},{3,7},{5,1},{7,3},{8,12},{10,14},{12... | collective-permute-start | bytes 393224 | tf_op jit(solution)/shard_map/ppermute | solution.py:420
  44.0 7.2 %collective-permute-start.15 = (bf16[64,1024]{1,0:T(8,128)(2,1)S(1)}, bf16[64,1024]{1,0:T(8,128)(2,1)S(1)}, u32[]{:S(2)}, u32[]{:S(2)}) collective-permute-start(bf16[64,1024]{1,0:T(8,128)(2,1)S(1)} %get-tuple-element.32), channel_id=1, source_target_pairs={{0,6},{2,4},{4,2},{6,0},{1,7},{3,5},{5,3},{7,1},{8,14},{10,12},{12... | collective-permute-start | bytes 393224 | tf_op jit(solution)/shard_map/ppermute | solution.py:420
  51.3 8.5 %collective-permute-start.16 = (bf16[32,1024]{1,0:T(8,128)(2,1)S(1)}, bf16[32,1024]{1,0:T(8,128)(2,1)S(1)}, u32[]{:S(2)}, u32[]{:S(2)}) collective-permute-start(bf16[32,1024]{1,0:T(8,128)(2,1)S(1)} %get-tuple-element.34), channel_id=1, source_target_pairs={{0,1},{1,0},{2,3},{3,2},{4,5},{5,4},{6,7},{7,6},{8,9},{9,8},{10,11... | collective-permute-start | bytes 196616 | tf_op jit(solution)/shard_map/ppermute | solution.py:422
